TPU v7x, 32 devices: a whole 2x2x4 slice. The times are simulated.
32 devices in a mesh: loop: 8 (over y, x, core), grp: 4 (over z).
Axes of the slice: x: 2, y: 2, z: 4, core: 2. Of those that a mesh axis runs over, the one named last changes fastest.
Arguments:
- queries: bfloat16 [8192, 512], P(('loop', 'grp')), may hold values from -24 to 24
- key_rows: bfloat16 [8192, 512], P(('loop', 'grp')), may hold values from -4 to 4
- value_rows: bfloat16 [8192, 512], P(('loop', 'grp')), may hold values from -6 to 6
- out_weight: bfloat16 [512, 512], replicated, may hold values from -0.25 to 0.25
- tile_list: int32 [32, 4], P(('loop', 'grp')), may hold values from 0 to 7, as said below
- expander_order: int32 [3, 8192], P(None, ('loop', 'grp')), may hold values from 0 to 255, as said below
- expander_bias: float32 [3, 8], replicated, may hold values from 2 to 6
Outputs:
- layer_output: bfloat16 [8192, 512], P(('loop', 'grp'))
Inputs may be any that keep to these rules, and one draw needn't show every extreme that they name: `tile_list`: entry 0 of every row is 3, the partition's own block. Each other entry is 3 + o for a loop offset o with 0 < |o| <= 3, distinct within a row, or the padding value 2 * 3 + 1; every row has at least one non-padding neighbour entry. `expander_order`: for each matching and each partition, the 256 entries of that partition are a permutation of 0 to 255.
All inputs are finite; a program needn't handle non-finite values.
Results may differ from a plain program's by a relative error of at most 0.0075.
Values may be sent and summed in bfloat16 or wider, within the bound.
No kernel may reach another device: no remote copies, remote signals or barrier semaphores. Data moves between devices by JAX's collectives and lax.ppermute only.
A program may use at most 128 MiB of HBM per device.

v0:
```python
import functools

import jax
import jax.numpy as jnp
from jax import lax
from jax.experimental import pallas as pl
from jax.experimental.pallas import tpu as pltpu
from jax.sharding import PartitionSpec as P

HEADS = 8
RADIUS = 3
MATCHINGS = 3
LANES = 128
LOG2E = 1.4426950408889634
NEG_FILL = -1e30
VMEM_BYTES = 40 * 1024 * 1024

F32 = jnp.float32
BF16 = jnp.bfloat16


def dot(a, b, contract=((1,), (0,))):
    return lax.dot_general(a, b, (contract, ((), ())), preferred_element_type=F32)


def place_table(order_row, rows):
    row_ids = lax.broadcasted_iota(jnp.int32, (rows, rows), 0)
    return jnp.where(row_ids == order_row, 1.0, 0.0).astype(BF16)


def prep_kernel(groups, k_ref, v_ref, order_ref, tile_ref, *bucket_refs):
    rows, width = k_ref.shape
    bucket = rows // groups
    half = width // 2
    keys = k_ref[...]
    vals = v_ref[...]
    order = order_ref[...]
    lane = lax.broadcasted_iota(jnp.int32, order.shape, 1)
    swapped = jnp.where(lane % 2 == 0, jnp.roll(order, -1, axis=1), jnp.roll(order, 1, axis=1))
    wanted = jnp.where(lane < bucket, swapped, order)
    for j in range(MATCHINGS):
        table = place_table(wanted[j : j + 1, :], rows)
        ordered_k = dot(table, keys, ((0,), (0,))).astype(BF16)
        ordered_v = dot(table, vals, ((0,), (0,))).astype(BF16)
        for b in range(groups):
            out = slice(j * bucket, (j + 1) * bucket)
            bucket_refs[b][out, :width] = ordered_k[b * bucket : (b + 1) * bucket]
            bucket_refs[b][out, width:] = ordered_v[b * bucket : (b + 1) * bucket]
    tile_ref[:width, :] = vals.T
    tile_ref[width : width + rows, :] = keys[:, :half]
    tile_ref[width + rows :, :] = keys[:, half:]


def blocks_kernel(loop_size, tiles_ref, q_ref, *refs):
    n_bufs = 2 * RADIUS + 1
    bufs = refs[:n_bufs]
    acc_out, stat_out, tile_vmem, qz, acc, m_ref, l_ref, sems = refs[n_bufs:]
    rows, width = q_ref.shape
    head = width // HEADS
    n_tiles = tiles_ref.shape[1]
    here = lax.axis_index("loop")

    def buffer_of(t):
        offset = tiles_ref[0, t]
        if loop_size == 8:
            away = here ^ lax.rem(here + offset - RADIUS + loop_size, loop_size)
            slot = jnp.where(away > 4, away - 1, away)
        else:
            slot = offset
        return slot, offset <= 2 * RADIUS

    for t in range(n_tiles):
        slot, live = buffer_of(t)
        for k in range(n_bufs):

            @pl.when(live & (slot == k))
            def _():
                pltpu.make_async_copy(bufs[k], tile_vmem.at[t], sems.at[t]).start()

    q_t = q_ref[...].T
    zeros = jnp.zeros((head, rows), BF16)
    for h in range(HEADS):
        mine = q_t[h * head : (h + 1) * head]
        parts = (mine, zeros) if h % 2 == 0 else (zeros, mine)
        qz[h] = jnp.concatenate(parts, axis=0)
    m_ref[...] = jnp.full(m_ref.shape, NEG_FILL, F32)
    l_ref[...] = jnp.zeros(l_ref.shape, F32)
    acc[...] = jnp.zeros(acc.shape, F32)
    scale = head ** (-0.5) * LOG2E

    def one_tile(t, carry):
        @pl.when(tiles_ref[0, t] <= 2 * RADIUS)
        def _():
            pltpu.make_async_copy(bufs[0], tile_vmem.at[t], sems.at[t]).wait()
            for h in range(HEADS):
                pair = h // 2
                base = width + (pair // 2) * rows
                keys = tile_vmem[t, base : base + rows, (pair % 2) * LANES : (pair % 2 + 1) * LANES]
                scores = dot(keys, qz[h])
                old = m_ref[h : h + 1, :]
                new = jnp.maximum(old, jnp.max(scores, axis=0, keepdims=True))
                alpha = jnp.exp2((old - new) * scale)
                w = jnp.exp2((scores - new) * scale)
                l_ref[h : h + 1, :] = l_ref[h : h + 1, :] * alpha + jnp.sum(w, axis=0, keepdims=True)
                m_ref[h : h + 1, :] = new
                mine = slice(h * head, (h + 1) * head)
                acc[mine, :] = acc[mine, :] * alpha + dot(tile_vmem[t, mine, :], w.astype(BF16))

        return carry

    lax.fori_loop(0, n_tiles, one_tile, 0)
    acc_out[...] = acc[...].T
    pad = jnp.zeros((LANES - 2 * HEADS, rows), F32)
    stat_out[...] = jnp.concatenate([m_ref[...], l_ref[...], pad], axis=0).T


def finish_kernel(groups, q_ref, order_ref, bias_ref, acc_ref, stat_ref, w_ref, *refs):
    bucket_refs = refs[:groups]
    out_ref = refs[groups]
    rows, width = q_ref.shape
    head = width // HEADS
    bucket = rows // groups
    scale = head ** (-0.5) * LOG2E
    unscale = head**0.5
    gather = (
        lax.broadcasted_iota(jnp.int32, (width, LANES), 0) // head
        == lax.broadcasted_iota(jnp.int32, (width, LANES), 1)
    )
    gather = jnp.where(gather, 1.0, 0.0).astype(BF16)
    spread = (
        lax.broadcasted_iota(jnp.int32, (LANES, width), 1) // head
        == lax.broadcasted_iota(jnp.int32, (LANES, width), 0)
    )
    spread = jnp.where(spread, 1.0, 0.0).astype(BF16)
    queries = q_ref[...].astype(F32)
    stat = stat_ref[...]
    lane = lax.broadcasted_iota(jnp.int32, stat.shape, 1)
    block_max = jnp.where(lane < HEADS, stat, 0.0)
    block_sum = jnp.where(lane < HEADS, jnp.roll(stat, -HEADS, axis=1), 1.0)
    edge_scores = []
    edge_vals = []
    for j in range(MATCHINGS):
        table = place_table(order_ref[j : j + 1, :], rows)
        mine = slice(j * bucket, (j + 1) * bucket)
        in_order = jnp.concatenate([ref[mine, :] for ref in bucket_refs], axis=0)
        partner = dot(table, in_order)
        prod = queries * partner[:, :width]
        high = prod.astype(BF16)
        low = (prod - high.astype(F32)).astype(BF16)
        edge = dot(high, gather) + dot(low, gather)
        edge_scores.append(edge + bias_ref[j : j + 1, :] * unscale)
        edge_vals.append(partner[:, width:])
    top = block_max
    for edge in edge_scores:
        top = jnp.maximum(top, edge)
    keep = jnp.exp2((block_max - top) * scale)
    edge_w = [jnp.exp2((edge - top) * scale) for edge in edge_scores]
    total = block_sum * keep
    for u in edge_w:
        total = total + u
    inv = 1.0 / total

    def wide(x):
        high = x.astype(BF16)
        low = (x - high.astype(F32)).astype(BF16)
        return dot(high, spread) + dot(low, spread)

    numer = acc_ref[...] * wide(keep)
    for u, vals in zip(edge_w, edge_vals):
        numer = numer + dot(u.astype(BF16), spread) * vals
    attended = (numer * wide(inv)).astype(BF16)
    out_ref[...] = dot(attended, w_ref[...]).astype(BF16)


def vmem_specs(n):
    return [pl.BlockSpec(memory_space=pltpu.VMEM)] * n


def shards(groups, loop_size, queries, key_rows, value_rows, out_weight, tile_list, expander_order, expander_bias):
    rows, width = queries.shape
    head = width // HEADS
    bucket = rows // groups
    params = pltpu.CompilerParams(vmem_limit_bytes=VMEM_BYTES)
    tile_shape = jax.ShapeDtypeStruct((width + 2 * rows, width // 2), BF16)
    bucket_shape = jax.ShapeDtypeStruct((MATCHINGS * bucket, 2 * width), BF16)
    own_tile, *outgoing = pl.pallas_call(
        functools.partial(prep_kernel, groups),
        out_shape=[tile_shape] + [bucket_shape] * groups,
        in_specs=vmem_specs(3),
        out_specs=vmem_specs(1 + groups),
        compiler_params=params,
        name="prep",
    )(key_rows, value_rows, expander_order)

    def over_grp(array, b):
        return lax.ppermute(array, "grp", [(i, i ^ b) for i in range(groups)])

    incoming = {b: over_grp(outgoing[b], b) for b in range(groups - 1, 0, -1)}

    def flipped(array, bits):
        return lax.ppermute(array, "loop", [(i, i ^ bits) for i in range(loop_size)])

    if loop_size == 8:
        side = flipped(own_tile, 2)
        across = flipped(own_tile, 5)
        twin = flipped(own_tile, 1)
        corner = flipped(side, 4)
        side_twin = flipped(side, 1)
        corner_twin = flipped(corner, 1)
        tiles = [own_tile, twin, side, side_twin, across, corner, corner_twin]
    else:
        tiles = []
        for offset in range(-RADIUS, RADIUS + 1):
            pairs = [(i, (i - offset) % loop_size) for i in range(loop_size)]
            tiles.append(lax.ppermute(own_tile, "loop", pairs) if offset else own_tile)

    acc, stat = pl.pallas_call(
        functools.partial(blocks_kernel, loop_size),
        out_shape=[
            jax.ShapeDtypeStruct((rows, width), F32),
            jax.ShapeDtypeStruct((rows, LANES), F32),
        ],
        in_specs=[pl.BlockSpec(memory_space=pltpu.SMEM)]
        + vmem_specs(1)
        + [pl.BlockSpec(memory_space=pl.ANY)] * len(tiles),
        out_specs=vmem_specs(2),
        scratch_shapes=[
            pltpu.VMEM((tile_list.shape[1],) + tile_shape.shape, BF16),
            pltpu.VMEM((HEADS, 2 * head, rows), BF16),
            pltpu.VMEM((width, rows), F32),
            pltpu.VMEM((HEADS, rows), F32),
            pltpu.VMEM((HEADS, rows), F32),
            pltpu.SemaphoreType.DMA((tile_list.shape[1],)),
        ],
        compiler_params=params,
        name="blocks",
    )(tile_list, queries, *tiles)

    bias = jnp.pad(expander_bias, ((0, 0), (0, LANES - HEADS)))
    buckets = [outgoing[0]] + [incoming[b] for b in range(1, groups)]
    return pl.pallas_call(
        functools.partial(finish_kernel, groups),
        out_shape=jax.ShapeDtypeStruct((rows, width), BF16),
        in_specs=vmem_specs(6 + groups),
        out_specs=pl.BlockSpec(memory_space=pltpu.VMEM),
        compiler_params=params,
        name="finish",
    )(queries, expander_order, bias, acc, stat, out_weight, *buckets)


def solution(mesh):
    placed = (
        P(("loop", "grp"), None),
        P(("loop", "grp"), None),
        P(("loop", "grp"), None),
        P(),
        P(("loop", "grp"), None),
        P(None, ("loop", "grp")),
        P(),
    )
    return jax.shard_map(
        functools.partial(shards, mesh.shape["grp"], mesh.shape["loop"]),
        mesh=mesh,
        in_specs=placed,
        out_specs=P(("loop", "grp"), None),
        check_vma=False,
    )
```

profile of v0, /device:TPU:14, one launch (start us, length us, event | category | flops | bytes accessed | tf_op | source)
XLA Modules:
  0.0 72.6 jit_solution(14229316361328735481)
XLA Ops:
  0.0 0.0 copy-start
  0.0 0.0 copy-start.2
  0.0 1.0 %copy-done.2 = bf16[256,512]{1,0:T(8,128)(2,1)S(1)} copy-done((bf16[256,512]{1,0:T(8,128)(2,1)S(1)}, bf16[256,512]{1,0:T(8,128)(2,1)}, u32[]{:S(2)}) %copy-start.2) | copy-done | bytes 262168
  1.0 0.0 copy-start.3
  1.0 0.9 %copy-done.3 = bf16[256,512]{1,0:T(8,128)(2,1)S(1)} copy-done((bf16[256,512]{1,0:T(8,128)(2,1)S(1)}, bf16[256,512]{1,0:T(8,128)(2,1)}, u32[]{:S(2)}) %copy-start.3) | copy-done | bytes 262168
  1.9 0.0 copy-start.4
  1.9 0.7 copy-done.4
  2.6 0.7 prep.1
  3.3 0.6 collective-permute-start.1
  3.9 13.1 %collective-permute-done.1.refs_2_ = bf16[1024,256]{1,0:T(8,128)(2,1)S(1)} collective-permute-done((bf16[1024,256]{1,0:T(8,128)(2,1)S(1)}, bf16[1024,256]{1,0:T(8,128)(2,1)S(1)}, u32[]{:S(2)}, u32[]{:S(2)}) %collective-permute-start.1) | collective-permute-done | bytes 524320 | tf_op jit(solution)/shard_map/ppermute | solution.py:201
  17.0 0.5 collective-permute-start.4
  17.5 0.0 collective-permute-start
  17.6 1.6 %collective-permute-start.3 = (bf16[1024,256]{1,0:T(8,128)(2,1)S(1)}, bf16[1024,256]{1,0:T(8,128)(2,1)S(1)}, u32[]{:S(2)}, u32[]{:S(2)}) collective-permute-start(bf16[1024,256]{1,0:T(8,128)(2,1)S(1)} %get-tuple-element.12.refs_0_), channel_id=1, source_target_pairs={{0,20},{4,16},{8,28},{12,24},{16,4},{20,0},{24,12},{28,8},{1,21},{... | collective-permute-start | bytes 1572872 | tf_op jit(solution)/shard_map/ppermute | solution.py:201
  19.2 0.0 collective-permute-start.2
  19.2 12.7 %collective-permute-done.4.refs_5_ = bf16[1024,256]{1,0:T(8,128)(2,1)S(1)} collective-permute-done((bf16[1024,256]{1,0:T(8,128)(2,1)S(1)}, bf16[1024,256]{1,0:T(8,128)(2,1)S(1)}, u32[]{:S(2)}, u32[]{:S(2)}) %collective-permute-start.4) | collective-permute-done | bytes 524320 | tf_op jit(solution)/shard_map/ppermute | solution.py:201
  31.9 0.0 collective-permute-start.5
  31.9 0.0 copy-start.7
  31.9 0.4 collective-permute-start.6
  32.4 0.0 collective-permute-done.refs_1_
  32.4 2.6 %collective-permute-start.7 = (bf16[192,1024]{1,0:T(8,128)(2,1)S(1)}, bf16[192,1024]{1,0:T(8,128)(2,1)S(1)}, u32[]{:S(2)}, u32[]{:S(2)}) collective-permute-start(bf16[192,1024]{1,0:T(8,128)(2,1)S(1)} %get-tuple-element.17), channel_id=1, source_target_pairs={{0,2},{1,3},{2,0},{3,1},{4,6},{5,7},{6,4},{7,5},{8,10},{9,11},{10,... | collective-permute-start | bytes 1179656 | tf_op jit(solution)/shard_map/ppermute | solution.py:196
  35.0 4.1 %collective-permute-done.3.refs_4_ = bf16[1024,256]{1,0:T(8,128)(2,1)S(1)} collective-permute-done((bf16[1024,256]{1,0:T(8,128)(2,1)S(1)}, bf16[1024,256]{1,0:T(8,128)(2,1)S(1)}, u32[]{:S(2)}, u32[]{:S(2)}) %collective-permute-start.3) | collective-permute-done | bytes 524320 | tf_op jit(solution)/shard_map/ppermute | solution.py:201
  39.1 0.0 copy-start.6
  39.1 1.6 %collective-permute-start.8 = (bf16[192,1024]{1,0:T(8,128)(2,1)S(1)}, bf16[192,1024]{1,0:T(8,128)(2,1)S(1)}, u32[]{:S(2)}, u32[]{:S(2)}) collective-permute-start(bf16[192,1024]{1,0:T(8,128)(2,1)S(1)} %get-tuple-element.18), channel_id=1, source_target_pairs={{0,3},{1,2},{2,1},{3,0},{4,7},{5,6},{6,5},{7,4},{8,11},{9,10},{10,... | collective-permute-start | bytes 1179656 | tf_op jit(solution)/shard_map/ppermute | solution.py:196
  40.7 0.0 copy-done.7
  40.7 0.0 copy-start.1
  40.7 0.0 collective-permute-done.2.refs_3_
  40.7 0.0 collective-permute-done.5.refs_6_
  40.7 0.0 copy-done
  40.7 0.0 copy-done.6
  40.7 7.9 %blocks.1 = (f32[256,512]{1,0:T(8,128)S(1)}, f32[256,128]{1,0:T(8,128)S(1)}) custom-call(s32[1,4]{1,0:T(1,128)S(1)} %copy-done.6, bf16[256,512]{1,0:T(8,128)(2,1)S(1)} %copy-done, bf16[1024,256]{1,0:T(8,128)(2,1)S(1)} %get-tuple-element.12.refs_0_, bf16[1024,256]{1,0:T(8,128)(2,1)S(1)} %collective-permute-done.refs_1_, ...), custom_call_target="tpu_custom_call" | custom-call | tf_op jit(solution)/shard_map/blocks/pallas_call | solution.py:217
  48.6 0.0 copy-start.5
  48.6 0.8 %collective-permute-done.6.refs_1_ = bf16[192,1024]{1,0:T(8,128)(2,1)S(1)} collective-permute-done((bf16[192,1024]{1,0:T(8,128)(2,1)S(1)}, bf16[192,1024]{1,0:T(8,128)(2,1)S(1)}, u32[]{:S(2)}, u32[]{:S(2)}) %collective-permute-start.6) | collective-permute-done | bytes 393248 | tf_op jit(solution)/shard_map/ppermute | solution.py:196
  49.4 11.9 %collective-permute-done.7.refs_2_ = bf16[192,1024]{1,0:T(8,128)(2,1)S(1)} collective-permute-done((bf16[192,1024]{1,0:T(8,128)(2,1)S(1)}, bf16[192,1024]{1,0:T(8,128)(2,1)S(1)}, u32[]{:S(2)}, u32[]{:S(2)}) %collective-permute-start.7) | collective-permute-done | bytes 393248 | tf_op jit(solution)/shard_map/ppermute | solution.py:196
  61.3 8.6 %collective-permute-done.8.refs_3_ = bf16[192,1024]{1,0:T(8,128)(2,1)S(1)} collective-permute-done((bf16[192,1024]{1,0:T(8,128)(2,1)S(1)}, bf16[192,1024]{1,0:T(8,128)(2,1)S(1)}, u32[]{:S(2)}, u32[]{:S(2)}) %collective-permute-start.8) | collective-permute-done | bytes 393248 | tf_op jit(solution)/shard_map/ppermute | solution.py:196
  70.0 0.0 copy-done.1
  70.0 0.0 copy-done.5
  70.0 2.6 %finish.1 = bf16[256,512]{1,0:T(8,128)(2,1)} custom-call(bf16[256,512]{1,0:T(8,128)(2,1)S(1)} %copy-done, s32[3,256]{1,0:T(4,128)S(1)} %copy-done.5, f32[3,128]{1,0:T(4,128)S(1)} %pad.4.bias_ref, f32[256,512]{1,0:T(8,128)S(1)} %get-tuple-element.13.acc_ref, f32[256,128]{1,0:T(8,128)S(1)} %get-tuple-element.14.stat_ref, bf16[512,512]{1,0:T(8,128)(2,1)S(1)} %copy-done.1, ...), custom_call_target="tpu_custom_call" | custom-call | tf_op jit(solution)/shard_map/finish/pallas_call | solution.py:241
  (1 shorter events, 0.0 us)
Async XLA Ops:
  0.0 40.7 %copy-start = (bf16[256,512]{1,0:T(8,128)(2,1)S(1)}, bf16[256,512]{1,0:T(8,128)(2,1)}, u32[]{:S(2)}) copy-start(bf16[256,512]{1,0:T(8,128)(2,1)} %q_ref.3) | copy-start | bytes 786436
  0.0 1.0 %copy-start.2 = (bf16[256,512]{1,0:T(8,128)(2,1)S(1)}, bf16[256,512]{1,0:T(8,128)(2,1)}, u32[]{:S(2)}) copy-start(bf16[256,512]{1,0:T(8,128)(2,1)} %k_ref.1) | copy-start | bytes 786436
  1.0 0.9 %copy-start.3 = (bf16[256,512]{1,0:T(8,128)(2,1)S(1)}, bf16[256,512]{1,0:T(8,128)(2,1)}, u32[]{:S(2)}) copy-start(bf16[256,512]{1,0:T(8,128)(2,1)} %v_ref.1) | copy-start | bytes 786436
  1.9 0.7 copy-start.4
  3.3 13.7 %collective-permute-start.1 = (bf16[1024,256]{1,0:T(8,128)(2,1)S(1)}, bf16[1024,256]{1,0:T(8,128)(2,1)S(1)}, u32[]{:S(2)}, u32[]{:S(2)}) collective-permute-start(bf16[1024,256]{1,0:T(8,128)(2,1)S(1)} %get-tuple-element.12.refs_0_), channel_id=1, source_target_pairs={{0,8},{4,12},{8,0},{12,4},{16,24},{20,28},{24,16},{28,20},{1,9},{5... | collective-permute-start | bytes 1572872 | tf_op jit(solution)/shard_map/ppermute | solution.py:201
  17.0 14.9 %collective-permute-start.4 = (bf16[1024,256]{1,0:T(8,128)(2,1)S(1)}, bf16[1024,256]{1,0:T(8,128)(2,1)S(1)}, u32[]{:S(2)}, u32[]{:S(2)}) collective-permute-start(bf16[1024,256]{1,0:T(8,128)(2,1)S(1)} %collective-permute-done.1.refs_2_), channel_id=1, source_target_pairs={{0,16},{4,20},{8,24},{12,28},{16,0},{20,4},{24,8},{28,12},{1,17},{... | collective-permute-start | bytes 1572872 | tf_op jit(solution)/shard_map/ppermute | solution.py:201
  17.5 14.8 %collective-permute-start = (bf16[1024,256]{1,0:T(8,128)(2,1)S(1)}, bf16[1024,256]{1,0:T(8,128)(2,1)S(1)}, u32[]{:S(2)}, u32[]{:S(2)}) collective-permute-start(bf16[1024,256]{1,0:T(8,128)(2,1)S(1)} %get-tuple-element.12.refs_0_), channel_id=1, source_target_pairs={{0,4},{4,0},{8,12},{12,8},{16,20},{20,16},{24,28},{28,24},{1,5},{5... | collective-permute-start | bytes 1572872 | tf_op jit(solution)/shard_map/ppermute | solution.py:201
  17.6 21.5 %collective-permute-start.3 = (bf16[1024,256]{1,0:T(8,128)(2,1)S(1)}, bf16[1024,256]{1,0:T(8,128)(2,1)S(1)}, u32[]{:S(2)}, u32[]{:S(2)}) collective-permute-start(bf16[1024,256]{1,0:T(8,128)(2,1)S(1)} %get-tuple-element.12.refs_0_), channel_id=1, source_target_pairs={{0,20},{4,16},{8,28},{12,24},{16,4},{20,0},{24,12},{28,8},{1,21},{... | collective-permute-start | bytes 1572872 | tf_op jit(solution)/shard_map/ppermute | solution.py:201
  19.2 21.5 %collective-permute-start.2 = (bf16[1024,256]{1,0:T(8,128)(2,1)S(1)}, bf16[1024,256]{1,0:T(8,128)(2,1)S(1)}, u32[]{:S(2)}, u32[]{:S(2)}) collective-permute-start(bf16[1024,256]{1,0:T(8,128)(2,1)S(1)} %collective-permute-done.1.refs_2_), channel_id=1, source_target_pairs={{0,4},{4,0},{8,12},{12,8},{16,20},{20,16},{24,28},{28,24},{1,5},{5... | collective-permute-start | bytes 1572872 | tf_op jit(solution)/shard_map/ppermute | solution.py:201
  31.9 8.8 %collective-permute-start.5 = (bf16[1024,256]{1,0:T(8,128)(2,1)S(1)}, bf16[1024,256]{1,0:T(8,128)(2,1)S(1)}, u32[]{:S(2)}, u32[]{:S(2)}) collective-permute-start(bf16[1024,256]{1,0:T(8,128)(2,1)S(1)} %collective-permute-done.4.refs_5_), channel_id=1, source_target_pairs={{0,4},{4,0},{8,12},{12,8},{16,20},{20,16},{24,28},{28,24},{1,5},{5... | collective-permute-start | bytes 1572872 | tf_op jit(solution)/shard_map/ppermute | solution.py:201
  31.9 8.8 %copy-start.7 = (f32[3,8]{1,0:T(4,128)S(1)}, f32[3,8]{1,0:T(4,128)}, u32[]{:S(2)}) copy-start(f32[3,8]{1,0:T(4,128)} %param.13) | copy-start | bytes 292
  31.9 17.5 %collective-permute-start.6 = (bf16[192,1024]{1,0:T(8,128)(2,1)S(1)}, bf16[192,1024]{1,0:T(8,128)(2,1)S(1)}, u32[]{:S(2)}, u32[]{:S(2)}) collective-permute-start(bf16[192,1024]{1,0:T(8,128)(2,1)S(1)} %get-tuple-element.16), channel_id=1, source_target_pairs={{0,1},{1,0},{2,3},{3,2},{4,5},{5,4},{6,7},{7,6},{8,9},{9,8},{10,11... | collective-permute-start | bytes 1179656 | tf_op jit(solution)/shard_map/ppermute | solution.py:196
  32.4 29.0 %collective-permute-start.7 = (bf16[192,1024]{1,0:T(8,128)(2,1)S(1)}, bf16[192,1024]{1,0:T(8,128)(2,1)S(1)}, u32[]{:S(2)}, u32[]{:S(2)}) collective-permute-start(bf16[192,1024]{1,0:T(8,128)(2,1)S(1)} %get-tuple-element.17), channel_id=1, source_target_pairs={{0,2},{1,3},{2,0},{3,1},{4,6},{5,7},{6,4},{7,5},{8,10},{9,11},{10,... | collective-permute-start | bytes 1179656 | tf_op jit(solution)/shard_map/ppermute | solution.py:196
  39.1 1.6 %copy-start.6 = (s32[1,4]{1,0:T(1,128)S(1)}, s32[1,4]{1,0:T(1,128)}, u32[]{:S(2)}) copy-start(s32[1,4]{1,0:T(1,128)} %tiles_ref.1) | copy-start | bytes 52
  39.1 30.9 %collective-permute-start.8 = (bf16[192,1024]{1,0:T(8,128)(2,1)S(1)}, bf16[192,1024]{1,0:T(8,128)(2,1)S(1)}, u32[]{:S(2)}, u32[]{:S(2)}) collective-permute-start(bf16[192,1024]{1,0:T(8,128)(2,1)S(1)} %get-tuple-element.18), channel_id=1, source_target_pairs={{0,3},{1,2},{2,1},{3,0},{4,7},{5,6},{6,5},{7,4},{8,11},{9,10},{10,... | collective-permute-start | bytes 1179656 | tf_op jit(solution)/shard_map/ppermute | solution.py:196
  40.7 29.3 %copy-start.1 = (bf16[512,512]{1,0:T(8,128)(2,1)S(1)}, bf16[512,512]{1,0:T(8,128)(2,1)}, u32[]{:S(2)}) copy-start(bf16[512,512]{1,0:T(8,128)(2,1)} %w_ref.1) | copy-start | bytes 1572868
  48.6 21.3 %copy-start.5 = (s32[3,256]{1,0:T(4,128)S(1)}, s32[3,256]{1,0:T(4,128)}, u32[]{:S(2)}) copy-start(s32[3,256]{1,0:T(4,128)} %order_ref.3) | copy-start | bytes 9220
where the time goes:
time: 72.7 us; the launch traced here: 72.6 us
  waiting for transfers between devices  51.3 us (71%)
  Pallas kernels  11.2 us (15%)
  starting transfers between devices  7.36 us (10%)
  local copies, waits for them, and re-layouts  2.65 us (4%)
    ppermute x6, waiting for transfers between devices, flipped(): lax.ppermute(array, 'loop', [(i, i ^ bits) for i in range(loop_size)])  30 us
    ppermute x3, waiting for transfers between devices, over_grp(): return lax.ppermute(array, 'grp', [(i, i ^ b) for i in range(groups)])  21.3 us
    pallas_call x1, Pallas kernels, shards(): pl.pallas_call(functools.partial(blocks_kernel, loop_size), out_shape=[ja...  7.88 us
    ppermute x3, starting transfers between devices, over_grp(): return lax.ppermute(array, 'grp', [(i, i ^ b) for i in range(groups)])  4.62 us
    ppermute x6, starting transfers between devices, flipped(): lax.ppermute(array, 'loop', [(i, i ^ bits) for i in range(loop_size)])  2.75 us
    unnamed x16, local copies, waits for them, and re-layouts  2.65 us
    pallas_call x1, Pallas kernels, shards(): pl.pallas_call(functools.partial(finish_kernel, groups), out_shape=jax.Sh...  2.61 us
  transfers between devices with their start and end apart: 9, of which 6 were waited for; matrix products, arithmetic and copies ran while one was open for 0% of the time, Pallas kernels for 11%

commit v1 on v0

--- a/solution.py
+++ b/solution.py
@@ -28,10 +28,19 @@
     return jnp.where(row_ids == order_row, 1.0, 0.0).astype(BF16)
 
 
-def prep_kernel(groups, k_ref, v_ref, order_ref, tile_ref, *bucket_refs):
+def prep_kernel(groups, k_hbm, v_hbm, order_hbm, tile_ref, out_ref, k_ref, v_ref, order_ref, sems):
     rows, width = k_ref.shape
     bucket = rows // groups
     half = width // 2
+    group = lax.axis_index("grp")
+    copies = [
+        pltpu.make_async_copy(src, dst, sems.at[i])
+        for i, (src, dst) in enumerate(((order_hbm, order_ref), (k_hbm, k_ref), (v_hbm, v_ref)))
+    ]
+    for copy in copies:
+        copy.start()
+    for copy in copies:
+        copy.wait()
     keys = k_ref[...]
     vals = v_ref[...]
     order = order_ref[...]
@@ -43,39 +52,58 @@
         ordered_k = dot(table, keys, ((0,), (0,))).astype(BF16)
         ordered_v = dot(table, vals, ((0,), (0,))).astype(BF16)
         for b in range(groups):
-            out = slice(j * bucket, (j + 1) * bucket)
-            bucket_refs[b][out, :width] = ordered_k[b * bucket : (b + 1) * bucket]
-            bucket_refs[b][out, width:] = ordered_v[b * bucket : (b + 1) * bucket]
+            mine = slice(j * bucket, (j + 1) * bucket)
+            out_ref[group ^ b, mine, :width] = ordered_k[b * bucket : (b + 1) * bucket]
+            out_ref[group ^ b, mine, width:] = ordered_v[b * bucket : (b + 1) * bucket]
     tile_ref[:width, :] = vals.T
     tile_ref[width : width + rows, :] = keys[:, :half]
     tile_ref[width + rows :, :] = keys[:, half:]
 
 
-def blocks_kernel(loop_size, tiles_ref, q_ref, *refs):
+def blocks_kernel(loop_size, served, first, last, tiles_ref, q_ref, *refs):
     n_bufs = 2 * RADIUS + 1
-    bufs = refs[:n_bufs]
-    acc_out, stat_out, tile_vmem, qz, acc, m_ref, l_ref, sems = refs[n_bufs:]
     rows, width = q_ref.shape
     head = width // HEADS
     n_tiles = tiles_ref.shape[1]
+    refs = list(refs)
+    bufs = {}
+    for slot, split in served.items():
+        if split:
+            bufs[slot] = (refs.pop(0), refs.pop(0))
+        else:
+            whole = refs.pop(0)
+            bufs[slot] = (whole.at[:width, :], whole.at[width:, :])
+    state = () if first else (refs.pop(0), refs.pop(0))
+    acc_out, stat_out = refs.pop(0), refs.pop(0)
+    tile_vmem, qz, acc, m_ref, l_ref, sems = refs
     here = lax.axis_index("loop")
 
-    def buffer_of(t):
+    def slot_of(t):
         offset = tiles_ref[0, t]
+        slot = offset
         if loop_size == 8:
             away = here ^ lax.rem(here + offset - RADIUS + loop_size, loop_size)
             slot = jnp.where(away > 4, away - 1, away)
-        else:
-            slot = offset
-        return slot, offset <= 2 * RADIUS
+        return jnp.where(offset <= 2 * RADIUS, slot, n_bufs)
+
+    def here_served(slot):
+        return functools.reduce(jnp.logical_or, [slot == k for k in served])
+
+    def halves(slot, t):
+        vals, keys = bufs[slot]
+        return (
+            pltpu.make_async_copy(vals, tile_vmem.at[t, :width, :], sems.at[t, 0]),
+            pltpu.make_async_copy(keys, tile_vmem.at[t, width:, :], sems.at[t, 1]),
+        )
 
     for t in range(n_tiles):
-        slot, live = buffer_of(t)
-        for k in range(n_bufs):
-
-            @pl.when(live & (slot == k))
+        slot = slot_of(t)
+        for k in served:
+
+            @pl.when(slot == k)
             def _():
-                pltpu.make_async_copy(bufs[k], tile_vmem.at[t], sems.at[t]).start()
+                for copy in halves(k, t):
+                    copy.start()
 
     q_t = q_ref[...].T
     zeros = jnp.zeros((head, rows), BF16)
@@ -83,15 +111,21 @@
         mine = q_t[h * head : (h + 1) * head]
         parts = (mine, zeros) if h % 2 == 0 else (zeros, mine)
         qz[h] = jnp.concatenate(parts, axis=0)
-    m_ref[...] = jnp.full(m_ref.shape, NEG_FILL, F32)
-    l_ref[...] = jnp.zeros(l_ref.shape, F32)
-    acc[...] = jnp.zeros(acc.shape, F32)
+    if first:
+        m_ref[...] = jnp.full(m_ref.shape, NEG_FILL, F32)
+        l_ref[...] = jnp.zeros(l_ref.shape, F32)
+        acc[...] = jnp.zeros(acc.shape, F32)
+    else:
+        acc[...] = state[0][...]
+        m_ref[...] = state[1][:HEADS]
+        l_ref[...] = state[1][HEADS:]
     scale = head ** (-0.5) * LOG2E
 
     def one_tile(t, carry):
-        @pl.when(tiles_ref[0, t] <= 2 * RADIUS)
+        @pl.when(here_served(slot_of(t)))
         def _():
-            pltpu.make_async_copy(bufs[0], tile_vmem.at[t], sems.at[t]).wait()
+            for copy in halves(next(iter(served)), t):
+                copy.wait()
             for h in range(HEADS):
                 pair = h // 2
                 base = width + (pair // 2) * rows
@@ -109,14 +143,18 @@
         return carry
 
     lax.fori_loop(0, n_tiles, one_tile, 0)
-    acc_out[...] = acc[...].T
-    pad = jnp.zeros((LANES - 2 * HEADS, rows), F32)
-    stat_out[...] = jnp.concatenate([m_ref[...], l_ref[...], pad], axis=0).T
-
-
-def finish_kernel(groups, q_ref, order_ref, bias_ref, acc_ref, stat_ref, w_ref, *refs):
-    bucket_refs = refs[:groups]
-    out_ref = refs[groups]
+    if last:
+        acc_out[...] = acc[...].T
+        pad = jnp.zeros((LANES - 2 * HEADS, rows), F32)
+        stat_out[...] = jnp.concatenate([m_ref[...], l_ref[...], pad], axis=0).T
+    else:
+        acc_out[...] = acc[...]
+        stat_out[:HEADS] = m_ref[...]
+        stat_out[HEADS:] = l_ref[...]
+
+
+def finish_kernel(groups, q_ref, order_ref, bias_ref, acc_ref, stat_ref, w_ref, come_ref, out_ref):
+    group = lax.axis_index("grp")
     rows, width = q_ref.shape
     head = width // HEADS
     bucket = rows // groups
@@ -142,7 +180,8 @@
     for j in range(MATCHINGS):
         table = place_table(order_ref[j : j + 1, :], rows)
         mine = slice(j * bucket, (j + 1) * bucket)
-        in_order = jnp.concatenate([ref[mine, :] for ref in bucket_refs], axis=0)
+        come = [come_ref[group ^ b, mine, :] for b in range(1, groups)]
+        in_order = jnp.concatenate([come_ref[group, mine, :]] + come, axis=0)
         partner = dot(table, in_order)
         prod = queries * partner[:, :width]
         high = prod.astype(BF16)
@@ -182,70 +221,84 @@
     bucket = rows // groups
     params = pltpu.CompilerParams(vmem_limit_bytes=VMEM_BYTES)
     tile_shape = jax.ShapeDtypeStruct((width + 2 * rows, width // 2), BF16)
-    bucket_shape = jax.ShapeDtypeStruct((MATCHINGS * bucket, 2 * width), BF16)
-    own_tile, *outgoing = pl.pallas_call(
+    bucket_shape = jax.ShapeDtypeStruct((groups, MATCHINGS * bucket, 2 * width), BF16)
+    own_tile, outgoing = pl.pallas_call(
         functools.partial(prep_kernel, groups),
-        out_shape=[tile_shape] + [bucket_shape] * groups,
-        in_specs=vmem_specs(3),
-        out_specs=vmem_specs(1 + groups),
+        out_shape=[tile_shape, bucket_shape],
+        in_specs=[pl.BlockSpec(memory_space=pltpu.HBM)] * 3,
+        out_specs=vmem_specs(2),
+        scratch_shapes=[
+            pltpu.VMEM((rows, width), BF16),
+            pltpu.VMEM((rows, width), BF16),
+            pltpu.VMEM(expander_order.shape, jnp.int32),
+            pltpu.SemaphoreType.DMA((3,)),
+        ],
         compiler_params=params,
         name="prep",
     )(key_rows, value_rows, expander_order)
 
-    def over_grp(array, b):
-        return lax.ppermute(array, "grp", [(i, i ^ b) for i in range(groups)])
-
-    incoming = {b: over_grp(outgoing[b], b) for b in range(groups - 1, 0, -1)}
+    incoming = lax.all_to_all(outgoing, "grp", split_axis=0, concat_axis=0, tiled=True)
 
     def flipped(array, bits):
         return lax.ppermute(array, "loop", [(i, i ^ bits) for i in range(loop_size)])
+
+    def attend(served, state, last):
+        slots = {slot: len(arrays) == 2 for slot, arrays in served.items()}
+        arrays = [array for group in served.values() for array in group]
+        if last:
+            acc_shape, stat_shape = (rows, width), (rows, LANES)
+        else:
+            acc_shape, stat_shape = (width, rows), (2 * HEADS, rows)
+        return pl.pallas_call(
+            functools.partial(blocks_kernel, loop_size, slots, not state, last),
+            out_shape=[jax.ShapeDtypeStruct(acc_shape, F32), jax.ShapeDtypeStruct(stat_shape, F32)],
+            in_specs=[pl.BlockSpec(memory_space=pltpu.SMEM)]
+            + vmem_specs(1)
+            + [pl.BlockSpec(memory_space=pl.ANY)] * len(arrays)
+            + vmem_specs(len(state)),
+            out_specs=vmem_specs(2),
+            scratch_shapes=[
+                pltpu.VMEM((tile_list.shape[1],) + tile_shape.shape, BF16),
+                pltpu.VMEM((HEADS, 2 * head, rows), BF16),
+                pltpu.VMEM((width, rows), F32),
+                pltpu.VMEM((HEADS, rows), F32),
+                pltpu.VMEM((HEADS, rows), F32),
+                pltpu.SemaphoreType.DMA((tile_list.shape[1], 2)),
+            ],
+            compiler_params=params,
+            name="corner_blocks" if state else "blocks",
+        )(tile_list, queries, *arrays, *state)
 
     if loop_size == 8:
         side = flipped(own_tile, 2)
         across = flipped(own_tile, 5)
         twin = flipped(own_tile, 1)
-        corner = flipped(side, 4)
+        side, across = lax.optimization_barrier((side, across))
+        corner_k = flipped(side[width:], 4)
+        corner_v = flipped(across[:width], 3)
         side_twin = flipped(side, 1)
-        corner_twin = flipped(corner, 1)
-        tiles = [own_tile, twin, side, side_twin, across, corner, corner_twin]
+        corner_twin_k = flipped(corner_k, 1)
+        corner_twin_v = flipped(corner_v, 1)
+        state = attend({0: [own_tile], 1: [twin], 2: [side], 3: [side_twin], 4: [across]}, (), False)
+        corners = {5: [corner_v, corner_k], 6: [corner_twin_v, corner_twin_k]}
+        acc, stat = attend(corners, state, True)
     else:
-        tiles = []
+        tiles = {}
         for offset in range(-RADIUS, RADIUS + 1):
             pairs = [(i, (i - offset) % loop_size) for i in range(loop_size)]
-            tiles.append(lax.ppermute(own_tile, "loop", pairs) if offset else own_tile)
-
-    acc, stat = pl.pallas_call(
-        functools.partial(blocks_kernel, loop_size),
-        out_shape=[
-            jax.ShapeDtypeStruct((rows, width), F32),
-            jax.ShapeDtypeStruct((rows, LANES), F32),
-        ],
-        in_specs=[pl.BlockSpec(memory_space=pltpu.SMEM)]
-        + vmem_specs(1)
-        + [pl.BlockSpec(memory_space=pl.ANY)] * len(tiles),
-        out_specs=vmem_specs(2),
-        scratch_shapes=[
-            pltpu.VMEM((tile_list.shape[1],) + tile_shape.shape, BF16),
-            pltpu.VMEM((HEADS, 2 * head, rows), BF16),
-            pltpu.VMEM((width, rows), F32),
-            pltpu.VMEM((HEADS, rows), F32),
-            pltpu.VMEM((HEADS, rows), F32),
-            pltpu.SemaphoreType.DMA((tile_list.shape[1],)),
-        ],
-        compiler_params=params,
-        name="blocks",
-    )(tile_list, queries, *tiles)
+            tile = lax.ppermute(own_tile, "loop", pairs) if offset else own_tile
+            tiles[offset + RADIUS] = [tile]
+        acc, stat = attend(tiles, (), True)
 
     bias = jnp.pad(expander_bias, ((0, 0), (0, LANES - HEADS)))
-    buckets = [outgoing[0]] + [incoming[b] for b in range(1, groups)]
     return pl.pallas_call(
         functools.partial(finish_kernel, groups),
         out_shape=jax.ShapeDtypeStruct((rows, width), BF16),
-        in_specs=vmem_specs(6 + groups),
+        in_specs=vmem_specs(7),
         out_specs=pl.BlockSpec(memory_space=pltpu.VMEM),
         compiler_params=params,
         name="finish",
-    )(queries, expander_order, bias, acc, stat, out_weight, *buckets)
+    )(queries, expander_order, bias, acc, stat, out_weight, incoming)
 
 
 def solution(mesh):

time: 72.7 us -> 50.9 us (0.70)
  the two profiles are of different devices: /device:TPU:14 before, /device:TPU:0 now
where the time goes in v1:
time: 50.9 us; the launch traced here: 50.6 us
  waiting for transfers between devices  20.9 us (41%)
  Pallas kernels  15.6 us (31%)
  starting transfers between devices  11.3 us (22%)
  local copies, waits for them, and re-layouts  2.66 us (5%)
    ppermute x8, waiting for transfers between devices, flipped(): lax.ppermute(array, 'loop', [(i, i ^ bits) for i in range(loop_size)])  20.4 us
    pallas_call x2, Pallas kernels, attend(): pl.pallas_call(functools.partial(blocks_kernel, loop_size, slots, not sta...  11.1 us
    all_to_all x1, starting transfers between devices, shards(): lax.all_to_all(outgoing, 'grp', split_axis=0, concat_axis=0, tiled=True)  6.46 us
    ppermute x8, starting transfers between devices, flipped(): lax.ppermute(array, 'loop', [(i, i ^ bits) for i in range(loop_size)])  4.81 us
    unnamed x16, local copies, waits for them, and re-layouts  2.62 us
    pallas_call x1, Pallas kernels, shards(): pl.pallas_call(functools.partial(finish_kernel, groups), out_shape=jax.Sh...  2.59 us
    pallas_call x1, Pallas kernels, shards(): pl.pallas_call(functools.partial(prep_kernel, groups), out_shape=[tile_sh...  1.92 us
  transfers between devices with their start and end apart: 9, of which 5 were waited for; matrix products, arithmetic and copies ran while one was open for 0% of the time, Pallas kernels for 22%

profile of v1, /device:TPU:0, one launch (start us, length us, event | category | flops | bytes accessed | tf_op | source)
XLA Modules:
  0.0 50.6 jit_solution(16561208362661522973)
XLA Ops:
  0.0 0.0 copy-start.2
  0.0 0.9 %copy-done.2 = bf16[256,512]{1,0:T(8,128)(2,1)S(1)} copy-done((bf16[256,512]{1,0:T(8,128)(2,1)S(1)}, bf16[256,512]{1,0:T(8,128)(2,1)}, u32[]{:S(2)}) %copy-start.2) | copy-done | bytes 262168
  1.0 0.0 copy-start.3
  1.0 0.9 %copy-done.3 = bf16[256,512]{1,0:T(8,128)(2,1)S(1)} copy-done((bf16[256,512]{1,0:T(8,128)(2,1)S(1)}, bf16[256,512]{1,0:T(8,128)(2,1)}, u32[]{:S(2)}) %copy-start.3) | copy-done | bytes 262168
  1.9 0.0 copy-start.4
  1.9 0.7 %copy-done.4 = s32[3,256]{1,0:T(4,128)S(1)} copy-done((s32[3,256]{1,0:T(4,128)S(1)}, s32[3,256]{1,0:T(4,128)}, u32[]{:S(2)}) %copy-start.4) | copy-done | bytes 3096
  2.6 1.9 %prep.1 = (bf16[1024,256]{1,0:T(8,128)(2,1)S(1)}, bf16[4,192,1024]{2,1,0:T(8,128)(2,1)}) custom-call(bf16[256,512]{1,0:T(8,128)(2,1)S(1)} %copy-done.2, bf16[256,512]{1,0:T(8,128)(2,1)S(1)} %copy-done.3, s32[3,256]{1,0:T(4,128)S(1)} %copy-done.4), custom_call_target="tpu_custom_call" | custom-call | tf_op jit(solution)/shard_map/prep/pallas_call | solution.py:225
  4.5 0.0 copy-start.7
  4.5 0.0 copy-start
  4.5 0.0 copy-start.6
  4.5 6.5 %all-to-all-start = ((bf16[4,192,1024]{2,1,0:T(8,128)(2,1)}), bf16[4,192,1024]{2,1,0:T(8,128)(2,1)S(1)}, u32[]{:S(2)}, u32[]{:S(2)}) async-start(bf16[4,192,1024]{2,1,0:T(8,128)(2,1)} %get-tuple-element.20), calls=%async_computation | async-start | bytes 3145728 | tf_op jit(solution)/shard_map/all_to_all | solution.py:240
  11.0 1.5 %collective-permute-start = (bf16[1024,256]{1,0:T(8,128)(2,1)S(1)}, bf16[1024,256]{1,0:T(8,128)(2,1)S(1)}, u32[]{:S(2)}, u32[]{:S(2)}) collective-permute-start(bf16[1024,256]{1,0:T(8,128)(2,1)S(1)} %get-tuple-element.13.refs_0_), channel_id=1, source_target_pairs={{0,8},{4,12},{8,0},{12,4},{16,24},{20,28},{24,16},{28,20},{1,9},{5... | collective-permute-start | bytes 1572872 | tf_op jit(solution)/shard_map/ppermute | solution.py:243
  12.5 0.4 collective-permute-start.1
  12.9 1.2 %collective-permute-start.6 = (bf16[1024,256]{1,0:T(8,128)(2,1)S(1)}, bf16[1024,256]{1,0:T(8,128)(2,1)S(1)}, u32[]{:S(2)}, u32[]{:S(2)}) collective-permute-start(bf16[1024,256]{1,0:T(8,128)(2,1)S(1)} %get-tuple-element.13.refs_0_), channel_id=1, source_target_pairs={{0,4},{4,0},{8,12},{12,8},{16,20},{20,16},{24,28},{28,24},{1,5},{5... | collective-permute-start | bytes 1572872 | tf_op jit(solution)/shard_map/ppermute | solution.py:243
  14.1 10.3 %collective-permute-done.refs_2_ = bf16[1024,256]{1,0:T(8,128)(2,1)S(1)} collective-permute-done((bf16[1024,256]{1,0:T(8,128)(2,1)S(1)}, bf16[1024,256]{1,0:T(8,128)(2,1)S(1)}, u32[]{:S(2)}, u32[]{:S(2)}) %collective-permute-start) | collective-permute-done | bytes 524320 | tf_op jit(solution)/shard_map/ppermute | solution.py:243
  24.4 2.3 %collective-permute-done.1.refs_4_ = bf16[1024,256]{1,0:T(8,128)(2,1)S(1)} collective-permute-done((bf16[1024,256]{1,0:T(8,128)(2,1)S(1)}, bf16[1024,256]{1,0:T(8,128)(2,1)S(1)}, u32[]{:S(2)}, u32[]{:S(2)}) %collective-permute-start.1) | collective-permute-done | bytes 524320 | tf_op jit(solution)/shard_map/ppermute | solution.py:243
  26.7 0.2 collective-permute-start.7
  26.9 0.9 %collective-permute-start.3 = (bf16[512,256]{1,0:T(8,128)(2,1)S(1)}, bf16[512,256]{1,0:T(8,128)(2,1)S(1)}, u32[]{:S(2)}, u32[]{:S(2)}) collective-permute-start(bf16[512,256]{1,0:T(8,128)(2,1)S(1)} %slice.7), channel_id=1, source_target_pairs={{0,16},{4,20},{8,24},{12,28},{16,0},{20,4},{24,8},{28,12},{1,17},{... | collective-permute-start | bytes 786440 | tf_op jit(solution)/shard_map/ppermute | solution.py:243
  27.8 0.4 collective-permute-start.2
  28.2 7.2 %collective-permute-done.3.refs_1_ = bf16[512,256]{1,0:T(8,128)(2,1)S(1)} collective-permute-done((bf16[512,256]{1,0:T(8,128)(2,1)S(1)}, bf16[512,256]{1,0:T(8,128)(2,1)S(1)}, u32[]{:S(2)}, u32[]{:S(2)}) %collective-permute-start.3) | collective-permute-done | bytes 262176 | tf_op jit(solution)/shard_map/ppermute | solution.py:243
  35.5 0.0 collective-permute-start.5
  35.5 0.7 %collective-permute-done.2.refs_0_ = bf16[512,256]{1,0:T(8,128)(2,1)S(1)} collective-permute-done((bf16[512,256]{1,0:T(8,128)(2,1)S(1)}, bf16[512,256]{1,0:T(8,128)(2,1)S(1)}, u32[]{:S(2)}, u32[]{:S(2)}) %collective-permute-start.2) | collective-permute-done | bytes 262176 | tf_op jit(solution)/shard_map/ppermute | solution.py:243
  36.2 0.1 collective-permute-start.4
  36.3 0.0 copy-done.7
  36.3 0.0 collective-permute-done.6.refs_1_
  36.3 0.0 collective-permute-done.7.refs_3_
  36.3 0.0 copy-done
  36.3 0.0 copy-done.6
  36.4 7.7 %blocks.1 = (f32[512,256]{1,0:T(8,128)S(1)}, f32[16,256]{1,0:T(8,128)S(1)}) custom-call(s32[1,4]{1,0:T(1,128)S(1)} %copy-done.6, bf16[256,512]{1,0:T(8,128)(2,1)S(1)} %copy-done, bf16[1024,256]{1,0:T(8,128)(2,1)S(1)} %get-tuple-element.13.refs_0_, bf16[1024,256]{1,0:T(8,128)(2,1)S(1)} %collective-permute-done.6.refs_1_, ...), custom_call_target="tpu_custom_call" | custom-call | tf_op jit(solution)/shard_map/blocks/pallas_call | solution.py:252
  44.1 0.0 copy-start.1
  44.1 0.0 copy-start.5
  44.1 0.0 collective-permute-done.5.refs_3_
  44.1 0.0 collective-permute-done.4.refs_2_
  44.1 3.4 %corner_blocks.1 = (f32[256,512]{1,0:T(8,128)S(1)}, f32[256,128]{1,0:T(8,128)S(1)}) custom-call(s32[1,4]{1,0:T(1,128)S(1)} %copy-done.6, bf16[256,512]{1,0:T(8,128)(2,1)S(1)} %copy-done, bf16[512,256]{1,0:T(8,128)(2,1)S(1)} %collective-permute-done.2.refs_0_, bf16[512,256]{1,0:T(8,128)(2,1)S(1)} %collective-permute-done.3.refs_1_, ...), custom_call_target="tpu_custom_call" | custom-call | tf_op jit(solution)/shard_map/corner_blocks/pallas_call | solution.py:252
  47.5 0.5 all-to-all-done.come_ref
  48.0 0.0 copy-done.1
  48.0 0.0 copy-done.5
  48.0 2.6 %finish.1 = bf16[256,512]{1,0:T(8,128)(2,1)} custom-call(bf16[256,512]{1,0:T(8,128)(2,1)S(1)} %copy-done, s32[3,256]{1,0:T(4,128)S(1)} %copy-done.5, f32[3,128]{1,0:T(4,128)S(1)} %pad.4.bias_ref, f32[256,512]{1,0:T(8,128)S(1)} %get-tuple-element.18.acc_ref, f32[256,128]{1,0:T(8,128)S(1)} %get-tuple-element.19.stat_ref, bf16[512,512]{1,0:T(8,128)(2,1)S(1)} %copy-done.1, ...), custom_call_target="tpu_custom_call" | custom-call | tf_op jit(solution)/shard_map/finish/pallas_call | solution.py:294
  (3 shorter events, 0.0 us)
Async XLA Ops:
  0.0 0.9 %copy-start.2 = (bf16[256,512]{1,0:T(8,128)(2,1)S(1)}, bf16[256,512]{1,0:T(8,128)(2,1)}, u32[]{:S(2)}) copy-start(bf16[256,512]{1,0:T(8,128)(2,1)} %k_hbm.1) | copy-start | bytes 786436
  1.0 0.9 %copy-start.3 = (bf16[256,512]{1,0:T(8,128)(2,1)S(1)}, bf16[256,512]{1,0:T(8,128)(2,1)}, u32[]{:S(2)}) copy-start(bf16[256,512]{1,0:T(8,128)(2,1)} %v_hbm.1) | copy-start | bytes 786436
  1.9 0.7 %copy-start.4 = (s32[3,256]{1,0:T(4,128)S(1)}, s32[3,256]{1,0:T(4,128)}, u32[]{:S(2)}) copy-start(s32[3,256]{1,0:T(4,128)} %order_ref.1) | copy-start | bytes 9220
  4.5 31.8 %copy-start.7 = (f32[3,8]{1,0:T(4,128)S(1)}, f32[3,8]{1,0:T(4,128)}, u32[]{:S(2)}) copy-start(f32[3,8]{1,0:T(4,128)} %param.13) | copy-start | bytes 292
  4.5 31.8 %copy-start = (bf16[256,512]{1,0:T(8,128)(2,1)S(1)}, bf16[256,512]{1,0:T(8,128)(2,1)}, u32[]{:S(2)}) copy-start(bf16[256,512]{1,0:T(8,128)(2,1)} %q_ref.5) | copy-start | bytes 786436
  4.5 31.8 %copy-start.6 = (s32[1,4]{1,0:T(1,128)S(1)}, s32[1,4]{1,0:T(1,128)}, u32[]{:S(2)}) copy-start(s32[1,4]{1,0:T(1,128)} %tiles_ref.3) | copy-start | bytes 52
  4.5 43.4 %all-to-all-start = ((bf16[4,192,1024]{2,1,0:T(8,128)(2,1)}), bf16[4,192,1024]{2,1,0:T(8,128)(2,1)S(1)}, u32[]{:S(2)}, u32[]{:S(2)}) async-start(bf16[4,192,1024]{2,1,0:T(8,128)(2,1)} %get-tuple-element.20), calls=%async_computation | async-start | bytes 3145728 | tf_op jit(solution)/shard_map/all_to_all | solution.py:240
  11.0 13.4 %collective-permute-start = (bf16[1024,256]{1,0:T(8,128)(2,1)S(1)}, bf16[1024,256]{1,0:T(8,128)(2,1)S(1)}, u32[]{:S(2)}, u32[]{:S(2)}) collective-permute-start(bf16[1024,256]{1,0:T(8,128)(2,1)S(1)} %get-tuple-element.13.refs_0_), channel_id=1, source_target_pairs={{0,8},{4,12},{8,0},{12,4},{16,24},{20,28},{24,16},{28,20},{1,9},{5... | collective-permute-start | bytes 1572872 | tf_op jit(solution)/shard_map/ppermute | solution.py:243
  12.5 14.2 %collective-permute-start.1 = (bf16[1024,256]{1,0:T(8,128)(2,1)S(1)}, bf16[1024,256]{1,0:T(8,128)(2,1)S(1)}, u32[]{:S(2)}, u32[]{:S(2)}) collective-permute-start(bf16[1024,256]{1,0:T(8,128)(2,1)S(1)} %get-tuple-element.13.refs_0_), channel_id=1, source_target_pairs={{0,20},{4,16},{8,28},{12,24},{16,4},{20,0},{24,12},{28,8},{1,21},{... | collective-permute-start | bytes 1572872 | tf_op jit(solution)/shard_map/ppermute | solution.py:243
  12.9 23.4 %collective-permute-start.6 = (bf16[1024,256]{1,0:T(8,128)(2,1)S(1)}, bf16[1024,256]{1,0:T(8,128)(2,1)S(1)}, u32[]{:S(2)}, u32[]{:S(2)}) collective-permute-start(bf16[1024,256]{1,0:T(8,128)(2,1)S(1)} %get-tuple-element.13.refs_0_), channel_id=1, source_target_pairs={{0,4},{4,0},{8,12},{12,8},{16,20},{20,16},{24,28},{28,24},{1,5},{5... | collective-permute-start | bytes 1572872 | tf_op jit(solution)/shard_map/ppermute | solution.py:243
  26.7 9.7 %collective-permute-start.7 = (bf16[1024,256]{1,0:T(8,128)(2,1)S(1)}, bf16[1024,256]{1,0:T(8,128)(2,1)S(1)}, u32[]{:S(2)}, u32[]{:S(2)}) collective-permute-start(bf16[1024,256]{1,0:T(8,128)(2,1)S(1)} %collective-permute-done.refs_2_), channel_id=1, source_target_pairs={{0,4},{4,0},{8,12},{12,8},{16,20},{20,16},{24,28},{28,24},{1,5},{5... | collective-permute-start | bytes 1572872 | tf_op jit(solution)/shard_map/ppermute | solution.py:243
  26.9 8.6 %collective-permute-start.3 = (bf16[512,256]{1,0:T(8,128)(2,1)S(1)}, bf16[512,256]{1,0:T(8,128)(2,1)S(1)}, u32[]{:S(2)}, u32[]{:S(2)}) collective-permute-start(bf16[512,256]{1,0:T(8,128)(2,1)S(1)} %slice.7), channel_id=1, source_target_pairs={{0,16},{4,20},{8,24},{12,28},{16,0},{20,4},{24,8},{28,12},{1,17},{... | collective-permute-start | bytes 786440 | tf_op jit(solution)/shard_map/ppermute | solution.py:243
  27.8 8.4 %collective-permute-start.2 = (bf16[512,256]{1,0:T(8,128)(2,1)S(1)}, bf16[512,256]{1,0:T(8,128)(2,1)S(1)}, u32[]{:S(2)}, u32[]{:S(2)}) collective-permute-start(bf16[512,256]{1,0:T(8,128)(2,1)S(1)} %slice.6), channel_id=1, source_target_pairs={{0,12},{4,8},{8,4},{12,0},{16,28},{20,24},{24,20},{28,16},{1,13},{... | collective-permute-start | bytes 786440 | tf_op jit(solution)/shard_map/ppermute | solution.py:243
  35.5 8.6 %collective-permute-start.5 = (bf16[512,256]{1,0:T(8,128)(2,1)S(1)}, bf16[512,256]{1,0:T(8,128)(2,1)S(1)}, u32[]{:S(2)}, u32[]{:S(2)}) collective-permute-start(bf16[512,256]{1,0:T(8,128)(2,1)S(1)} %collective-permute-done.3.refs_1_), channel_id=1, source_target_pairs={{0,4},{4,0},{8,12},{12,8},{16,20},{20,16},{24,28},{28,24},{1,5},{5... | collective-permute-start | bytes 786440 | tf_op jit(solution)/shard_map/ppermute | solution.py:243
  36.2 7.9 %collective-permute-start.4 = (bf16[512,256]{1,0:T(8,128)(2,1)S(1)}, bf16[512,256]{1,0:T(8,128)(2,1)S(1)}, u32[]{:S(2)}, u32[]{:S(2)}) collective-permute-start(bf16[512,256]{1,0:T(8,128)(2,1)S(1)} %collective-permute-done.2.refs_0_), channel_id=1, source_target_pairs={{0,4},{4,0},{8,12},{12,8},{16,20},{20,16},{24,28},{28,24},{1,5},{5... | collective-permute-start | bytes 786440 | tf_op jit(solution)/shard_map/ppermute | solution.py:243
  44.1 3.9 %copy-start.1 = (bf16[512,512]{1,0:T(8,128)(2,1)S(1)}, bf16[512,512]{1,0:T(8,128)(2,1)}, u32[]{:S(2)}) copy-start(bf16[512,512]{1,0:T(8,128)(2,1)} %w_ref.1) | copy-start | bytes 1572868
  44.1 3.9 %copy-start.5 = (s32[3,256]{1,0:T(4,128)S(1)}, s32[3,256]{1,0:T(4,128)}, u32[]{:S(2)}) copy-start(s32[3,256]{1,0:T(4,128)} %order_ref.1) | copy-start | bytes 9220

commit v2 on v1

--- a/solution.py
+++ b/solution.py
@@ -11,10 +11,13 @@
 RADIUS = 3
 MATCHINGS = 3
 LANES = 128
+ORDER_ROWS = 16
 LOG2E = 1.4426950408889634
 NEG_FILL = -1e30
 VMEM_BYTES = 40 * 1024 * 1024
 
+CHEAP = pl.CostEstimate(flops=1000, bytes_accessed=1000, transcendentals=0)
+LONG = pl.CostEstimate(flops=2 * 10**9, bytes_accessed=1000, transcendentals=0)
 F32 = jnp.float32
 BF16 = jnp.bfloat16
 
@@ -28,14 +31,15 @@
     return jnp.where(row_ids == order_row, 1.0, 0.0).astype(BF16)
 
 
-def prep_kernel(groups, k_hbm, v_hbm, order_hbm, tile_ref, out_ref, k_ref, v_ref, order_ref, sems):
+def prep_kernel(groups, k_hbm, v_hbm, order_hbm, tile_ref, *refs):
+    out_refs = refs[:groups]
+    k_ref, v_ref, order_ref, sems = refs[groups:]
     rows, width = k_ref.shape
     bucket = rows // groups
     half = width // 2
-    group = lax.axis_index("grp")
     copies = [
         pltpu.make_async_copy(src, dst, sems.at[i])
-        for i, (src, dst) in enumerate(((order_hbm, order_ref), (k_hbm, k_ref), (v_hbm, v_ref)))
+        for i, (src, dst) in enumerate(((order_hbm, order_ref), (v_hbm, v_ref), (k_hbm, k_ref)))
     ]
     for copy in copies:
         copy.start()
@@ -44,20 +48,46 @@
     keys = k_ref[...]
     vals = v_ref[...]
     order = order_ref[...]
+    tile_ref[:width, :] = vals.T
+    tile_ref[width : width + rows, :] = keys[:, :half]
+    tile_ref[width + rows :, :] = keys[:, half:]
+    for ref in out_refs:
+        if ref.shape[0] > MATCHINGS * bucket:
+            ref[:rows, :] = keys
+            below = slice(rows, rows + ORDER_ROWS)
+            padded = jnp.concatenate([order, jnp.zeros((ORDER_ROWS - MATCHINGS, rows), jnp.int32)], axis=0)
+            ref[below, :rows] = padded.astype(F32).astype(BF16)
+            ref[below, rows:] = jnp.zeros((ORDER_ROWS, width - rows), BF16)
     lane = lax.broadcasted_iota(jnp.int32, order.shape, 1)
     swapped = jnp.where(lane % 2 == 0, jnp.roll(order, -1, axis=1), jnp.roll(order, 1, axis=1))
     wanted = jnp.where(lane < bucket, swapped, order)
+    n_paired = sum(ref.shape[1] == 2 * width for ref in out_refs)
     for j in range(MATCHINGS):
         table = place_table(wanted[j : j + 1, :], rows)
-        ordered_k = dot(table, keys, ((0,), (0,))).astype(BF16)
+        ordered_k = dot(table[:, : n_paired * bucket], keys, ((0,), (0,))).astype(BF16)
         ordered_v = dot(table, vals, ((0,), (0,))).astype(BF16)
-        for b in range(groups):
-            mine = slice(j * bucket, (j + 1) * bucket)
-            out_ref[group ^ b, mine, :width] = ordered_k[b * bucket : (b + 1) * bucket]
-            out_ref[group ^ b, mine, width:] = ordered_v[b * bucket : (b + 1) * bucket]
-    tile_ref[:width, :] = vals.T
-    tile_ref[width : width + rows, :] = keys[:, :half]
-    tile_ref[width + rows :, :] = keys[:, half:]
+        for b, out_ref in enumerate(out_refs):
+            first = out_ref.shape[0] - MATCHINGS * bucket + j * bucket
+            mine = slice(first, first + bucket)
+            at = slice(b * bucket, (b + 1) * bucket)
+            if b < n_paired:
+                out_ref[mine, :width] = ordered_k[at]
+                out_ref[mine, width:] = ordered_v[at]
+            else:
+                out_ref[mine, :] = ordered_v[at]
+
+
+def relay_kernel(groups, message_ref, mine_ref, next_ref):
+    bucket = mine_ref.shape[0] // MATCHINGS
+    rows = bucket * groups
+    keys = message_ref[:rows, :]
+    order = message_ref[rows : rows + ORDER_ROWS, :rows].astype(F32).astype(jnp.int32)
+    for j in range(MATCHINGS):
+        table = place_table(order[j : j + 1, :], rows)[:, 2 * bucket :]
+        ordered = dot(table, keys, ((0,), (0,))).astype(BF16)
+        mine = slice(j * bucket, (j + 1) * bucket)
+        mine_ref[mine, :] = ordered[:bucket]
+        next_ref[mine, :] = ordered[bucket:]
 
 
 def blocks_kernel(loop_size, served, first, last, tiles_ref, q_ref, *refs):
@@ -153,8 +183,19 @@
         stat_out[HEADS:] = l_ref[...]
 
 
-def finish_kernel(groups, q_ref, order_ref, bias_ref, acc_ref, stat_ref, w_ref, come_ref, out_ref):
-    group = lax.axis_index("grp")
+def rows_in_order(refs, j, bucket, first, width):
+    parts = []
+    for ref in refs:
+        top = ref.shape[0] - (MATCHINGS - j) * bucket
+        left = first if ref.shape[1] == 2 * width else 0
+        parts.append(ref[top : top + bucket, left : left + width])
+    return jnp.concatenate(parts, axis=0)
+
+
+def weigh_kernel(groups, q_ref, order_ref, bias_ref, acc_ref, stat_ref, *refs):
+    key_refs = refs[:groups]
+    val_refs = refs[groups : 2 * groups - 1]
+    part_ref, edge_ref = refs[2 * groups - 1 :]
     rows, width = q_ref.shape
     head = width // HEADS
     bucket = rows // groups
@@ -176,19 +217,13 @@
     block_max = jnp.where(lane < HEADS, stat, 0.0)
     block_sum = jnp.where(lane < HEADS, jnp.roll(stat, -HEADS, axis=1), 1.0)
     edge_scores = []
-    edge_vals = []
     for j in range(MATCHINGS):
         table = place_table(order_ref[j : j + 1, :], rows)
-        mine = slice(j * bucket, (j + 1) * bucket)
-        come = [come_ref[group ^ b, mine, :] for b in range(1, groups)]
-        in_order = jnp.concatenate([come_ref[group, mine, :]] + come, axis=0)
-        partner = dot(table, in_order)
-        prod = queries * partner[:, :width]
+        prod = queries * dot(table, rows_in_order(key_refs, j, bucket, 0, width))
         high = prod.astype(BF16)
         low = (prod - high.astype(F32)).astype(BF16)
         edge = dot(high, gather) + dot(low, gather)
         edge_scores.append(edge + bias_ref[j : j + 1, :] * unscale)
-        edge_vals.append(partner[:, width:])
     top = block_max
     for edge in edge_scores:
         top = jnp.maximum(top, edge)
@@ -204,11 +239,26 @@
         low = (x - high.astype(F32)).astype(BF16)
         return dot(high, spread) + dot(low, spread)
 
-    numer = acc_ref[...] * wide(keep)
-    for u, vals in zip(edge_w, edge_vals):
-        numer = numer + dot(u.astype(BF16), spread) * vals
-    attended = (numer * wide(inv)).astype(BF16)
-    out_ref[...] = dot(attended, w_ref[...]).astype(BF16)
+    numer = acc_ref[...] * wide(keep * inv)
+    for j in range(MATCHINGS):
+        table = place_table(order_ref[j : j + 1, :], rows)[:, : rows - bucket]
+        edge = wide(edge_w[j].astype(BF16).astype(F32) * inv)
+        edge_ref[j] = edge
+        numer = numer + edge * dot(table, rows_in_order(val_refs, j, bucket, width, width))
+    part_ref[...] = numer
+
+
+def finish_kernel(groups, order_ref, part_ref, edge_ref, w_ref, val_ref, out_ref):
+    rows, width = part_ref.shape
+    bucket = rows // groups
+    numer = part_ref[...]
+    for j in range(MATCHINGS):
+        table = place_table(order_ref[j : j + 1, :], rows)[:, rows - bucket :]
+        numer = numer + edge_ref[j] * dot(table, rows_in_order([val_ref], j, bucket, width, width))
+    out_ref[...] = dot(numer.astype(BF16), w_ref[...]).astype(BF16)
+
+
+fence = lax.optimization_barrier
 
 
 def vmem_specs(n):
@@ -221,23 +271,27 @@
     bucket = rows // groups
     params = pltpu.CompilerParams(vmem_limit_bytes=VMEM_BYTES)
     tile_shape = jax.ShapeDtypeStruct((width + 2 * rows, width // 2), BF16)
-    bucket_shape = jax.ShapeDtypeStruct((groups, MATCHINGS * bucket, 2 * width), BF16)
-    own_tile, outgoing = pl.pallas_call(
+    relayed = loop_size == 8 and groups == 4
+    kv_shape = jax.ShapeDtypeStruct((MATCHINGS * bucket, 2 * width), BF16)
+    one_shape = jax.ShapeDtypeStruct((MATCHINGS * bucket, width), BF16)
+    message_shape = jax.ShapeDtypeStruct((rows + ORDER_ROWS + MATCHINGS * bucket, width), BF16)
+    bucket_shapes = [kv_shape, kv_shape, message_shape, one_shape] if relayed else [kv_shape] * groups
+    own_tile, *outgoing = pl.pallas_call(
         functools.partial(prep_kernel, groups),
-        out_shape=[tile_shape, bucket_shape],
+        out_shape=[tile_shape] + bucket_shapes,
         in_specs=[pl.BlockSpec(memory_space=pltpu.HBM)] * 3,
-        out_specs=vmem_specs(2),
+        out_specs=vmem_specs(1 + groups),
         scratch_shapes=[
             pltpu.VMEM((rows, width), BF16),
             pltpu.VMEM((rows, width), BF16),
             pltpu.VMEM(expander_order.shape, jnp.int32),
             pltpu.SemaphoreType.DMA((3,)),
         ],
-        compiler_params=params,
         name="prep",
     )(key_rows, value_rows, expander_order)
 
-    incoming = lax.all_to_all(outgoing, "grp", split_axis=0, concat_axis=0, tiled=True)
+    def over_grp(array, b):
+        return lax.ppermute(array, "grp", [(i, i ^ b) for i in range(groups)])
 
     def flipped(array, bits):
         return lax.ppermute(array, "loop", [(i, i ^ bits) for i in range(loop_size)])
@@ -266,22 +320,43 @@
                 pltpu.SemaphoreType.DMA((tile_list.shape[1], 2)),
             ],
             compiler_params=params,
-            name="corner_blocks" if state else "blocks",
+            cost_estimate=CHEAP,
+            name="blocks" + "_".join(map(str, served)),
         )(tile_list, queries, *arrays, *state)
 
-    if loop_size == 8:
+    if relayed:
+        message = over_grp(outgoing[2], 2)
+        near = over_grp(outgoing[1], 1)
         side = flipped(own_tile, 2)
         across = flipped(own_tile, 5)
-        twin = flipped(own_tile, 1)
-        side, across = lax.optimization_barrier((side, across))
+        state = attend({0: [own_tile]}, (), False)
+        side, across, tile, state = fence((side, across, own_tile, state))
+        twin = flipped(tile, 1)
         corner_k = flipped(side[width:], 4)
         corner_v = flipped(across[:width], 3)
+        state = attend({2: [side], 4: [across]}, state, False)
+        message, near, state = fence((message, near, state))
+        keys_2, passed = pl.pallas_call(
+            functools.partial(relay_kernel, groups),
+            out_shape=[one_shape] * 2,
+            in_specs=vmem_specs(1),
+            out_specs=vmem_specs(2),
+            compiler_params=params,
+            cost_estimate=LONG,
+            name="relay",
+        )(message)
+        corner_k, corner_v, twin, side, keys_2, passed, far_vals, state = fence(
+            (corner_k, corner_v, twin, side, keys_2, passed, outgoing[3], state)
+        )
         side_twin = flipped(side, 1)
         corner_twin_k = flipped(corner_k, 1)
         corner_twin_v = flipped(corner_v, 1)
-        state = attend({0: [own_tile], 1: [twin], 2: [side], 3: [side_twin], 4: [across]}, (), False)
-        corners = {5: [corner_v, corner_k], 6: [corner_twin_v, corner_twin_k]}
-        acc, stat = attend(corners, state, True)
+        keys_3 = over_grp(passed, 1)
+        vals_3 = over_grp(far_vals, 3)
+        late = {1: [twin], 3: [side_twin], 5: [corner_v, corner_k], 6: [corner_twin_v, corner_twin_k]}
+        acc, stat = attend(late, state, True)
+        key_parts = [outgoing[0], near, keys_2, keys_3]
+        val_parts = [outgoing[0], near, message, vals_3]
     else:
         tiles = {}
         for offset in range(-RADIUS, RADIUS + 1):
@@ -289,16 +364,30 @@
             tile = lax.ppermute(own_tile, "loop", pairs) if offset else own_tile
             tiles[offset + RADIUS] = [tile]
         acc, stat = attend(tiles, (), True)
+        key_parts = val_parts = [outgoing[0]] + [over_grp(outgoing[b], b) for b in range(1, groups)]
 
     bias = jnp.pad(expander_bias, ((0, 0), (0, LANES - HEADS)))
+    part, edge = pl.pallas_call(
+        functools.partial(weigh_kernel, groups),
+        out_shape=[
+            jax.ShapeDtypeStruct((rows, width), F32),
+            jax.ShapeDtypeStruct((MATCHINGS, rows, width), F32),
+        ],
+        in_specs=vmem_specs(4 + 2 * groups),
+        out_specs=vmem_specs(2),
+        compiler_params=params,
+        cost_estimate=CHEAP,
+        name="weigh",
+    )(queries, expander_order, bias, acc, stat, *key_parts, *val_parts[:-1])
     return pl.pallas_call(
         functools.partial(finish_kernel, groups),
         out_shape=jax.ShapeDtypeStruct((rows, width), BF16),
-        in_specs=vmem_specs(7),
+        in_specs=vmem_specs(5),
         out_specs=pl.BlockSpec(memory_space=pltpu.VMEM),
         compiler_params=params,
+        cost_estimate=CHEAP,
         name="finish",
-    )(queries, expander_order, bias, acc, stat, out_weight, incoming)
+    )(expander_order, part, edge, out_weight, val_parts[-1])
 
 
 def solution(mesh):

time: 50.9 us -> 47.5 us (0.933)
  waiting for transfers between devices: 20.9 us -> 12.2 us
  Pallas kernels: 15.6 us -> 19.4 us
  starting transfers between devices: 11.3 us -> 13.9 us
  local copies, waits for them, and re-layouts: 2.66 us -> 1.68 us
    ppermute x8, waiting for transfers between devices: 20.4 us -> 3.94 us  [flipped(): lax.ppermute(array, 'loop', [(i, i ^ bits) for i in range(loop_size)])]
    ppermute x0 -> x4, waiting for transfers between devices: none -> 8.3 us  [over_grp(): return lax.ppermute(array, 'grp', [(i, i ^ b) for i in range(groups)])]
    ppermute x0 -> x4, starting transfers between devices: none -> 7.67 us  [over_grp(): return lax.ppermute(array, 'grp', [(i, i ^ b) for i in range(groups)])]
    all_to_all x1 -> x0, starting transfers between devices: 6.46 us -> none  [shards(): lax.all_to_all(outgoing, 'grp', split_axis=0, concat_axis=0, tiled=True)]
    pallas_call x0 -> x2, Pallas kernels: none -> 2.31 us  [the longest x1 2.01 us: shards(): pl.pallas_call(functools.partial(weigh_kernel, groups), out_shape=[jax.Sh...]
    pallas_call x2 -> x3, Pallas kernels: 11.1 us -> 12.8 us  [attend(): pl.pallas_call(functools.partial(blocks_kernel, loop_size, slots, not sta...]
    ppermute x8, starting transfers between devices: 4.81 us -> 6.21 us  [flipped(): lax.ppermute(array, 'loop', [(i, i ^ bits) for i in range(loop_size)])]
    pallas_call x1, Pallas kernels: 2.59 us -> 1.39 us  [shards(): pl.pallas_call(functools.partial(finish_kernel, groups), out_shape=jax.Sh...]
  transfers between devices with their start and end apart: 9 -> 12, of which waited for: 5 -> 5; matrix products, arithmetic and copies ran while one was open for 0% -> 0% of each run, Pallas kernels for 22% -> 32%
where the time goes in v2:
time: 47.5 us; the launch traced here: 47.3 us
  Pallas kernels  19.4 us (41%)
  starting transfers between devices  13.9 us (29%)
  waiting for transfers between devices  12.2 us (26%)
  local copies, waits for them, and re-layouts  1.68 us (4%)
    pallas_call x3, Pallas kernels, attend(): pl.pallas_call(functools.partial(blocks_kernel, loop_size, slots, not sta...  12.8 us
    ppermute x4, waiting for transfers between devices, over_grp(): return lax.ppermute(array, 'grp', [(i, i ^ b) for i in range(groups)])  8.3 us
    ppermute x4, starting transfers between devices, over_grp(): return lax.ppermute(array, 'grp', [(i, i ^ b) for i in range(groups)])  7.67 us
    ppermute x8, starting transfers between devices, flipped(): lax.ppermute(array, 'loop', [(i, i ^ bits) for i in range(loop_size)])  6.21 us
    ppermute x8, waiting for transfers between devices, flipped(): lax.ppermute(array, 'loop', [(i, i ^ bits) for i in range(loop_size)])  3.94 us
    pallas_call x1, Pallas kernels, shards(): pl.pallas_call(functools.partial(prep_kernel, groups), out_shape=[tile_sh...  2.9 us
    pallas_call x1, Pallas kernels, shards(): pl.pallas_call(functools.partial(weigh_kernel, groups), out_shape=[jax.Sh...  2.01 us
    unnamed x18, local copies, waits for them, and re-layouts  1.64 us
  transfers between devices with their start and end apart: 12, of which 5 were waited for; matrix products, arithmetic and copies ran while one was open for 0% of the time, Pallas kernels for 32%

profile of v2, /device:TPU:0, one launch (start us, length us, event | category | flops | bytes accessed | tf_op | source)
XLA Modules:
  0.0 47.3 jit_solution(5962409924620707627)
XLA Ops:
  0.0 0.0 copy-start.1
  0.0 2.9 %prep.1 = (bf16[1024,256]{1,0:T(8,128)(2,1)}, bf16[192,1024]{1,0:T(8,128)(2,1)}, bf16[192,1024]{1,0:T(8,128)(2,1)}, bf16[464,512]{1,0:T(8,128)(2,1)}, bf16[192,512]{1,0:T(8,128)(2,1)}) custom-call(bf16[256,512]{1,0:T(8,128)(2,1)} %k_hbm.1, bf16[256,512]{1,0:T(8,128)(2,1)} %v_hbm.1, s32[3,256]{1,0:T(4,128)} %order_ref.3), custom_call_target="tpu_custom_call" | custom-call | tf_op jit(solution)/shard_map/prep/pallas_call | solution.py:279
  2.9 3.0 %collective-permute-start = (bf16[1024,256]{1,0:T(8,128)(2,1)}, bf16[1024,256]{1,0:T(8,128)(2,1)S(1)}, u32[]{:S(2)}, u32[]{:S(2)}) collective-permute-start(bf16[1024,256]{1,0:T(8,128)(2,1)} %get-tuple-element.43.refs_0_), channel_id=1, source_target_pairs={{0,8},{4,12},{8,0},{12,4},{16,24},{20,28},{24,16},{28,20},{1,9},{5... | collective-permute-start | bytes 1572872 | tf_op jit(solution)/shard_map/ppermute | solution.py:297
  5.9 0.7 %collective-permute-start.1 = (bf16[1024,256]{1,0:T(8,128)(2,1)}, bf16[1024,256]{1,0:T(8,128)(2,1)S(1)}, u32[]{:S(2)}, u32[]{:S(2)}) collective-permute-start(bf16[1024,256]{1,0:T(8,128)(2,1)} %get-tuple-element.43.refs_0_), channel_id=1, source_target_pairs={{0,20},{4,16},{8,28},{12,24},{16,4},{20,0},{24,12},{28,8},{1,21},{... | collective-permute-start | bytes 1572872 | tf_op jit(solution)/shard_map/ppermute | solution.py:297
  6.6 2.6 %collective-permute-start.5 = (bf16[464,512]{1,0:T(8,128)(2,1)}, bf16[464,512]{1,0:T(8,128)(2,1)S(1)}, u32[]{:S(2)}, u32[]{:S(2)}) collective-permute-start(bf16[464,512]{1,0:T(8,128)(2,1)} %get-tuple-element.44), channel_id=1, source_target_pairs={{0,2},{1,3},{2,0},{3,1},{4,6},{5,7},{6,4},{7,5},{8,10},{9,11},{10,... | collective-permute-start | bytes 1425416 | tf_op jit(solution)/shard_map/ppermute | solution.py:294
  9.2 1.6 %collective-permute-start.6 = (bf16[192,1024]{1,0:T(8,128)(2,1)}, bf16[192,1024]{1,0:T(8,128)(2,1)S(1)}, u32[]{:S(2)}, u32[]{:S(2)}) collective-permute-start(bf16[192,1024]{1,0:T(8,128)(2,1)} %get-tuple-element.45), channel_id=1, source_target_pairs={{0,1},{1,0},{2,3},{3,2},{4,5},{5,4},{6,7},{7,6},{8,9},{9,8},{10,11... | collective-permute-start | bytes 1179656 | tf_op jit(solution)/shard_map/ppermute | solution.py:294
  10.8 0.0 copy-start
  10.8 0.9 %copy-done = bf16[256,512]{1,0:T(8,128)(2,1)S(1)} copy-done((bf16[256,512]{1,0:T(8,128)(2,1)S(1)}, bf16[256,512]{1,0:T(8,128)(2,1)}, u32[]{:S(2)}) %copy-start) | copy-done | bytes 262168
  11.7 0.0 copy-start.5
  11.7 0.7 %copy-done.5 = s32[1,4]{1,0:T(1,128)S(1)} copy-done((s32[1,4]{1,0:T(1,128)S(1)}, s32[1,4]{1,0:T(1,128)}, u32[]{:S(2)}) %copy-start.5) | copy-done | bytes 40
  12.4 4.0 %blocks0.1 = (f32[512,256]{1,0:T(8,128)S(1)}, f32[16,256]{1,0:T(8,128)S(1)}) custom-call(s32[1,4]{1,0:T(1,128)S(1)} %copy-done.5, bf16[256,512]{1,0:T(8,128)(2,1)S(1)} %copy-done, bf16[1024,256]{1,0:T(8,128)(2,1)} %get-tuple-element.43.refs_0_), custom_call_target="tpu_custom_call" | custom-call | flops 1000 | bytes 1000 | tf_op jit(solution)/shard_map/blocks0/pallas_call | solution.py:306
  16.3 1.7 %collective-permute-done.refs_0_ = bf16[1024,256]{1,0:T(8,128)(2,1)S(1)} collective-permute-done((bf16[1024,256]{1,0:T(8,128)(2,1)}, bf16[1024,256]{1,0:T(8,128)(2,1)S(1)}, u32[]{:S(2)}, u32[]{:S(2)}) %collective-permute-start) | collective-permute-done | bytes 524320 | tf_op jit(solution)/shard_map/ppermute | solution.py:297
  18.1 2.2 %collective-permute-done.1.refs_1_ = bf16[1024,256]{1,0:T(8,128)(2,1)S(1)} collective-permute-done((bf16[1024,256]{1,0:T(8,128)(2,1)}, bf16[1024,256]{1,0:T(8,128)(2,1)S(1)}, u32[]{:S(2)}, u32[]{:S(2)}) %collective-permute-start.1) | collective-permute-done | bytes 524320 | tf_op jit(solution)/shard_map/ppermute | solution.py:297
  20.3 0.2 collective-permute-start.4
  20.5 1.2 %collective-permute-start.2 = (bf16[512,256]{1,0:T(8,128)(2,1)S(1)}, bf16[512,256]{1,0:T(8,128)(2,1)S(1)}, u32[]{:S(2)}, u32[]{:S(2)}) collective-permute-start(bf16[512,256]{1,0:T(8,128)(2,1)S(1)} %slice.6), channel_id=1, source_target_pairs={{0,16},{4,20},{8,24},{12,28},{16,0},{20,4},{24,8},{28,12},{1,17},{... | collective-permute-start | bytes 786440 | tf_op jit(solution)/shard_map/ppermute | solution.py:297
  21.7 0.4 collective-permute-start.3
  22.1 0.0 copy-done.1
  22.2 3.2 %blocks2_4.1 = (f32[512,256]{1,0:T(8,128)S(1)}, f32[16,256]{1,0:T(8,128)S(1)}) custom-call(s32[1,4]{1,0:T(1,128)S(1)} %copy-done.5, bf16[256,512]{1,0:T(8,128)(2,1)S(1)} %copy-done.1, bf16[1024,256]{1,0:T(8,128)(2,1)S(1)} %collective-permute-done.refs_0_, bf16[1024,256]{1,0:T(8,128)(2,1)S(1)} %collective-permute-done.1.refs_1_, ...), custom_call_target="tpu_custom_call" | custom-call | flops 1000 | bytes 1000 | tf_op jit(solution)/shard_map/blocks2_4/pallas_call | solution.py:306
  25.3 3.9 %collective-permute-done.6.refs_1_.refs_5_ = bf16[192,1024]{1,0:T(8,128)(2,1)S(1)} collective-permute-done((bf16[192,1024]{1,0:T(8,128)(2,1)}, bf16[192,1024]{1,0:T(8,128)(2,1)S(1)}, u32[]{:S(2)}, u32[]{:S(2)}) %collective-permute-start.6) | collective-permute-done | bytes 393248 | tf_op jit(solution)/shard_map/ppermute | solution.py:294
  29.2 2.4 %collective-permute-done.5.message_ref.refs_6_ = bf16[464,512]{1,0:T(8,128)(2,1)S(1)} collective-permute-done((bf16[464,512]{1,0:T(8,128)(2,1)}, bf16[464,512]{1,0:T(8,128)(2,1)S(1)}, u32[]{:S(2)}, u32[]{:S(2)}) %collective-permute-start.5) | collective-permute-done | bytes 475168 | tf_op jit(solution)/shard_map/ppermute | solution.py:294
  31.6 0.0 copy-start.8
  31.6 0.0 copy-start.7
  31.6 0.0 copy-start.6
  31.6 0.3 relay.1
  31.9 0.0 copy-start.2
  31.9 0.0 copy-start.4
  31.9 0.0 collective-permute-done.2.refs_3_
  32.0 0.0 collective-permute-done.3.refs_2_
  32.0 0.0 collective-permute-done.4.refs_0_
  32.0 0.2 collective-permute-start.7
  32.1 0.4 collective-permute-start.8
  32.6 0.1 collective-permute-start.9
  32.7 0.8 %collective-permute-start.10 = (bf16[192,512]{1,0:T(8,128)(2,1)S(1)}, bf16[192,512]{1,0:T(8,128)(2,1)S(1)}, u32[]{:S(2)}, u32[]{:S(2)}) collective-permute-start(bf16[192,512]{1,0:T(8,128)(2,1)S(1)} %get-tuple-element.67), channel_id=1, source_target_pairs={{0,1},{1,0},{2,3},{3,2},{4,5},{5,4},{6,7},{7,6},{8,9},{9,8},{10,11... | collective-permute-start | bytes 589832 | tf_op jit(solution)/shard_map/ppermute | solution.py:294
  33.5 0.0 copy-done.8
  33.5 2.7 %collective-permute-start.11 = (bf16[192,512]{1,0:T(8,128)(2,1)S(1)}, bf16[192,512]{1,0:T(8,128)(2,1)S(1)}, u32[]{:S(2)}, u32[]{:S(2)}) collective-permute-start(bf16[192,512]{1,0:T(8,128)(2,1)S(1)} %copy-done.8), channel_id=1, source_target_pairs={{0,3},{1,2},{2,1},{3,0},{4,7},{5,6},{6,5},{7,4},{8,11},{9,10},{10,... | collective-permute-start | bytes 589832 | tf_op jit(solution)/shard_map/ppermute | solution.py:294
  36.2 0.0 copy-done.7
  36.2 0.0 collective-permute-done.8.refs_4_
  36.2 0.0 collective-permute-done.9.refs_5_
  36.2 0.0 collective-permute-done.7.refs_1_
  36.2 0.0 copy-done.6
  36.2 5.7 %blocks1_3_5_6.1 = (f32[256,512]{1,0:T(8,128)S(1)}, f32[256,128]{1,0:T(8,128)S(1)}) custom-call(s32[1,4]{1,0:T(1,128)S(1)} %copy-done.6, bf16[256,512]{1,0:T(8,128)(2,1)S(1)} %copy-done.1, bf16[1024,256]{1,0:T(8,128)(2,1)S(1)} %collective-permute-done.4.refs_0_, bf16[1024,256]{1,0:T(8,128)(2,1)S(1)} %collective-permute-done.7.refs_1_, ...), custom_call_target="tpu_custom_call" | custom-call | flops 1000 | bytes 1000 | tf_op jit(solution)/shard_map/blocks1_3_5_6/pallas_call | solution.py:306
  41.9 0.0 collective-permute-done.10.refs_3_
  41.9 0.0 copy-done.2
  41.9 0.0 copy-done.4
  41.9 0.0 copy-start.3
  41.9 2.0 %weigh.1 = (f32[256,512]{1,0:T(8,128)S(1)}, f32[3,256,512]{2,1,0:T(8,128)S(1)}) custom-call(bf16[256,512]{1,0:T(8,128)(2,1)S(1)} %copy-done.1, s32[3,256]{1,0:T(4,128)S(1)} %copy-done.4, f32[3,128]{1,0:T(4,128)S(1)} %pad.4.bias_ref, f32[256,512]{1,0:T(8,128)S(1)} %get-tuple-element.62.acc_ref, f32[256,128]{1,0:T(8,128)S(1)} %get-tuple-element.63.stat_ref, ...), custom_call_target="tpu_custom_call" | custom-call | flops 1000 | bytes 1000 | tf_op jit(solution)/shard_map/weigh/pallas_call | solution.py:370
  43.9 2.0 %collective-permute-done.11.val_ref = bf16[192,512]{1,0:T(8,128)(2,1)S(1)} collective-permute-done((bf16[192,512]{1,0:T(8,128)(2,1)S(1)}, bf16[192,512]{1,0:T(8,128)(2,1)S(1)}, u32[]{:S(2)}, u32[]{:S(2)}) %collective-permute-start.11) | collective-permute-done | bytes 196640 | tf_op jit(solution)/shard_map/ppermute | solution.py:294
  45.9 0.0 copy-done.3
  45.9 1.4 %finish.1 = bf16[256,512]{1,0:T(8,128)(2,1)} custom-call(s32[3,256]{1,0:T(4,128)S(1)} %copy-done.4, f32[256,512]{1,0:T(8,128)S(1)} %get-tuple-element.68.part_ref, f32[3,256,512]{2,1,0:T(8,128)S(1)} %get-tuple-element.69.edge_ref, bf16[512,512]{1,0:T(8,128)(2,1)S(1)} %copy-done.3, bf16[192,512]{1,0:T(8,128)(2,1)S(1)} %collective-permute-done.11.val_ref), custom_call_target="tpu_custom_call" | custom-call | flops 1000 | bytes 1000 | tf_op jit(solution)/shard_map/finish/pallas_call | solution.py:382
  (3 shorter events, 0.0 us)
Async XLA Ops:
  0.0 22.2 %copy-start.1 = (bf16[256,512]{1,0:T(8,128)(2,1)S(1)}, bf16[256,512]{1,0:T(8,128)(2,1)}, u32[]{:S(2)}) copy-start(bf16[256,512]{1,0:T(8,128)(2,1)} %q_ref.7) | copy-start | bytes 786436
  2.9 15.1 %collective-permute-start = (bf16[1024,256]{1,0:T(8,128)(2,1)}, bf16[1024,256]{1,0:T(8,128)(2,1)S(1)}, u32[]{:S(2)}, u32[]{:S(2)}) collective-permute-start(bf16[1024,256]{1,0:T(8,128)(2,1)} %get-tuple-element.43.refs_0_), channel_id=1, source_target_pairs={{0,8},{4,12},{8,0},{12,4},{16,24},{20,28},{24,16},{28,20},{1,9},{5... | collective-permute-start | bytes 1572872 | tf_op jit(solution)/shard_map/ppermute | solution.py:297
  5.9 14.3 %collective-permute-start.1 = (bf16[1024,256]{1,0:T(8,128)(2,1)}, bf16[1024,256]{1,0:T(8,128)(2,1)S(1)}, u32[]{:S(2)}, u32[]{:S(2)}) collective-permute-start(bf16[1024,256]{1,0:T(8,128)(2,1)} %get-tuple-element.43.refs_0_), channel_id=1, source_target_pairs={{0,20},{4,16},{8,28},{12,24},{16,4},{20,0},{24,12},{28,8},{1,21},{... | collective-permute-start | bytes 1572872 | tf_op jit(solution)/shard_map/ppermute | solution.py:297
  6.6 25.0 %collective-permute-start.5 = (bf16[464,512]{1,0:T(8,128)(2,1)}, bf16[464,512]{1,0:T(8,128)(2,1)S(1)}, u32[]{:S(2)}, u32[]{:S(2)}) collective-permute-start(bf16[464,512]{1,0:T(8,128)(2,1)} %get-tuple-element.44), channel_id=1, source_target_pairs={{0,2},{1,3},{2,0},{3,1},{4,6},{5,7},{6,4},{7,5},{8,10},{9,11},{10,... | collective-permute-start | bytes 1425416 | tf_op jit(solution)/shard_map/ppermute | solution.py:294
  9.2 20.0 %collective-permute-start.6 = (bf16[192,1024]{1,0:T(8,128)(2,1)}, bf16[192,1024]{1,0:T(8,128)(2,1)S(1)}, u32[]{:S(2)}, u32[]{:S(2)}) collective-permute-start(bf16[192,1024]{1,0:T(8,128)(2,1)} %get-tuple-element.45), channel_id=1, source_target_pairs={{0,1},{1,0},{2,3},{3,2},{4,5},{5,4},{6,7},{7,6},{8,9},{9,8},{10,11... | collective-permute-start | bytes 1179656 | tf_op jit(solution)/shard_map/ppermute | solution.py:294
  10.8 0.9 %copy-start = (bf16[256,512]{1,0:T(8,128)(2,1)S(1)}, bf16[256,512]{1,0:T(8,128)(2,1)}, u32[]{:S(2)}) copy-start(bf16[256,512]{1,0:T(8,128)(2,1)} %q_ref.7) | copy-start | bytes 786436
  11.7 0.7 %copy-start.5 = (s32[1,4]{1,0:T(1,128)S(1)}, s32[1,4]{1,0:T(1,128)}, u32[]{:S(2)}) copy-start(s32[1,4]{1,0:T(1,128)} %tiles_ref.5) | copy-start | bytes 52
  20.3 11.7 %collective-permute-start.4 = (bf16[1024,256]{1,0:T(8,128)(2,1)}, bf16[1024,256]{1,0:T(8,128)(2,1)S(1)}, u32[]{:S(2)}, u32[]{:S(2)}) collective-permute-start(bf16[1024,256]{1,0:T(8,128)(2,1)} %get-tuple-element.43.refs_0_), channel_id=1, source_target_pairs={{0,4},{4,0},{8,12},{12,8},{16,20},{20,16},{24,28},{28,24},{1,5},{5... | collective-permute-start | bytes 1572872 | tf_op jit(solution)/shard_map/ppermute | solution.py:297
  20.5 11.5 %collective-permute-start.2 = (bf16[512,256]{1,0:T(8,128)(2,1)S(1)}, bf16[512,256]{1,0:T(8,128)(2,1)S(1)}, u32[]{:S(2)}, u32[]{:S(2)}) collective-permute-start(bf16[512,256]{1,0:T(8,128)(2,1)S(1)} %slice.6), channel_id=1, source_target_pairs={{0,16},{4,20},{8,24},{12,28},{16,0},{20,4},{24,8},{28,12},{1,17},{... | collective-permute-start | bytes 786440 | tf_op jit(solution)/shard_map/ppermute | solution.py:297
  21.7 10.2 %collective-permute-start.3 = (bf16[512,256]{1,0:T(8,128)(2,1)S(1)}, bf16[512,256]{1,0:T(8,128)(2,1)S(1)}, u32[]{:S(2)}, u32[]{:S(2)}) collective-permute-start(bf16[512,256]{1,0:T(8,128)(2,1)S(1)} %slice.7), channel_id=1, source_target_pairs={{0,12},{4,8},{8,4},{12,0},{16,28},{20,24},{24,20},{28,16},{1,13},{... | collective-permute-start | bytes 786440 | tf_op jit(solution)/shard_map/ppermute | solution.py:297
  31.6 1.9 %copy-start.8 = (bf16[192,512]{1,0:T(8,128)(2,1)S(1)}, bf16[192,512]{1,0:T(8,128)(2,1)}, u32[]{:S(2)}) copy-start(bf16[192,512]{1,0:T(8,128)(2,1)} %get-tuple-element.70) | copy-start | bytes 589828
  31.6 4.5 %copy-start.7 = (f32[3,8]{1,0:T(4,128)S(1)}, f32[3,8]{1,0:T(4,128)}, u32[]{:S(2)}) copy-start(f32[3,8]{1,0:T(4,128)} %param.13) | copy-start | bytes 292
  31.6 4.6 %copy-start.6 = (s32[1,4]{1,0:T(1,128)S(1)}, s32[1,4]{1,0:T(1,128)}, u32[]{:S(2)}) copy-start(s32[1,4]{1,0:T(1,128)} %tiles_ref.5) | copy-start | bytes 52
  31.9 10.0 %copy-start.2 = (bf16[192,1024]{1,0:T(8,128)(2,1)S(1)}, bf16[192,1024]{1,0:T(8,128)(2,1)}, u32[]{:S(2)}) copy-start(bf16[192,1024]{1,0:T(8,128)(2,1)} %get-tuple-element.64.refs_0_.refs_4_) | copy-start | bytes 1179652
  31.9 10.0 %copy-start.4 = (s32[3,256]{1,0:T(4,128)S(1)}, s32[3,256]{1,0:T(4,128)}, u32[]{:S(2)}) copy-start(s32[3,256]{1,0:T(4,128)} %order_ref.3) | copy-start | bytes 9220
  32.0 4.2 %collective-permute-start.7 = (bf16[1024,256]{1,0:T(8,128)(2,1)S(1)}, bf16[1024,256]{1,0:T(8,128)(2,1)S(1)}, u32[]{:S(2)}, u32[]{:S(2)}) collective-permute-start(bf16[1024,256]{1,0:T(8,128)(2,1)S(1)} %collective-permute-done.refs_0_), channel_id=1, source_target_pairs={{0,4},{4,0},{8,12},{12,8},{16,20},{20,16},{24,28},{28,24},{1,5},{5... | collective-permute-start | bytes 1572872 | tf_op jit(solution)/shard_map/ppermute | solution.py:297
  32.1 4.0 %collective-permute-start.8 = (bf16[512,256]{1,0:T(8,128)(2,1)S(1)}, bf16[512,256]{1,0:T(8,128)(2,1)S(1)}, u32[]{:S(2)}, u32[]{:S(2)}) collective-permute-start(bf16[512,256]{1,0:T(8,128)(2,1)S(1)} %collective-permute-done.3.refs_2_), channel_id=1, source_target_pairs={{0,4},{4,0},{8,12},{12,8},{16,20},{20,16},{24,28},{28,24},{1,5},{5... | collective-permute-start | bytes 786440 | tf_op jit(solution)/shard_map/ppermute | solution.py:297
  32.6 3.6 %collective-permute-start.9 = (bf16[512,256]{1,0:T(8,128)(2,1)S(1)}, bf16[512,256]{1,0:T(8,128)(2,1)S(1)}, u32[]{:S(2)}, u32[]{:S(2)}) collective-permute-start(bf16[512,256]{1,0:T(8,128)(2,1)S(1)} %collective-permute-done.2.refs_3_), channel_id=1, source_target_pairs={{0,4},{4,0},{8,12},{12,8},{16,20},{20,16},{24,28},{28,24},{1,5},{5... | collective-permute-start | bytes 786440 | tf_op jit(solution)/shard_map/ppermute | solution.py:297
  32.7 9.2 %collective-permute-start.10 = (bf16[192,512]{1,0:T(8,128)(2,1)S(1)}, bf16[192,512]{1,0:T(8,128)(2,1)S(1)}, u32[]{:S(2)}, u32[]{:S(2)}) collective-permute-start(bf16[192,512]{1,0:T(8,128)(2,1)S(1)} %get-tuple-element.67), channel_id=1, source_target_pairs={{0,1},{1,0},{2,3},{3,2},{4,5},{5,4},{6,7},{7,6},{8,9},{9,8},{10,11... | collective-permute-start | bytes 589832 | tf_op jit(solution)/shard_map/ppermute | solution.py:294
  33.5 12.5 %collective-permute-start.11 = (bf16[192,512]{1,0:T(8,128)(2,1)S(1)}, bf16[192,512]{1,0:T(8,128)(2,1)S(1)}, u32[]{:S(2)}, u32[]{:S(2)}) collective-permute-start(bf16[192,512]{1,0:T(8,128)(2,1)S(1)} %copy-done.8), channel_id=1, source_target_pairs={{0,3},{1,2},{2,1},{3,0},{4,7},{5,6},{6,5},{7,4},{8,11},{9,10},{10,... | collective-permute-start | bytes 589832 | tf_op jit(solution)/shard_map/ppermute | solution.py:294
  41.9 4.0 %copy-start.3 = (bf16[512,512]{1,0:T(8,128)(2,1)S(1)}, bf16[512,512]{1,0:T(8,128)(2,1)}, u32[]{:S(2)}) copy-start(bf16[512,512]{1,0:T(8,128)(2,1)} %w_ref.1) | copy-start | bytes 1572868

commit v3 on v2

v3 whole, which is shorter than its diff:
```python
import functools

import jax
import jax.numpy as jnp
from jax import lax
from jax.experimental import pallas as pl
from jax.experimental.pallas import tpu as pltpu
from jax.sharding import PartitionSpec as P

HEADS = 8
RADIUS = 3
MATCHINGS = 3
LANES = 128
ORDER_ROWS = 16
LOG2E = 1.4426950408889634
NEG_FILL = -1e30
VMEM_BYTES = 40 * 1024 * 1024

CHEAP = pl.CostEstimate(flops=1000, bytes_accessed=1000, transcendentals=0)
F32 = jnp.float32
BF16 = jnp.bfloat16


def dot(a, b, contract=((1,), (0,))):
    return lax.dot_general(a, b, (contract, ((), ())), preferred_element_type=F32)


def place_table(order_row, rows):
    row_ids = lax.broadcasted_iota(jnp.int32, (rows, rows), 0)
    return jnp.where(row_ids == order_row, 1.0, 0.0).astype(BF16)


def prep_kernel(groups, k_hbm, v_hbm, order_hbm, tile_ref, *refs):
    out_refs = refs[:-4]
    k_ref, v_ref, order_ref, sems = refs[-4:]
    rows, width = k_ref.shape
    bucket = rows // groups
    half = width // 2
    copies = [
        pltpu.make_async_copy(src, dst, sems.at[i])
        for i, (src, dst) in enumerate(((order_hbm, order_ref), (v_hbm, v_ref), (k_hbm, k_ref)))
    ]
    for copy in copies:
        copy.start()
    for copy in copies:
        copy.wait()
    keys = k_ref[...]
    vals = v_ref[...]
    order = order_ref[...]
    tile_ref[:width, :] = vals.T
    tile_ref[width : width + rows, :] = keys[:, :half]
    tile_ref[width + rows :, :] = keys[:, half:]
    paired = [ref for ref in out_refs if ref.shape[1] == 2 * width]
    for ref in out_refs[len(paired) :]:
        ref[:rows, :] = keys
        padded = jnp.concatenate([order, jnp.zeros((ORDER_ROWS - MATCHINGS, rows), jnp.int32)], axis=0)
        ref[rows:, :rows] = padded.astype(F32).astype(BF16)
        ref[rows:, rows:] = jnp.zeros((ORDER_ROWS, width - rows), BF16)
    lane = lax.broadcasted_iota(jnp.int32, order.shape, 1)
    swapped = jnp.where(lane % 2 == 0, jnp.roll(order, -1, axis=1), jnp.roll(order, 1, axis=1))
    wanted = jnp.where(lane < bucket, swapped, order)
    for j in range(MATCHINGS):
        table = place_table(wanted[j : j + 1, :], rows)[:, : len(paired) * bucket]
        ordered_k = dot(table, keys, ((0,), (0,))).astype(BF16)
        ordered_v = dot(table, vals, ((0,), (0,))).astype(BF16)
        mine = slice(j * bucket, (j + 1) * bucket)
        for b, out_ref in enumerate(paired):
            at = slice(b * bucket, (b + 1) * bucket)
            out_ref[mine, :width] = ordered_k[at]
            out_ref[mine, width:] = ordered_v[at]


def relay_kernel(groups, order_ref, rows_ref, mine_ref, next_ref):
    bucket = mine_ref.shape[0] // MATCHINGS
    rows = bucket * groups
    full = rows_ref[:rows, :]
    order = order_ref[rows:, :rows].astype(F32).astype(jnp.int32)
    for j in range(MATCHINGS):
        table = place_table(order[j : j + 1, :], rows)[:, 2 * bucket :]
        ordered = dot(table, full, ((0,), (0,))).astype(BF16)
        mine = slice(j * bucket, (j + 1) * bucket)
        mine_ref[mine, :] = ordered[:bucket]
        next_ref[mine, :] = ordered[bucket:]


def blocks_kernel(loop_size, served, first, last, tiles_ref, *refs):
    n_bufs = 2 * RADIUS + 1
    refs = list(refs)
    bufs = {slot: refs.pop(0) for slot in served}
    if first:
        q_ref, pairs_ref = refs.pop(0), None
    else:
        pairs_ref, acc_in, stat_in = refs.pop(0), refs.pop(0), refs.pop(0)
    acc_out, stat_out = refs.pop(0), refs.pop(0)
    if pairs_ref is None:
        pairs_ref = refs.pop(0)
    if last:
        acc, stat, tile_vmem, sems = refs
    else:
        (acc, stat), (tile_vmem, sems) = (acc_out, stat_out), refs
    width, rows = acc.shape
    head = width // HEADS
    n_tiles = tiles_ref.shape[1]
    here = lax.axis_index("loop")

    def slot_of(t):
        offset = tiles_ref[0, t]
        slot = offset
        if loop_size == 8:
            away = here ^ lax.rem(here + offset - RADIUS + loop_size, loop_size)
            slot = jnp.where(away > 4, away - 1, away)
        return jnp.where(offset <= 2 * RADIUS, slot, n_bufs)

    def here_served(slot):
        return functools.reduce(jnp.logical_or, [slot == k for k in served])

    def fetch(slot, t):
        return pltpu.make_async_copy(bufs[slot], tile_vmem.at[t], sems.at[t])

    for t in range(n_tiles):
        slot = slot_of(t)
        for k in served:

            @pl.when(slot == k)
            def _():
                fetch(k, t).start()

    if first:
        q_t = q_ref[...].T
        zeros = jnp.zeros((head, rows), BF16)
        for p in range(HEADS // 2):
            even = q_t[2 * p * head : (2 * p + 1) * head]
            odd = q_t[(2 * p + 1) * head : (2 * p + 2) * head]
            pairs_ref[p, :head, :rows] = even
            pairs_ref[p, :head, rows:] = zeros
            pairs_ref[p, head:, :rows] = zeros
            pairs_ref[p, head:, rows:] = odd
        stat[:HEADS] = jnp.full((HEADS, rows), NEG_FILL, F32)
        stat[HEADS:] = jnp.zeros((HEADS, rows), F32)
        acc[...] = jnp.zeros(acc.shape, F32)
    else:
        acc[...] = acc_in[...]
        stat[...] = stat_in[...]
    scale = head ** (-0.5) * LOG2E

    def one_tile(t, carry):
        @pl.when(here_served(slot_of(t)))
        def _():
            fetch(next(iter(served)), t).wait()
            scores = []
            for p in range(HEADS // 2):
                base = width + (p // 2) * rows
                keys = tile_vmem[t, base : base + rows, (p % 2) * LANES : (p % 2 + 1) * LANES]
                scores.append(dot(keys, pairs_ref[p]))
            for p in range(HEADS // 2):
                old = jnp.concatenate([stat[2 * p : 2 * p + 1], stat[2 * p + 1 : 2 * p + 2]], axis=1)
                new = jnp.maximum(old, jnp.max(scores[p], axis=0, keepdims=True))
                alpha = jnp.exp2((old - new) * scale)
                w = jnp.exp2((scores[p] - new) * scale)
                total = jnp.sum(w, axis=0, keepdims=True)
                w = w.astype(BF16)
                for side in range(2):
                    h = 2 * p + side
                    half = slice(side * rows, (side + 1) * rows)
                    mine = slice(h * head, (h + 1) * head)
                    stat[h : h + 1] = new[:, half]
                    stat[HEADS + h : HEADS + h + 1] = stat[HEADS + h : HEADS + h + 1] * alpha[:, half] + total[:, half]
                    acc[mine, :] = acc[mine, :] * alpha[:, half] + dot(tile_vmem[t, mine, :], w[:, half])

        return carry

    lax.fori_loop(0, n_tiles, one_tile, 0)
    if last:
        acc_out[...] = acc[...].T
        pad = jnp.zeros((LANES - 2 * HEADS, rows), F32)
        stat_out[...] = jnp.concatenate([stat[...], pad], axis=0).T


def rows_in_order(refs, j, bucket, first, width):
    parts = []
    for ref in refs:
        top = ref.shape[0] - (MATCHINGS - j) * bucket
        left = first if ref.shape[1] == 2 * width else 0
        parts.append(ref[top : top + bucket, left : left + width])
    return jnp.concatenate(parts, axis=0)


def weigh_kernel(groups, q_ref, order_ref, bias_ref, acc_ref, stat_ref, *refs):
    key_refs = refs[:groups]
    val_refs = refs[groups : 2 * groups - 1]
    part_ref, edge_ref = refs[2 * groups - 1 :]
    rows, width = q_ref.shape
    head = width // HEADS
    bucket = rows // groups
    scale = head ** (-0.5) * LOG2E
    unscale = head**0.5
    gather = (
        lax.broadcasted_iota(jnp.int32, (width, LANES), 0) // head
        == lax.broadcasted_iota(jnp.int32, (width, LANES), 1)
    )
    gather = jnp.where(gather, 1.0, 0.0).astype(BF16)
    spread = (
        lax.broadcasted_iota(jnp.int32, (LANES, width), 1) // head
        == lax.broadcasted_iota(jnp.int32, (LANES, width), 0)
    )
    spread = jnp.where(spread, 1.0, 0.0).astype(BF16)
    queries = q_ref[...].astype(F32)
    stat = stat_ref[...]
    lane = lax.broadcasted_iota(jnp.int32, stat.shape, 1)
    block_max = jnp.where(lane < HEADS, stat, 0.0)
    block_sum = jnp.where(lane < HEADS, jnp.roll(stat, -HEADS, axis=1), 1.0)
    edge_scores = []
    for j in range(MATCHINGS):
        table = place_table(order_ref[j : j + 1, :], rows)
        prod = queries * dot(table, rows_in_order(key_refs, j, bucket, 0, width))
        high = prod.astype(BF16)
        low = (prod - high.astype(F32)).astype(BF16)
        edge = dot(high, gather) + dot(low, gather)
        edge_scores.append(edge + bias_ref[j : j + 1, :] * unscale)
    top = block_max
    for edge in edge_scores:
        top = jnp.maximum(top, edge)
    keep = jnp.exp2((block_max - top) * scale)
    edge_w = [jnp.exp2((edge - top) * scale) for edge in edge_scores]
    total = block_sum * keep
    for u in edge_w:
        total = total + u
    inv = 1.0 / total

    def wide(x):
        high = x.astype(BF16)
        low = (x - high.astype(F32)).astype(BF16)
        return dot(high, spread) + dot(low, spread)

    numer = acc_ref[...] * wide(keep * inv)
    for j in range(MATCHINGS):
        table = place_table(order_ref[j : j + 1, :], rows)[:, : rows - bucket]
        edge = wide(edge_w[j].astype(BF16).astype(F32) * inv)
        edge_ref[j] = edge
        numer = numer + edge * dot(table, rows_in_order(val_refs, j, bucket, width, width))
    part_ref[...] = numer


def finish_kernel(groups, order_ref, part_ref, edge_ref, w_ref, val_ref, out_ref):
    rows, width = part_ref.shape
    bucket = rows // groups
    numer = part_ref[...]
    for j in range(MATCHINGS):
        table = place_table(order_ref[j : j + 1, :], rows)[:, rows - bucket :]
        numer = numer + edge_ref[j] * dot(table, rows_in_order([val_ref], j, bucket, width, width))
    out_ref[...] = dot(numer.astype(BF16), w_ref[...]).astype(BF16)


fence = lax.optimization_barrier


def vmem_specs(n):
    return [pl.BlockSpec(memory_space=pltpu.VMEM)] * n


def shards(groups, loop_size, queries, key_rows, value_rows, out_weight, tile_list, expander_order, expander_bias):
    rows, width = queries.shape
    head = width // HEADS
    bucket = rows // groups
    params = pltpu.CompilerParams(vmem_limit_bytes=VMEM_BYTES)
    tile_shape = jax.ShapeDtypeStruct((width + 2 * rows, width // 2), BF16)
    relayed = loop_size == 8 and groups == 4
    kv_shape = jax.ShapeDtypeStruct((MATCHINGS * bucket, 2 * width), BF16)
    one_shape = jax.ShapeDtypeStruct((MATCHINGS * bucket, width), BF16)
    full_shape = jax.ShapeDtypeStruct((rows + ORDER_ROWS, width), BF16)
    bucket_shapes = [kv_shape, kv_shape, full_shape] if relayed else [kv_shape] * groups
    own_tile, *outgoing = pl.pallas_call(
        functools.partial(prep_kernel, groups),
        out_shape=[tile_shape] + bucket_shapes,
        in_specs=[pl.BlockSpec(memory_space=pltpu.HBM)] * 3,
        out_specs=vmem_specs(1 + len(bucket_shapes)),
        scratch_shapes=[
            pltpu.VMEM((rows, width), BF16),
            pltpu.VMEM((rows, width), BF16),
            pltpu.VMEM(expander_order.shape, jnp.int32),
            pltpu.SemaphoreType.DMA((3,)),
        ],
        name="prep",
    )(key_rows, value_rows, expander_order)

    def over_grp(array, b):
        return lax.ppermute(array, "grp", [(i, i ^ b) for i in range(groups)])

    def flipped(array, bits):
        return lax.ppermute(array, "loop", [(i, i ^ bits) for i in range(loop_size)])

    def attend(served, state, last):
        shapes = [(width, rows), (2 * HEADS, rows)]
        if last:
            shapes = [(rows, width), (rows, LANES)] + shapes
        out_shape = [jax.ShapeDtypeStruct(shape, F32) for shape in shapes[:2]]
        scratch = [pltpu.VMEM(shape, F32) for shape in shapes[2:]]
        pairs_shape = jax.ShapeDtypeStruct((HEADS // 2, 2 * head, 2 * rows), BF16)
        if state is None:
            out_shape.append(pairs_shape)
        others = [queries] if state is None else state
        aliases = {} if state is None or last else {len(served) + 2: 0, len(served) + 3: 1}
        acc, stat, *pairs = pl.pallas_call(
            functools.partial(blocks_kernel, loop_size, tuple(served), state is None, last),
            out_shape=out_shape,
            in_specs=[pl.BlockSpec(memory_space=pltpu.SMEM)]
            + [pl.BlockSpec(memory_space=pl.ANY)] * len(served)
            + vmem_specs(len(others)),
            out_specs=vmem_specs(len(out_shape)),
            scratch_shapes=scratch
            + [
                pltpu.VMEM((tile_list.shape[1],) + tile_shape.shape, BF16),
                pltpu.SemaphoreType.DMA((tile_list.shape[1],)),
            ],
            input_output_aliases=aliases,
            compiler_params=params,
            cost_estimate=CHEAP,
            name="blocks" + "_".join(map(str, served)),
        )(tile_list, *served.values(), *others)
        return [pairs[0] if state is None else state[0], acc, stat]

    if relayed:

        def relay(order, full, name):
            return pl.pallas_call(
                functools.partial(relay_kernel, groups),
                out_shape=[one_shape] * 2,
                in_specs=vmem_specs(2),
                out_specs=vmem_specs(2),
                compiler_params=params,
                cost_estimate=CHEAP,
                name=name,
            )(order, full)

        full_k = over_grp(outgoing[2], 2)
        near = over_grp(outgoing[1], 1)
        side = flipped(own_tile, 2)
        across = flipped(own_tile, 5)
        twin = flipped(own_tile, 1)
        state = attend({0: own_tile}, None, False)
        side, across, twin, own_vals, state = fence((side, across, twin, value_rows, state))
        corner = flipped(side, 4)
        corner_twin = flipped(across, 2)
        side_twin = flipped(side, 1)
        full_v = over_grp(own_vals, 2)
        keys_2, passed = relay(full_k, full_k, "relay_keys")
        keys_3 = over_grp(passed, 1)
        state = attend({1: twin, 2: side, 4: across}, state, False)
        full_v, near, keys_3, state = fence((full_v, near, keys_3, state))
        vals_2, passed = relay(full_k, full_v, "relay_vals")
        vals_3 = over_grp(passed, 1)
        key_parts = [outgoing[0], near, keys_2, keys_3]
        val_parts = [outgoing[0], near, vals_2, vals_3]
        late = {3: side_twin, 5: corner, 6: corner_twin}
        _, acc, stat = attend(late, state, True)
    else:
        tiles = {}
        for offset in range(-RADIUS, RADIUS + 1):
            pairs = [(i, (i - offset) % loop_size) for i in range(loop_size)]
            tile = lax.ppermute(own_tile, "loop", pairs) if offset else own_tile
            tiles[offset + RADIUS] = tile
        _, acc, stat = attend(tiles, None, True)
        key_parts = val_parts = [outgoing[0]] + [over_grp(outgoing[b], b) for b in range(1, groups)]

    bias = jnp.pad(expander_bias, ((0, 0), (0, LANES - HEADS)))
    part, edge = pl.pallas_call(
        functools.partial(weigh_kernel, groups),
        out_shape=[
            jax.ShapeDtypeStruct((rows, width), F32),
            jax.ShapeDtypeStruct((MATCHINGS, rows, width), F32),
        ],
        in_specs=vmem_specs(4 + 2 * groups),
        out_specs=vmem_specs(2),
        compiler_params=params,
        cost_estimate=CHEAP,
        name="weigh",
    )(queries, expander_order, bias, acc, stat, *key_parts, *val_parts[:-1])
    return pl.pallas_call(
        functools.partial(finish_kernel, groups),
        out_shape=jax.ShapeDtypeStruct((rows, width), BF16),
        in_specs=vmem_specs(5),
        out_specs=pl.BlockSpec(memory_space=pltpu.VMEM),
        compiler_params=params,
        cost_estimate=CHEAP,
        name="finish",
    )(expander_order, part, edge, out_weight, val_parts[-1])


def solution(mesh):
    placed = (
        P(("loop", "grp"), None),
        P(("loop", "grp"), None),
        P(("loop", "grp"), None),
        P(),
        P(("loop", "grp"), None),
        P(None, ("loop", "grp")),
        P(),
    )
    return jax.shard_map(
        functools.partial(shards, mesh.shape["grp"], mesh.shape["loop"]),
        mesh=mesh,
        in_specs=placed,
        out_specs=P(("loop", "grp"), None),
        check_vma=False,
    )
```

time: 47.5 us -> 46 us (0.968)
  Pallas kernels: 19.4 us -> 13.2 us
  waiting for transfers between devices: 12.2 us -> 15.2 us
  local copies, waits for them, and re-layouts: 1.68 us -> 2.67 us
  starting transfers between devices: 13.9 us -> 14.6 us
    pallas_call x4 -> x5, Pallas kernels: 13.1 us -> 7.2 us  [the longest x3 6.59 us: attend(): pl.pallas_call(functools.partial(blocks_kernel, loop_size, tuple(served),...]
    ppermute x4 -> x5, waiting for transfers between devices: 8.3 us -> 11.1 us  [over_grp(): return lax.ppermute(array, 'grp', [(i, i ^ b) for i in range(groups)])]
    unnamed x18 -> x16, local copies, waits for them, and re-layouts: 1.64 us -> 2.67 us
    ppermute x4 -> x5, starting transfers between devices: 7.67 us -> 8.09 us  [over_grp(): return lax.ppermute(array, 'grp', [(i, i ^ b) for i in range(groups)])]
    ppermute x8 -> x6, starting transfers between devices: 6.21 us -> 6.54 us  [flipped(): lax.ppermute(array, 'loop', [(i, i ^ bits) for i in range(loop_size)])]
    ppermute x8 -> x6, waiting for transfers between devices: 3.94 us -> 4.08 us  [flipped(): lax.ppermute(array, 'loop', [(i, i ^ bits) for i in range(loop_size)])]
  transfers between devices with their start and end apart: 12 -> 11, of which waited for: 5 -> 6; matrix products, arithmetic and copies ran while one was open for 0% -> 0% of each run, Pallas kernels for 32% -> 20%
where the time goes in v3:
time: 46 us; the launch traced here: 45.8 us
  waiting for transfers between devices  15.2 us (33%)
  starting transfers between devices  14.6 us (32%)
  Pallas kernels  13.2 us (29%)
  local copies, waits for them, and re-layouts  2.67 us (6%)
    ppermute x5, waiting for transfers between devices, over_grp(): return lax.ppermute(array, 'grp', [(i, i ^ b) for i in range(groups)])  11.1 us
    ppermute x5, starting transfers between devices, over_grp(): return lax.ppermute(array, 'grp', [(i, i ^ b) for i in range(groups)])  8.09 us
    pallas_call x3, Pallas kernels, attend(): pl.pallas_call(functools.partial(blocks_kernel, loop_size, tuple(served),...  6.59 us
    ppermute x6, starting transfers between devices, flipped(): lax.ppermute(array, 'loop', [(i, i ^ bits) for i in range(loop_size)])  6.54 us
    ppermute x6, waiting for transfers between devices, flipped(): lax.ppermute(array, 'loop', [(i, i ^ bits) for i in range(loop_size)])  4.08 us
    unnamed x16, local copies, waits for them, and re-layouts  2.67 us
    pallas_call x1, Pallas kernels, shards(): pl.pallas_call(functools.partial(prep_kernel, groups), out_shape=[tile_sh...  2.63 us
    pallas_call x1, Pallas kernels, shards(): pl.pallas_call(functools.partial(weigh_kernel, groups), out_shape=[jax.Sh...  2.01 us
  transfers between devices with their start and end apart: 11, of which 6 were waited for; matrix products, arithmetic and copies ran while one was open for 0% of the time, Pallas kernels for 20%

profile of v3, /device:TPU:0, one launch (start us, length us, event | category | flops | bytes accessed | tf_op | source)
XLA Modules:
  0.0 45.8 jit_solution(14766801530479772944)
XLA Ops:
  0.0 2.6 %prep.1 = (bf16[1024,256]{1,0:T(8,128)(2,1)}, bf16[192,1024]{1,0:T(8,128)(2,1)}, bf16[192,1024]{1,0:T(8,128)(2,1)}, bf16[272,512]{1,0:T(8,128)(2,1)}) custom-call(bf16[256,512]{1,0:T(8,128)(2,1)} %k_hbm.1, bf16[256,512]{1,0:T(8,128)(2,1)} %v_hbm.1, s32[3,256]{1,0:T(4,128)} %order_ref.3), custom_call_target="tpu_custom_call" | custom-call | tf_op jit(solution)/shard_map/prep/pallas_call | solution.py:272
  2.6 3.0 %collective-permute-start = (bf16[1024,256]{1,0:T(8,128)(2,1)}, bf16[1024,256]{1,0:T(8,128)(2,1)S(1)}, u32[]{:S(2)}, u32[]{:S(2)}) collective-permute-start(bf16[1024,256]{1,0:T(8,128)(2,1)} %get-tuple-element.35.refs_0_), channel_id=1, source_target_pairs={{0,8},{4,12},{8,0},{12,4},{16,24},{20,28},{24,16},{28,20},{1,9},{5... | collective-permute-start | bytes 1572872 | tf_op jit(solution)/shard_map/ppermute | solution.py:290
  5.6 0.7 %collective-permute-start.1 = (bf16[1024,256]{1,0:T(8,128)(2,1)}, bf16[1024,256]{1,0:T(8,128)(2,1)S(1)}, u32[]{:S(2)}, u32[]{:S(2)}) collective-permute-start(bf16[1024,256]{1,0:T(8,128)(2,1)} %get-tuple-element.35.refs_0_), channel_id=1, source_target_pairs={{0,20},{4,16},{8,28},{12,24},{16,4},{20,0},{24,12},{28,8},{1,21},{... | collective-permute-start | bytes 1572872 | tf_op jit(solution)/shard_map/ppermute | solution.py:290
  6.3 1.0 %collective-permute-start.2 = (bf16[1024,256]{1,0:T(8,128)(2,1)}, bf16[1024,256]{1,0:T(8,128)(2,1)S(1)}, u32[]{:S(2)}, u32[]{:S(2)}) collective-permute-start(bf16[1024,256]{1,0:T(8,128)(2,1)} %get-tuple-element.35.refs_0_), channel_id=1, source_target_pairs={{0,4},{4,0},{8,12},{12,8},{16,20},{20,16},{24,28},{28,24},{1,5},{5... | collective-permute-start | bytes 1572872 | tf_op jit(solution)/shard_map/ppermute | solution.py:290
  7.3 1.6 %collective-permute-start.7 = (bf16[192,1024]{1,0:T(8,128)(2,1)}, bf16[192,1024]{1,0:T(8,128)(2,1)S(1)}, u32[]{:S(2)}, u32[]{:S(2)}) collective-permute-start(bf16[192,1024]{1,0:T(8,128)(2,1)} %get-tuple-element.42), channel_id=1, source_target_pairs={{0,1},{1,0},{2,3},{3,2},{4,5},{5,4},{6,7},{7,6},{8,9},{9,8},{10,11... | collective-permute-start | bytes 1179656 | tf_op jit(solution)/shard_map/ppermute | solution.py:287
  8.9 2.6 %collective-permute-start.8 = (bf16[272,512]{1,0:T(8,128)(2,1)}, bf16[272,512]{1,0:T(8,128)(2,1)S(1)}, u32[]{:S(2)}, u32[]{:S(2)}) collective-permute-start(bf16[272,512]{1,0:T(8,128)(2,1)} %get-tuple-element.43), channel_id=1, source_target_pairs={{0,2},{1,3},{2,0},{3,1},{4,6},{5,7},{6,4},{7,5},{8,10},{9,11},{10,... | collective-permute-start | bytes 835592 | tf_op jit(solution)/shard_map/ppermute | solution.py:287
  11.4 0.0 copy-start.1
  11.4 0.9 %copy-done.1 = bf16[256,512]{1,0:T(8,128)(2,1)S(1)} copy-done((bf16[256,512]{1,0:T(8,128)(2,1)S(1)}, bf16[256,512]{1,0:T(8,128)(2,1)}, u32[]{:S(2)}) %copy-start.1) | copy-done | bytes 262168
  12.4 0.0 copy-start.3
  12.4 1.0 %copy-done.3 = bf16[1024,256]{1,0:T(8,128)(2,1)S(1)} copy-done((bf16[1024,256]{1,0:T(8,128)(2,1)S(1)}, bf16[1024,256]{1,0:T(8,128)(2,1)}, u32[]{:S(2)}) %copy-start.3) | copy-done | bytes 524312
  13.4 0.0 copy-start.6
  13.4 0.7 %copy-done.6 = s32[1,4]{1,0:T(1,128)S(1)} copy-done((s32[1,4]{1,0:T(1,128)S(1)}, s32[1,4]{1,0:T(1,128)}, u32[]{:S(2)}) %copy-start.6) | copy-done | bytes 40
  14.1 1.8 %blocks0.1 = (f32[512,256]{1,0:T(8,128)S(1)}, f32[16,256]{1,0:T(8,128)S(1)}, bf16[4,128,512]{2,1,0:T(8,128)(2,1)S(1)}) custom-call(s32[1,4]{1,0:T(1,128)S(1)} %copy-done.6, bf16[1024,256]{1,0:T(8,128)(2,1)S(1)} %copy-done.3, bf16[256,512]{1,0:T(8,128)(2,1)S(1)} %copy-done.1), custom_call_target="tpu_custom_call" | custom-call | flops 1000 | bytes 1000 | tf_op jit(solution)/shard_map/blocks0/pallas_call | solution.py:303
  15.9 1.9 %collective-permute-done.refs_1_ = bf16[1024,256]{1,0:T(8,128)(2,1)S(1)} collective-permute-done((bf16[1024,256]{1,0:T(8,128)(2,1)}, bf16[1024,256]{1,0:T(8,128)(2,1)S(1)}, u32[]{:S(2)}, u32[]{:S(2)}) %collective-permute-start) | collective-permute-done | bytes 524320 | tf_op jit(solution)/shard_map/ppermute | solution.py:290
  17.8 2.2 %collective-permute-done.1.refs_2_ = bf16[1024,256]{1,0:T(8,128)(2,1)S(1)} collective-permute-done((bf16[1024,256]{1,0:T(8,128)(2,1)}, bf16[1024,256]{1,0:T(8,128)(2,1)S(1)}, u32[]{:S(2)}, u32[]{:S(2)}) %collective-permute-start.1) | collective-permute-done | bytes 524320 | tf_op jit(solution)/shard_map/ppermute | solution.py:290
  20.0 0.0 collective-permute-done.2.refs_0_
  20.0 0.2 collective-permute-start.3
  20.2 1.1 %collective-permute-start.4 = (bf16[1024,256]{1,0:T(8,128)(2,1)S(1)}, bf16[1024,256]{1,0:T(8,128)(2,1)S(1)}, u32[]{:S(2)}, u32[]{:S(2)}) collective-permute-start(bf16[1024,256]{1,0:T(8,128)(2,1)S(1)} %collective-permute-done.refs_1_), channel_id=1, source_target_pairs={{0,16},{4,20},{8,24},{12,28},{16,0},{20,4},{24,8},{28,12},{1,17},{... | collective-permute-start | bytes 1572872 | tf_op jit(solution)/shard_map/ppermute | solution.py:290
  21.3 0.5 %collective-permute-start.5 = (bf16[1024,256]{1,0:T(8,128)(2,1)S(1)}, bf16[1024,256]{1,0:T(8,128)(2,1)S(1)}, u32[]{:S(2)}, u32[]{:S(2)}) collective-permute-start(bf16[1024,256]{1,0:T(8,128)(2,1)S(1)} %collective-permute-done.1.refs_2_), channel_id=1, source_target_pairs={{0,8},{4,12},{8,0},{12,4},{16,24},{20,28},{24,16},{28,20},{1,9},{5... | collective-permute-start | bytes 1572872 | tf_op jit(solution)/shard_map/ppermute | solution.py:290
  21.9 1.8 %collective-permute-done.8.order_ref.rows_ref = bf16[272,512]{1,0:T(8,128)(2,1)S(1)} collective-permute-done((bf16[272,512]{1,0:T(8,128)(2,1)}, bf16[272,512]{1,0:T(8,128)(2,1)S(1)}, u32[]{:S(2)}, u32[]{:S(2)}) %collective-permute-start.8) | collective-permute-done | bytes 278560 | tf_op jit(solution)/shard_map/ppermute | solution.py:287
  23.7 3.3 %collective-permute-start.6 = (bf16[256,512]{1,0:T(8,128)(2,1)}, bf16[256,512]{1,0:T(8,128)(2,1)S(1)}, u32[]{:S(2)}, u32[]{:S(2)}) collective-permute-start(bf16[256,512]{1,0:T(8,128)(2,1)} %v_hbm.1), channel_id=1, source_target_pairs={{0,2},{1,3},{2,0},{3,1},{4,6},{5,7},{6,4},{7,5},{8,10},{9,11},{10,... | collective-permute-start | bytes 786440 | tf_op jit(solution)/shard_map/ppermute | solution.py:287
  27.0 0.3 relay_keys.1
  27.3 0.0 collective-permute-done.7.refs_1_.refs_5_
  27.3 0.0 copy-start.7
  27.3 0.2 collective-permute-start.9
  27.5 1.8 %blocks1_2_4.1 = (f32[512,256]{1,0:T(8,128)S(1)}, f32[16,256]{1,0:T(8,128)S(1)}) custom-call(s32[1,4]{1,0:T(1,128)S(1)} %copy-done.6, bf16[1024,256]{1,0:T(8,128)(2,1)S(1)} %collective-permute-done.2.refs_0_, bf16[1024,256]{1,0:T(8,128)(2,1)S(1)} %collective-permute-done.refs_1_, ...), custom_call_target="tpu_custom_call", output_to_operand_aliasing={{0}: (5, {}), {1}: (6, {})} | custom-call | flops 1000 | bytes 1000 | tf_op jit(solution)/shard_map/blocks1_2_4/pallas_call | solution.py:303
  29.3 7.0 %collective-permute-done.9.refs_3_ = bf16[192,512]{1,0:T(8,128)(2,1)S(1)} collective-permute-done((bf16[192,512]{1,0:T(8,128)(2,1)S(1)}, bf16[192,512]{1,0:T(8,128)(2,1)S(1)}, u32[]{:S(2)}, u32[]{:S(2)}) %collective-permute-start.9) | collective-permute-done | bytes 196640 | tf_op jit(solution)/shard_map/ppermute | solution.py:287
  36.3 2.1 %collective-permute-done.6.rows_ref = bf16[256,512]{1,0:T(8,128)(2,1)S(1)} collective-permute-done((bf16[256,512]{1,0:T(8,128)(2,1)}, bf16[256,512]{1,0:T(8,128)(2,1)S(1)}, u32[]{:S(2)}, u32[]{:S(2)}) %collective-permute-start.6) | collective-permute-done | bytes 262176 | tf_op jit(solution)/shard_map/ppermute | solution.py:287
  38.4 0.0 copy-start
  38.4 0.0 copy-start.2
  38.4 0.0 copy-start.5
  38.4 0.3 relay_vals.1
  38.7 0.5 %collective-permute-start.10 = (bf16[192,512]{1,0:T(8,128)(2,1)S(1)}, bf16[192,512]{1,0:T(8,128)(2,1)S(1)}, u32[]{:S(2)}, u32[]{:S(2)}) collective-permute-start(bf16[192,512]{1,0:T(8,128)(2,1)S(1)} %get-tuple-element.64), channel_id=1, source_target_pairs={{0,1},{1,0},{2,3},{3,2},{4,5},{5,4},{6,7},{7,6},{8,9},{9,8},{10,11... | collective-permute-start | bytes 589832 | tf_op jit(solution)/shard_map/ppermute | solution.py:287
  39.2 0.0 copy-done.7
  39.2 0.0 collective-permute-done.3.refs_0_
  39.2 0.0 collective-permute-done.4.refs_1_
  39.2 0.0 collective-permute-done.5.refs_2_
  39.2 3.0 %blocks3_5_6.1 = (f32[256,512]{1,0:T(8,128)S(1)}, f32[256,128]{1,0:T(8,128)S(1)}) custom-call(s32[1,4]{1,0:T(1,128)S(1)} %copy-done.6, bf16[1024,256]{1,0:T(8,128)(2,1)S(1)} %collective-permute-done.3.refs_0_, bf16[1024,256]{1,0:T(8,128)(2,1)S(1)} %collective-permute-done.4.refs_1_, bf16[1024,256]{1,0:T(8,128)(2,1)S(1)} %collective-permute-done.5.refs_2_, ...), custom_call_target="tpu_custom_call" | custom-call | flops 1000 | bytes 1000 | tf_op jit(solution)/shard_map/blocks3_5_6/pallas_call | solution.py:303
  42.2 0.0 copy-start.4
  42.2 0.0 copy-done
  42.2 0.0 copy-done.2
  42.2 0.0 copy-done.5
  42.2 2.0 %weigh.1 = (f32[256,512]{1,0:T(8,128)S(1)}, f32[3,256,512]{2,1,0:T(8,128)S(1)}) custom-call(bf16[256,512]{1,0:T(8,128)(2,1)S(1)} %copy-done.2, s32[3,256]{1,0:T(4,128)S(1)} %copy-done.5, f32[3,128]{1,0:T(4,128)S(1)} %pad.4.bias_ref, f32[256,512]{1,0:T(8,128)S(1)} %get-tuple-element.54.acc_ref, f32[256,128]{1,0:T(8,128)S(1)} %get-tuple-element.55.stat_ref, ...), custom_call_target="tpu_custom_call" | custom-call | flops 1000 | bytes 1000 | tf_op jit(solution)/shard_map/weigh/pallas_call | solution.py:366
  44.3 0.2 collective-permute-done.10.val_ref
  44.5 0.0 copy-done.4
  44.5 1.4 %finish.1 = bf16[256,512]{1,0:T(8,128)(2,1)} custom-call(s32[3,256]{1,0:T(4,128)S(1)} %copy-done.5, f32[256,512]{1,0:T(8,128)S(1)} %get-tuple-element.62.part_ref, f32[3,256,512]{2,1,0:T(8,128)S(1)} %get-tuple-element.63.edge_ref, bf16[512,512]{1,0:T(8,128)(2,1)S(1)} %copy-done.4, bf16[192,512]{1,0:T(8,128)(2,1)S(1)} %collective-permute-done.10.val_ref), custom_call_target="tpu_custom_call" | custom-call | flops 1000 | bytes 1000 | tf_op jit(solution)/shard_map/finish/pallas_call | solution.py:378
  (1 shorter events, 0.0 us)
Async XLA Ops:
  2.6 15.1 %collective-permute-start = (bf16[1024,256]{1,0:T(8,128)(2,1)}, bf16[1024,256]{1,0:T(8,128)(2,1)S(1)}, u32[]{:S(2)}, u32[]{:S(2)}) collective-permute-start(bf16[1024,256]{1,0:T(8,128)(2,1)} %get-tuple-element.35.refs_0_), channel_id=1, source_target_pairs={{0,8},{4,12},{8,0},{12,4},{16,24},{20,28},{24,16},{28,20},{1,9},{5... | collective-permute-start | bytes 1572872 | tf_op jit(solution)/shard_map/ppermute | solution.py:290
  5.6 14.3 %collective-permute-start.1 = (bf16[1024,256]{1,0:T(8,128)(2,1)}, bf16[1024,256]{1,0:T(8,128)(2,1)S(1)}, u32[]{:S(2)}, u32[]{:S(2)}) collective-permute-start(bf16[1024,256]{1,0:T(8,128)(2,1)} %get-tuple-element.35.refs_0_), channel_id=1, source_target_pairs={{0,20},{4,16},{8,28},{12,24},{16,4},{20,0},{24,12},{28,8},{1,21},{... | collective-permute-start | bytes 1572872 | tf_op jit(solution)/shard_map/ppermute | solution.py:290
  6.3 13.7 %collective-permute-start.2 = (bf16[1024,256]{1,0:T(8,128)(2,1)}, bf16[1024,256]{1,0:T(8,128)(2,1)S(1)}, u32[]{:S(2)}, u32[]{:S(2)}) collective-permute-start(bf16[1024,256]{1,0:T(8,128)(2,1)} %get-tuple-element.35.refs_0_), channel_id=1, source_target_pairs={{0,4},{4,0},{8,12},{12,8},{16,20},{20,16},{24,28},{28,24},{1,5},{5... | collective-permute-start | bytes 1572872 | tf_op jit(solution)/shard_map/ppermute | solution.py:290
  7.3 20.0 %collective-permute-start.7 = (bf16[192,1024]{1,0:T(8,128)(2,1)}, bf16[192,1024]{1,0:T(8,128)(2,1)S(1)}, u32[]{:S(2)}, u32[]{:S(2)}) collective-permute-start(bf16[192,1024]{1,0:T(8,128)(2,1)} %get-tuple-element.42), channel_id=1, source_target_pairs={{0,1},{1,0},{2,3},{3,2},{4,5},{5,4},{6,7},{7,6},{8,9},{9,8},{10,11... | collective-permute-start | bytes 1179656 | tf_op jit(solution)/shard_map/ppermute | solution.py:287
  8.9 14.8 %collective-permute-start.8 = (bf16[272,512]{1,0:T(8,128)(2,1)}, bf16[272,512]{1,0:T(8,128)(2,1)S(1)}, u32[]{:S(2)}, u32[]{:S(2)}) collective-permute-start(bf16[272,512]{1,0:T(8,128)(2,1)} %get-tuple-element.43), channel_id=1, source_target_pairs={{0,2},{1,3},{2,0},{3,1},{4,6},{5,7},{6,4},{7,5},{8,10},{9,11},{10,... | collective-permute-start | bytes 835592 | tf_op jit(solution)/shard_map/ppermute | solution.py:287
  11.4 0.9 %copy-start.1 = (bf16[256,512]{1,0:T(8,128)(2,1)S(1)}, bf16[256,512]{1,0:T(8,128)(2,1)}, u32[]{:S(2)}) copy-start(bf16[256,512]{1,0:T(8,128)(2,1)} %q_ref.1) | copy-start | bytes 786436
  12.4 1.0 %copy-start.3 = (bf16[1024,256]{1,0:T(8,128)(2,1)S(1)}, bf16[1024,256]{1,0:T(8,128)(2,1)}, u32[]{:S(2)}) copy-start(bf16[1024,256]{1,0:T(8,128)(2,1)} %get-tuple-element.35.refs_0_) | copy-start | bytes 1572868
  13.4 0.7 %copy-start.6 = (s32[1,4]{1,0:T(1,128)S(1)}, s32[1,4]{1,0:T(1,128)}, u32[]{:S(2)}) copy-start(s32[1,4]{1,0:T(1,128)} %tiles_ref.5) | copy-start | bytes 52
  20.0 19.2 %collective-permute-start.3 = (bf16[1024,256]{1,0:T(8,128)(2,1)S(1)}, bf16[1024,256]{1,0:T(8,128)(2,1)S(1)}, u32[]{:S(2)}, u32[]{:S(2)}) collective-permute-start(bf16[1024,256]{1,0:T(8,128)(2,1)S(1)} %collective-permute-done.refs_1_), channel_id=1, source_target_pairs={{0,4},{4,0},{8,12},{12,8},{16,20},{20,16},{24,28},{28,24},{1,5},{5... | collective-permute-start | bytes 1572872 | tf_op jit(solution)/shard_map/ppermute | solution.py:290
  20.2 19.0 %collective-permute-start.4 = (bf16[1024,256]{1,0:T(8,128)(2,1)S(1)}, bf16[1024,256]{1,0:T(8,128)(2,1)S(1)}, u32[]{:S(2)}, u32[]{:S(2)}) collective-permute-start(bf16[1024,256]{1,0:T(8,128)(2,1)S(1)} %collective-permute-done.refs_1_), channel_id=1, source_target_pairs={{0,16},{4,20},{8,24},{12,28},{16,0},{20,4},{24,8},{28,12},{1,17},{... | collective-permute-start | bytes 1572872 | tf_op jit(solution)/shard_map/ppermute | solution.py:290
  21.3 17.9 %collective-permute-start.5 = (bf16[1024,256]{1,0:T(8,128)(2,1)S(1)}, bf16[1024,256]{1,0:T(8,128)(2,1)S(1)}, u32[]{:S(2)}, u32[]{:S(2)}) collective-permute-start(bf16[1024,256]{1,0:T(8,128)(2,1)S(1)} %collective-permute-done.1.refs_2_), channel_id=1, source_target_pairs={{0,8},{4,12},{8,0},{12,4},{16,24},{20,28},{24,16},{28,20},{1,9},{5... | collective-permute-start | bytes 1572872 | tf_op jit(solution)/shard_map/ppermute | solution.py:290
  23.7 14.7 %collective-permute-start.6 = (bf16[256,512]{1,0:T(8,128)(2,1)}, bf16[256,512]{1,0:T(8,128)(2,1)S(1)}, u32[]{:S(2)}, u32[]{:S(2)}) collective-permute-start(bf16[256,512]{1,0:T(8,128)(2,1)} %v_hbm.1), channel_id=1, source_target_pairs={{0,2},{1,3},{2,0},{3,1},{4,6},{5,7},{6,4},{7,5},{8,10},{9,11},{10,... | collective-permute-start | bytes 786440 | tf_op jit(solution)/shard_map/ppermute | solution.py:287
  27.3 11.9 %copy-start.7 = (f32[3,8]{1,0:T(4,128)S(1)}, f32[3,8]{1,0:T(4,128)}, u32[]{:S(2)}) copy-start(f32[3,8]{1,0:T(4,128)} %param.13) | copy-start | bytes 292
  27.3 9.0 %collective-permute-start.9 = (bf16[192,512]{1,0:T(8,128)(2,1)S(1)}, bf16[192,512]{1,0:T(8,128)(2,1)S(1)}, u32[]{:S(2)}, u32[]{:S(2)}) collective-permute-start(bf16[192,512]{1,0:T(8,128)(2,1)S(1)} %get-tuple-element.44), channel_id=1, source_target_pairs={{0,1},{1,0},{2,3},{3,2},{4,5},{5,4},{6,7},{7,6},{8,9},{9,8},{10,11... | collective-permute-start | bytes 589832 | tf_op jit(solution)/shard_map/ppermute | solution.py:287
  38.4 3.8 %copy-start = (bf16[192,1024]{1,0:T(8,128)(2,1)S(1)}, bf16[192,1024]{1,0:T(8,128)(2,1)}, u32[]{:S(2)}) copy-start(bf16[192,1024]{1,0:T(8,128)(2,1)} %get-tuple-element.56.refs_0_.refs_4_) | copy-start | bytes 1179652
  38.4 3.8 %copy-start.2 = (bf16[256,512]{1,0:T(8,128)(2,1)S(1)}, bf16[256,512]{1,0:T(8,128)(2,1)}, u32[]{:S(2)}) copy-start(bf16[256,512]{1,0:T(8,128)(2,1)} %q_ref.1) | copy-start | bytes 786436
  38.4 3.8 %copy-start.5 = (s32[3,256]{1,0:T(4,128)S(1)}, s32[3,256]{1,0:T(4,128)}, u32[]{:S(2)}) copy-start(s32[3,256]{1,0:T(4,128)} %order_ref.3) | copy-start | bytes 9220
  38.7 5.7 %collective-permute-start.10 = (bf16[192,512]{1,0:T(8,128)(2,1)S(1)}, bf16[192,512]{1,0:T(8,128)(2,1)S(1)}, u32[]{:S(2)}, u32[]{:S(2)}) collective-permute-start(bf16[192,512]{1,0:T(8,128)(2,1)S(1)} %get-tuple-element.64), channel_id=1, source_target_pairs={{0,1},{1,0},{2,3},{3,2},{4,5},{5,4},{6,7},{7,6},{8,9},{9,8},{10,11... | collective-permute-start | bytes 589832 | tf_op jit(solution)/shard_map/ppermute | solution.py:287
  42.2 2.2 %copy-start.4 = (bf16[512,512]{1,0:T(8,128)(2,1)S(1)}, bf16[512,512]{1,0:T(8,128)(2,1)}, u32[]{:S(2)}) copy-start(bf16[512,512]{1,0:T(8,128)(2,1)} %w_ref.1) | copy-start | bytes 1572868

commit v4 on v3

--- a/solution.py
+++ b/solution.py
@@ -16,6 +16,7 @@
 NEG_FILL = -1e30
 VMEM_BYTES = 40 * 1024 * 1024
 
+LONG = pl.CostEstimate(flops=10**10, bytes_accessed=1000, transcendentals=0)
 CHEAP = pl.CostEstimate(flops=1000, bytes_accessed=1000, transcendentals=0)
 F32 = jnp.float32
 BF16 = jnp.bfloat16
@@ -241,7 +242,7 @@
     part_ref[...] = numer
 
 
-def finish_kernel(groups, order_ref, part_ref, edge_ref, w_ref, val_ref, out_ref):
+def finish_kernel(groups, val_ref, order_ref, part_ref, edge_ref, w_ref, out_ref):
     rows, width = part_ref.shape
     bucket = rows // groups
     numer = part_ref[...]
@@ -314,7 +315,7 @@
             ],
             input_output_aliases=aliases,
             compiler_params=params,
-            cost_estimate=CHEAP,
+            cost_estimate=LONG if state is None else CHEAP,
             name="blocks" + "_".join(map(str, served)),
         )(tile_list, *served.values(), *others)
         return [pairs[0] if state is None else state[0], acc, stat]
@@ -338,15 +339,16 @@
         across = flipped(own_tile, 5)
         twin = flipped(own_tile, 1)
         state = attend({0: own_tile}, None, False)
-        side, across, twin, own_vals, state = fence((side, across, twin, value_rows, state))
+        side, across, twin, state = fence((side, across, twin, state))
         corner = flipped(side, 4)
         corner_twin = flipped(across, 2)
         side_twin = flipped(side, 1)
+        full_k, own_vals = fence((full_k, value_rows))
         full_v = over_grp(own_vals, 2)
         keys_2, passed = relay(full_k, full_k, "relay_keys")
         keys_3 = over_grp(passed, 1)
         state = attend({1: twin, 2: side, 4: across}, state, False)
-        full_v, near, keys_3, state = fence((full_v, near, keys_3, state))
+        full_v, near, state = fence((full_v, near, state))
         vals_2, passed = relay(full_k, full_v, "relay_vals")
         vals_3 = over_grp(passed, 1)
         key_parts = [outgoing[0], near, keys_2, keys_3]
@@ -383,7 +385,7 @@
         compiler_params=params,
         cost_estimate=CHEAP,
         name="finish",
-    )(expander_order, part, edge, out_weight, val_parts[-1])
+    )(val_parts[-1], expander_order, part, edge, out_weight)
 
 
 def solution(mesh):

time: 46 us -> 44.6 us (0.970)
  waiting for transfers between devices: 15.2 us -> 14 us
    ppermute x5, waiting for transfers between devices: 11.1 us -> 9.93 us  [over_grp(): return lax.ppermute(array, 'grp', [(i, i ^ b) for i in range(groups)])]
    unnamed x16 -> x18, local copies, waits for them, and re-layouts: 2.67 us -> 2.67 us
  transfers between devices with their start and end apart: 11 -> 11, of which waited for: 6 -> 5; matrix products, arithmetic and copies ran while one was open for 0% -> 0% of each run, Pallas kernels for 20% -> 21%
where the time goes in v4:
time: 44.6 us; the launch traced here: 44.4 us
  starting transfers between devices  14.3 us (32%)
  waiting for transfers between devices  14 us (31%)
  Pallas kernels  13.2 us (30%)
  local copies, waits for them, and re-layouts  2.68 us (6%)
    ppermute x5, waiting for transfers between devices, over_grp(): return lax.ppermute(array, 'grp', [(i, i ^ b) for i in range(groups)])  9.93 us
    ppermute x5, starting transfers between devices, over_grp(): return lax.ppermute(array, 'grp', [(i, i ^ b) for i in range(groups)])  7.8 us
    pallas_call x3, Pallas kernels, attend(): pl.pallas_call(functools.partial(blocks_kernel, loop_size, tuple(served),...  6.6 us
    ppermute x6, starting transfers between devices, flipped(): lax.ppermute(array, 'loop', [(i, i ^ bits) for i in range(loop_size)])  6.54 us
    ppermute x6, waiting for transfers between devices, flipped(): lax.ppermute(array, 'loop', [(i, i ^ bits) for i in range(loop_size)])  4.08 us
    unnamed x18, local copies, waits for them, and re-layouts  2.67 us
    pallas_call x1, Pallas kernels, shards(): pl.pallas_call(functools.partial(prep_kernel, groups), out_shape=[tile_sh...  2.64 us
    pallas_call x1, Pallas kernels, shards(): pl.pallas_call(functools.partial(weigh_kernel, groups), out_shape=[jax.Sh...  2.02 us
  transfers between devices with their start and end apart: 11, of which 5 were waited for; matrix products, arithmetic and copies ran while one was open for 0% of the time, Pallas kernels for 21%

profile of v4, /device:TPU:0, one launch (start us, length us, event | category | flops | bytes accessed | tf_op | source)
XLA Modules:
  0.0 44.4 jit_solution(4520092659397600872)
XLA Ops:
  0.0 2.6 %prep.1 = (bf16[1024,256]{1,0:T(8,128)(2,1)}, bf16[192,1024]{1,0:T(8,128)(2,1)}, bf16[192,1024]{1,0:T(8,128)(2,1)}, bf16[272,512]{1,0:T(8,128)(2,1)}) custom-call(bf16[256,512]{1,0:T(8,128)(2,1)} %k_hbm.1, bf16[256,512]{1,0:T(8,128)(2,1)} %v_hbm.1, s32[3,256]{1,0:T(4,128)} %order_ref.3), custom_call_target="tpu_custom_call" | custom-call | tf_op jit(solution)/shard_map/prep/pallas_call | solution.py:273
  2.6 3.0 %collective-permute-start.3 = (bf16[1024,256]{1,0:T(8,128)(2,1)}, bf16[1024,256]{1,0:T(8,128)(2,1)S(1)}, u32[]{:S(2)}, u32[]{:S(2)}) collective-permute-start(bf16[1024,256]{1,0:T(8,128)(2,1)} %get-tuple-element.39.refs_0_), channel_id=1, source_target_pairs={{0,8},{4,12},{8,0},{12,4},{16,24},{20,28},{24,16},{28,20},{1,9},{5... | collective-permute-start | bytes 1572872 | tf_op jit(solution)/shard_map/ppermute | solution.py:291
  5.6 0.7 %collective-permute-start.4 = (bf16[1024,256]{1,0:T(8,128)(2,1)}, bf16[1024,256]{1,0:T(8,128)(2,1)S(1)}, u32[]{:S(2)}, u32[]{:S(2)}) collective-permute-start(bf16[1024,256]{1,0:T(8,128)(2,1)} %get-tuple-element.39.refs_0_), channel_id=1, source_target_pairs={{0,20},{4,16},{8,28},{12,24},{16,4},{20,0},{24,12},{28,8},{1,21},{... | collective-permute-start | bytes 1572872 | tf_op jit(solution)/shard_map/ppermute | solution.py:291
  6.3 1.0 %collective-permute-start.5 = (bf16[1024,256]{1,0:T(8,128)(2,1)}, bf16[1024,256]{1,0:T(8,128)(2,1)S(1)}, u32[]{:S(2)}, u32[]{:S(2)}) collective-permute-start(bf16[1024,256]{1,0:T(8,128)(2,1)} %get-tuple-element.39.refs_0_), channel_id=1, source_target_pairs={{0,4},{4,0},{8,12},{12,8},{16,20},{20,16},{24,28},{28,24},{1,5},{5... | collective-permute-start | bytes 1572872 | tf_op jit(solution)/shard_map/ppermute | solution.py:291
  7.3 2.6 %collective-permute-start = (bf16[272,512]{1,0:T(8,128)(2,1)}, bf16[272,512]{1,0:T(8,128)(2,1)S(1)}, u32[]{:S(2)}, u32[]{:S(2)}) collective-permute-start(bf16[272,512]{1,0:T(8,128)(2,1)} %get-tuple-element.35), channel_id=1, source_target_pairs={{0,2},{1,3},{2,0},{3,1},{4,6},{5,7},{6,4},{7,5},{8,10},{9,11},{10,... | collective-permute-start | bytes 835592 | tf_op jit(solution)/shard_map/ppermute | solution.py:288
  9.9 1.6 %collective-permute-start.2 = (bf16[192,1024]{1,0:T(8,128)(2,1)}, bf16[192,1024]{1,0:T(8,128)(2,1)S(1)}, u32[]{:S(2)}, u32[]{:S(2)}) collective-permute-start(bf16[192,1024]{1,0:T(8,128)(2,1)} %get-tuple-element.38), channel_id=1, source_target_pairs={{0,1},{1,0},{2,3},{3,2},{4,5},{5,4},{6,7},{7,6},{8,9},{9,8},{10,11... | collective-permute-start | bytes 1179656 | tf_op jit(solution)/shard_map/ppermute | solution.py:288
  11.5 0.0 copy-start.2
  11.5 0.9 %copy-done.2 = bf16[256,512]{1,0:T(8,128)(2,1)S(1)} copy-done((bf16[256,512]{1,0:T(8,128)(2,1)S(1)}, bf16[256,512]{1,0:T(8,128)(2,1)}, u32[]{:S(2)}) %copy-start.2) | copy-done | bytes 262168
  12.4 0.0 copy-start.5
  12.4 0.7 %copy-done.5 = s32[1,4]{1,0:T(1,128)S(1)} copy-done((s32[1,4]{1,0:T(1,128)S(1)}, s32[1,4]{1,0:T(1,128)}, u32[]{:S(2)}) %copy-start.5) | copy-done | bytes 40
  13.1 0.0 copy-start.6
  13.1 1.0 %copy-done.6 = bf16[1024,256]{1,0:T(8,128)(2,1)S(1)} copy-done((bf16[1024,256]{1,0:T(8,128)(2,1)S(1)}, bf16[1024,256]{1,0:T(8,128)(2,1)}, u32[]{:S(2)}) %copy-start.6) | copy-done | bytes 524312
  14.1 0.0 copy-start.7
  14.1 1.8 %blocks0.1 = (f32[512,256]{1,0:T(8,128)S(1)}, f32[16,256]{1,0:T(8,128)S(1)}, bf16[4,128,512]{2,1,0:T(8,128)(2,1)S(1)}) custom-call(s32[1,4]{1,0:T(1,128)S(1)} %copy-done.5, bf16[1024,256]{1,0:T(8,128)(2,1)S(1)} %copy-done.6, bf16[256,512]{1,0:T(8,128)(2,1)S(1)} %copy-done.2), custom_call_target="tpu_custom_call" | custom-call | flops 10000000000 | bytes 1000 | tf_op jit(solution)/shard_map/blocks0/pallas_call | solution.py:304
  15.9 1.9 %collective-permute-done.3.refs_1_ = bf16[1024,256]{1,0:T(8,128)(2,1)S(1)} collective-permute-done((bf16[1024,256]{1,0:T(8,128)(2,1)}, bf16[1024,256]{1,0:T(8,128)(2,1)S(1)}, u32[]{:S(2)}, u32[]{:S(2)}) %collective-permute-start.3) | collective-permute-done | bytes 524320 | tf_op jit(solution)/shard_map/ppermute | solution.py:291
  17.8 2.2 %collective-permute-done.4.refs_2_ = bf16[1024,256]{1,0:T(8,128)(2,1)S(1)} collective-permute-done((bf16[1024,256]{1,0:T(8,128)(2,1)}, bf16[1024,256]{1,0:T(8,128)(2,1)S(1)}, u32[]{:S(2)}, u32[]{:S(2)}) %collective-permute-start.4) | collective-permute-done | bytes 524320 | tf_op jit(solution)/shard_map/ppermute | solution.py:291
  20.0 0.0 collective-permute-done.5.refs_0_
  20.0 0.2 collective-permute-start.7
  20.2 1.1 %collective-permute-start.8 = (bf16[1024,256]{1,0:T(8,128)(2,1)S(1)}, bf16[1024,256]{1,0:T(8,128)(2,1)S(1)}, u32[]{:S(2)}, u32[]{:S(2)}) collective-permute-start(bf16[1024,256]{1,0:T(8,128)(2,1)S(1)} %collective-permute-done.3.refs_1_), channel_id=1, source_target_pairs={{0,16},{4,20},{8,24},{12,28},{16,0},{20,4},{24,8},{28,12},{1,17},{... | collective-permute-start | bytes 1572872 | tf_op jit(solution)/shard_map/ppermute | solution.py:291
  21.3 0.5 %collective-permute-start.9 = (bf16[1024,256]{1,0:T(8,128)(2,1)S(1)}, bf16[1024,256]{1,0:T(8,128)(2,1)S(1)}, u32[]{:S(2)}, u32[]{:S(2)}) collective-permute-start(bf16[1024,256]{1,0:T(8,128)(2,1)S(1)} %collective-permute-done.4.refs_2_), channel_id=1, source_target_pairs={{0,8},{4,12},{8,0},{12,4},{16,24},{20,28},{24,16},{28,20},{1,9},{5... | collective-permute-start | bytes 1572872 | tf_op jit(solution)/shard_map/ppermute | solution.py:291
  21.9 1.1 %collective-permute-done.order_ref.rows_ref = bf16[272,512]{1,0:T(8,128)(2,1)S(1)} collective-permute-done((bf16[272,512]{1,0:T(8,128)(2,1)}, bf16[272,512]{1,0:T(8,128)(2,1)S(1)}, u32[]{:S(2)}, u32[]{:S(2)}) %collective-permute-start) | collective-permute-done | bytes 278560 | tf_op jit(solution)/shard_map/ppermute | solution.py:288
  23.0 0.0 copy-done.7
  23.0 1.4 %collective-permute-start.1 = (bf16[256,512]{1,0:T(8,128)(2,1)S(1)}, bf16[256,512]{1,0:T(8,128)(2,1)S(1)}, u32[]{:S(2)}, u32[]{:S(2)}) collective-permute-start(bf16[256,512]{1,0:T(8,128)(2,1)S(1)} %copy-done.7), channel_id=1, source_target_pairs={{0,2},{1,3},{2,0},{3,1},{4,6},{5,7},{6,4},{7,5},{8,10},{9,11},{10,... | collective-permute-start | bytes 786440 | tf_op jit(solution)/shard_map/ppermute | solution.py:288
  24.5 0.3 relay_keys.1
  24.8 0.0 copy-start.8
  24.8 1.8 %blocks1_2_4.1 = (f32[512,256]{1,0:T(8,128)S(1)}, f32[16,256]{1,0:T(8,128)S(1)}) custom-call(s32[1,4]{1,0:T(1,128)S(1)} %copy-done.5, bf16[1024,256]{1,0:T(8,128)(2,1)S(1)} %collective-permute-done.5.refs_0_, bf16[1024,256]{1,0:T(8,128)(2,1)S(1)} %collective-permute-done.3.refs_1_, ...), custom_call_target="tpu_custom_call", output_to_operand_aliasing={{0}: (5, {}), {1}: (6, {})} | custom-call | flops 1000 | bytes 1000 | tf_op jit(solution)/shard_map/blocks1_2_4/pallas_call | solution.py:304
  26.6 0.0 collective-permute-done.2.refs_1_.refs_5_
  26.6 1.7 %collective-permute-start.10 = (bf16[192,512]{1,0:T(8,128)(2,1)S(1)}, bf16[192,512]{1,0:T(8,128)(2,1)S(1)}, u32[]{:S(2)}, u32[]{:S(2)}) collective-permute-start(bf16[192,512]{1,0:T(8,128)(2,1)S(1)} %get-tuple-element.61), channel_id=1, source_target_pairs={{0,1},{1,0},{2,3},{3,2},{4,5},{5,4},{6,7},{7,6},{8,9},{9,8},{10,11... | collective-permute-start | bytes 589832 | tf_op jit(solution)/shard_map/ppermute | solution.py:288
  28.3 8.6 %collective-permute-done.1.rows_ref = bf16[256,512]{1,0:T(8,128)(2,1)S(1)} collective-permute-done((bf16[256,512]{1,0:T(8,128)(2,1)S(1)}, bf16[256,512]{1,0:T(8,128)(2,1)S(1)}, u32[]{:S(2)}, u32[]{:S(2)}) %collective-permute-start.1) | collective-permute-done | bytes 262176 | tf_op jit(solution)/shard_map/ppermute | solution.py:288
  37.0 0.0 copy-start
  37.0 0.0 copy-start.3
  37.0 0.0 copy-start.4
  37.0 0.3 relay_vals.1
  37.3 0.5 %collective-permute-start.6 = (bf16[192,512]{1,0:T(8,128)(2,1)S(1)}, bf16[192,512]{1,0:T(8,128)(2,1)S(1)}, u32[]{:S(2)}, u32[]{:S(2)}) collective-permute-start(bf16[192,512]{1,0:T(8,128)(2,1)S(1)} %get-tuple-element.52), channel_id=1, source_target_pairs={{0,1},{1,0},{2,3},{3,2},{4,5},{5,4},{6,7},{7,6},{8,9},{9,8},{10,11... | collective-permute-start | bytes 589832 | tf_op jit(solution)/shard_map/ppermute | solution.py:288
  37.8 0.0 copy-done.8
  37.8 0.0 collective-permute-done.7.refs_0_
  37.8 0.0 collective-permute-done.8.refs_1_
  37.8 0.0 collective-permute-done.9.refs_2_
  37.8 3.0 %blocks3_5_6.1 = (f32[256,512]{1,0:T(8,128)S(1)}, f32[256,128]{1,0:T(8,128)S(1)}) custom-call(s32[1,4]{1,0:T(1,128)S(1)} %copy-done.5, bf16[1024,256]{1,0:T(8,128)(2,1)S(1)} %collective-permute-done.7.refs_0_, bf16[1024,256]{1,0:T(8,128)(2,1)S(1)} %collective-permute-done.8.refs_1_, bf16[1024,256]{1,0:T(8,128)(2,1)S(1)} %collective-permute-done.9.refs_2_, ...), custom_call_target="tpu_custom_call" | custom-call | flops 1000 | bytes 1000 | tf_op jit(solution)/shard_map/blocks3_5_6/pallas_call | solution.py:304
  40.8 0.0 copy-start.1
  40.8 0.0 collective-permute-done.10.refs_3_
  40.8 0.0 copy-done
  40.8 0.0 copy-done.3
  40.8 0.0 copy-done.4
  40.9 2.0 %weigh.1 = (f32[256,512]{1,0:T(8,128)S(1)}, f32[3,256,512]{2,1,0:T(8,128)S(1)}) custom-call(bf16[256,512]{1,0:T(8,128)(2,1)S(1)} %copy-done.3, s32[3,256]{1,0:T(4,128)S(1)} %copy-done.4, f32[3,128]{1,0:T(4,128)S(1)} %pad.4.bias_ref, f32[256,512]{1,0:T(8,128)S(1)} %get-tuple-element.56.acc_ref, f32[256,128]{1,0:T(8,128)S(1)} %get-tuple-element.57.stat_ref, ...), custom_call_target="tpu_custom_call" | custom-call | flops 1000 | bytes 1000 | tf_op jit(solution)/shard_map/weigh/pallas_call | solution.py:368
  42.9 0.1 collective-permute-done.6.val_ref
  43.0 0.0 copy-done.1
  43.0 1.4 %finish.1 = bf16[256,512]{1,0:T(8,128)(2,1)} custom-call(bf16[192,512]{1,0:T(8,128)(2,1)S(1)} %collective-permute-done.6.val_ref, s32[3,256]{1,0:T(4,128)S(1)} %copy-done.4, f32[256,512]{1,0:T(8,128)S(1)} %get-tuple-element.63.part_ref, f32[3,256,512]{2,1,0:T(8,128)S(1)} %get-tuple-element.64.edge_ref, bf16[512,512]{1,0:T(8,128)(2,1)S(1)} %copy-done.1), custom_call_target="tpu_custom_call" | custom-call | flops 1000 | bytes 1000 | tf_op jit(solution)/shard_map/finish/pallas_call | solution.py:380
  (1 shorter events, 0.0 us)
Async XLA Ops:
  2.6 15.1 %collective-permute-start.3 = (bf16[1024,256]{1,0:T(8,128)(2,1)}, bf16[1024,256]{1,0:T(8,128)(2,1)S(1)}, u32[]{:S(2)}, u32[]{:S(2)}) collective-permute-start(bf16[1024,256]{1,0:T(8,128)(2,1)} %get-tuple-element.39.refs_0_), channel_id=1, source_target_pairs={{0,8},{4,12},{8,0},{12,4},{16,24},{20,28},{24,16},{28,20},{1,9},{5... | collective-permute-start | bytes 1572872 | tf_op jit(solution)/shard_map/ppermute | solution.py:291
  5.6 14.3 %collective-permute-start.4 = (bf16[1024,256]{1,0:T(8,128)(2,1)}, bf16[1024,256]{1,0:T(8,128)(2,1)S(1)}, u32[]{:S(2)}, u32[]{:S(2)}) collective-permute-start(bf16[1024,256]{1,0:T(8,128)(2,1)} %get-tuple-element.39.refs_0_), channel_id=1, source_target_pairs={{0,20},{4,16},{8,28},{12,24},{16,4},{20,0},{24,12},{28,8},{1,21},{... | collective-permute-start | bytes 1572872 | tf_op jit(solution)/shard_map/ppermute | solution.py:291
  6.3 13.7 %collective-permute-start.5 = (bf16[1024,256]{1,0:T(8,128)(2,1)}, bf16[1024,256]{1,0:T(8,128)(2,1)S(1)}, u32[]{:S(2)}, u32[]{:S(2)}) collective-permute-start(bf16[1024,256]{1,0:T(8,128)(2,1)} %get-tuple-element.39.refs_0_), channel_id=1, source_target_pairs={{0,4},{4,0},{8,12},{12,8},{16,20},{20,16},{24,28},{28,24},{1,5},{5... | collective-permute-start | bytes 1572872 | tf_op jit(solution)/shard_map/ppermute | solution.py:291
  7.3 15.8 %collective-permute-start = (bf16[272,512]{1,0:T(8,128)(2,1)}, bf16[272,512]{1,0:T(8,128)(2,1)S(1)}, u32[]{:S(2)}, u32[]{:S(2)}) collective-permute-start(bf16[272,512]{1,0:T(8,128)(2,1)} %get-tuple-element.35), channel_id=1, source_target_pairs={{0,2},{1,3},{2,0},{3,1},{4,6},{5,7},{6,4},{7,5},{8,10},{9,11},{10,... | collective-permute-start | bytes 835592 | tf_op jit(solution)/shard_map/ppermute | solution.py:288
  9.9 16.7 %collective-permute-start.2 = (bf16[192,1024]{1,0:T(8,128)(2,1)}, bf16[192,1024]{1,0:T(8,128)(2,1)S(1)}, u32[]{:S(2)}, u32[]{:S(2)}) collective-permute-start(bf16[192,1024]{1,0:T(8,128)(2,1)} %get-tuple-element.38), channel_id=1, source_target_pairs={{0,1},{1,0},{2,3},{3,2},{4,5},{5,4},{6,7},{7,6},{8,9},{9,8},{10,11... | collective-permute-start | bytes 1179656 | tf_op jit(solution)/shard_map/ppermute | solution.py:288
  11.5 0.9 %copy-start.2 = (bf16[256,512]{1,0:T(8,128)(2,1)S(1)}, bf16[256,512]{1,0:T(8,128)(2,1)}, u32[]{:S(2)}) copy-start(bf16[256,512]{1,0:T(8,128)(2,1)} %q_ref.1) | copy-start | bytes 786436
  12.4 0.7 %copy-start.5 = (s32[1,4]{1,0:T(1,128)S(1)}, s32[1,4]{1,0:T(1,128)}, u32[]{:S(2)}) copy-start(s32[1,4]{1,0:T(1,128)} %tiles_ref.5) | copy-start | bytes 52
  13.1 1.0 %copy-start.6 = (bf16[1024,256]{1,0:T(8,128)(2,1)S(1)}, bf16[1024,256]{1,0:T(8,128)(2,1)}, u32[]{:S(2)}) copy-start(bf16[1024,256]{1,0:T(8,128)(2,1)} %get-tuple-element.39.refs_0_) | copy-start | bytes 1572868
  14.1 8.9 %copy-start.7 = (bf16[256,512]{1,0:T(8,128)(2,1)S(1)}, bf16[256,512]{1,0:T(8,128)(2,1)}, u32[]{:S(2)}) copy-start(bf16[256,512]{1,0:T(8,128)(2,1)} %v_hbm.1) | copy-start | bytes 786436
  20.0 17.8 %collective-permute-start.7 = (bf16[1024,256]{1,0:T(8,128)(2,1)S(1)}, bf16[1024,256]{1,0:T(8,128)(2,1)S(1)}, u32[]{:S(2)}, u32[]{:S(2)}) collective-permute-start(bf16[1024,256]{1,0:T(8,128)(2,1)S(1)} %collective-permute-done.3.refs_1_), channel_id=1, source_target_pairs={{0,4},{4,0},{8,12},{12,8},{16,20},{20,16},{24,28},{28,24},{1,5},{5... | collective-permute-start | bytes 1572872 | tf_op jit(solution)/shard_map/ppermute | solution.py:291
  20.2 17.6 %collective-permute-start.8 = (bf16[1024,256]{1,0:T(8,128)(2,1)S(1)}, bf16[1024,256]{1,0:T(8,128)(2,1)S(1)}, u32[]{:S(2)}, u32[]{:S(2)}) collective-permute-start(bf16[1024,256]{1,0:T(8,128)(2,1)S(1)} %collective-permute-done.3.refs_1_), channel_id=1, source_target_pairs={{0,16},{4,20},{8,24},{12,28},{16,0},{20,4},{24,8},{28,12},{1,17},{... | collective-permute-start | bytes 1572872 | tf_op jit(solution)/shard_map/ppermute | solution.py:291
  21.3 16.4 %collective-permute-start.9 = (bf16[1024,256]{1,0:T(8,128)(2,1)S(1)}, bf16[1024,256]{1,0:T(8,128)(2,1)S(1)}, u32[]{:S(2)}, u32[]{:S(2)}) collective-permute-start(bf16[1024,256]{1,0:T(8,128)(2,1)S(1)} %collective-permute-done.4.refs_2_), channel_id=1, source_target_pairs={{0,8},{4,12},{8,0},{12,4},{16,24},{20,28},{24,16},{28,20},{1,9},{5... | collective-permute-start | bytes 1572872 | tf_op jit(solution)/shard_map/ppermute | solution.py:291
  23.0 13.9 %collective-permute-start.1 = (bf16[256,512]{1,0:T(8,128)(2,1)S(1)}, bf16[256,512]{1,0:T(8,128)(2,1)S(1)}, u32[]{:S(2)}, u32[]{:S(2)}) collective-permute-start(bf16[256,512]{1,0:T(8,128)(2,1)S(1)} %copy-done.7), channel_id=1, source_target_pairs={{0,2},{1,3},{2,0},{3,1},{4,6},{5,7},{6,4},{7,5},{8,10},{9,11},{10,... | collective-permute-start | bytes 786440 | tf_op jit(solution)/shard_map/ppermute | solution.py:288
  24.8 13.0 %copy-start.8 = (f32[3,8]{1,0:T(4,128)S(1)}, f32[3,8]{1,0:T(4,128)}, u32[]{:S(2)}) copy-start(f32[3,8]{1,0:T(4,128)} %param.13) | copy-start | bytes 292
  26.6 14.2 %collective-permute-start.10 = (bf16[192,512]{1,0:T(8,128)(2,1)S(1)}, bf16[192,512]{1,0:T(8,128)(2,1)S(1)}, u32[]{:S(2)}, u32[]{:S(2)}) collective-permute-start(bf16[192,512]{1,0:T(8,128)(2,1)S(1)} %get-tuple-element.61), channel_id=1, source_target_pairs={{0,1},{1,0},{2,3},{3,2},{4,5},{5,4},{6,7},{7,6},{8,9},{9,8},{10,11... | collective-permute-start | bytes 589832 | tf_op jit(solution)/shard_map/ppermute | solution.py:288
  37.0 3.9 %copy-start = (bf16[192,1024]{1,0:T(8,128)(2,1)S(1)}, bf16[192,1024]{1,0:T(8,128)(2,1)}, u32[]{:S(2)}) copy-start(bf16[192,1024]{1,0:T(8,128)(2,1)} %get-tuple-element.58.refs_0_.refs_4_) | copy-start | bytes 1179652
  37.0 3.9 %copy-start.3 = (bf16[256,512]{1,0:T(8,128)(2,1)S(1)}, bf16[256,512]{1,0:T(8,128)(2,1)}, u32[]{:S(2)}) copy-start(bf16[256,512]{1,0:T(8,128)(2,1)} %q_ref.1) | copy-start | bytes 786436
  37.0 3.9 %copy-start.4 = (s32[3,256]{1,0:T(4,128)S(1)}, s32[3,256]{1,0:T(4,128)}, u32[]{:S(2)}) copy-start(s32[3,256]{1,0:T(4,128)} %order_ref.3) | copy-start | bytes 9220
  37.3 5.7 %collective-permute-start.6 = (bf16[192,512]{1,0:T(8,128)(2,1)S(1)}, bf16[192,512]{1,0:T(8,128)(2,1)S(1)}, u32[]{:S(2)}, u32[]{:S(2)}) collective-permute-start(bf16[192,512]{1,0:T(8,128)(2,1)S(1)} %get-tuple-element.52), channel_id=1, source_target_pairs={{0,1},{1,0},{2,3},{3,2},{4,5},{5,4},{6,7},{7,6},{8,9},{9,8},{10,11... | collective-permute-start | bytes 589832 | tf_op jit(solution)/shard_map/ppermute | solution.py:288
  40.8 2.2 %copy-start.1 = (bf16[512,512]{1,0:T(8,128)(2,1)S(1)}, bf16[512,512]{1,0:T(8,128)(2,1)}, u32[]{:S(2)}) copy-start(bf16[512,512]{1,0:T(8,128)(2,1)} %w_ref.1) | copy-start | bytes 1572868

commit v5 on v4

--- a/solution.py
+++ b/solution.py
@@ -32,43 +32,35 @@
 
 
 def prep_kernel(groups, k_hbm, v_hbm, order_hbm, tile_ref, *refs):
-    out_refs = refs[:-4]
-    k_ref, v_ref, order_ref, sems = refs[-4:]
-    rows, width = k_ref.shape
+    out_refs, (order_ref, sems) = refs[:-2], refs[-2:]
+    rows, width = k_hbm.shape
     bucket = rows // groups
-    half = width // 2
-    copies = [
-        pltpu.make_async_copy(src, dst, sems.at[i])
-        for i, (src, dst) in enumerate(((order_hbm, order_ref), (v_hbm, v_ref), (k_hbm, k_ref)))
-    ]
+    places = [(order_hbm, order_ref), (k_hbm, tile_ref.at[:, :width]), (v_hbm, tile_ref.at[:, width:])]
+    copies = [pltpu.make_async_copy(src, dst, sems.at[i]) for i, (src, dst) in enumerate(places)]
     for copy in copies:
         copy.start()
-    for copy in copies:
+    copies[0].wait()
+    order = order_ref[...]
+    lane = lax.broadcasted_iota(jnp.int32, order.shape, 1)
+    swapped = jnp.where(lane % 2 == 0, jnp.roll(order, -1, axis=1), jnp.roll(order, 1, axis=1))
+    wanted = jnp.where(lane < bucket, swapped, order)
+    paired = [ref for ref in out_refs if ref.shape[1] == 2 * width]
+    n_slots = len(paired) * bucket
+    tables = [place_table(wanted[j : j + 1, :], rows)[:, :n_slots] for j in range(MATCHINGS)]
+    table = jnp.concatenate(tables, axis=1)
+    for copy in copies[1:]:
         copy.wait()
-    keys = k_ref[...]
-    vals = v_ref[...]
-    order = order_ref[...]
-    tile_ref[:width, :] = vals.T
-    tile_ref[width : width + rows, :] = keys[:, :half]
-    tile_ref[width + rows :, :] = keys[:, half:]
-    paired = [ref for ref in out_refs if ref.shape[1] == 2 * width]
+    tile = tile_ref[...]
     for ref in out_refs[len(paired) :]:
-        ref[:rows, :] = keys
+        ref[:rows, :] = tile[:, :width]
         padded = jnp.concatenate([order, jnp.zeros((ORDER_ROWS - MATCHINGS, rows), jnp.int32)], axis=0)
         ref[rows:, :rows] = padded.astype(F32).astype(BF16)
         ref[rows:, rows:] = jnp.zeros((ORDER_ROWS, width - rows), BF16)
-    lane = lax.broadcasted_iota(jnp.int32, order.shape, 1)
-    swapped = jnp.where(lane % 2 == 0, jnp.roll(order, -1, axis=1), jnp.roll(order, 1, axis=1))
-    wanted = jnp.where(lane < bucket, swapped, order)
+    ordered = dot(table, tile, ((0,), (0,))).astype(BF16)
     for j in range(MATCHINGS):
-        table = place_table(wanted[j : j + 1, :], rows)[:, : len(paired) * bucket]
-        ordered_k = dot(table, keys, ((0,), (0,))).astype(BF16)
-        ordered_v = dot(table, vals, ((0,), (0,))).astype(BF16)
         mine = slice(j * bucket, (j + 1) * bucket)
         for b, out_ref in enumerate(paired):
-            at = slice(b * bucket, (b + 1) * bucket)
-            out_ref[mine, :width] = ordered_k[at]
-            out_ref[mine, width:] = ordered_v[at]
+            out_ref[mine, :] = ordered[j * n_slots + b * bucket : j * n_slots + (b + 1) * bucket]
 
 
 def relay_kernel(groups, order_ref, rows_ref, mine_ref, next_ref):
@@ -76,12 +68,12 @@
     rows = bucket * groups
     full = rows_ref[:rows, :]
     order = order_ref[rows:, :rows].astype(F32).astype(jnp.int32)
+    tables = [place_table(order[j : j + 1, :], rows)[:, 2 * bucket :] for j in range(MATCHINGS)]
+    ordered = dot(jnp.concatenate(tables, axis=1), full, ((0,), (0,))).astype(BF16)
     for j in range(MATCHINGS):
-        table = place_table(order[j : j + 1, :], rows)[:, 2 * bucket :]
-        ordered = dot(table, full, ((0,), (0,))).astype(BF16)
         mine = slice(j * bucket, (j + 1) * bucket)
-        mine_ref[mine, :] = ordered[:bucket]
-        next_ref[mine, :] = ordered[bucket:]
+        mine_ref[mine, :] = ordered[2 * j * bucket : (2 * j + 1) * bucket]
+        next_ref[mine, :] = ordered[(2 * j + 1) * bucket : (2 * j + 2) * bucket]
 
 
 def blocks_kernel(loop_size, served, first, last, tiles_ref, *refs):
@@ -150,9 +142,9 @@
             fetch(next(iter(served)), t).wait()
             scores = []
             for p in range(HEADS // 2):
-                base = width + (p // 2) * rows
-                keys = tile_vmem[t, base : base + rows, (p % 2) * LANES : (p % 2 + 1) * LANES]
+                keys = tile_vmem[t, :, 2 * p * head : (2 * p + 2) * head]
                 scores.append(dot(keys, pairs_ref[p]))
+            vals = tile_vmem[t, :, width:].T
             for p in range(HEADS // 2):
                 old = jnp.concatenate([stat[2 * p : 2 * p + 1], stat[2 * p + 1 : 2 * p + 2]], axis=1)
                 new = jnp.maximum(old, jnp.max(scores[p], axis=0, keepdims=True))
@@ -166,7 +158,7 @@
                     mine = slice(h * head, (h + 1) * head)
                     stat[h : h + 1] = new[:, half]
                     stat[HEADS + h : HEADS + h + 1] = stat[HEADS + h : HEADS + h + 1] * alpha[:, half] + total[:, half]
-                    acc[mine, :] = acc[mine, :] * alpha[:, half] + dot(tile_vmem[t, mine, :], w[:, half])
+                    acc[mine, :] = acc[mine, :] * alpha[:, half] + dot(vals[mine, :], w[:, half])
 
         return carry
 
@@ -186,38 +178,43 @@
     return jnp.concatenate(parts, axis=0)
 
 
-def weigh_kernel(groups, q_ref, order_ref, bias_ref, acc_ref, stat_ref, *refs):
+def score_kernel(groups, q_ref, order_ref, bias_ref, *refs):
     key_refs = refs[:groups]
-    val_refs = refs[groups : 2 * groups - 1]
-    part_ref, edge_ref = refs[2 * groups - 1 :]
+    score_ref = refs[groups]
     rows, width = q_ref.shape
     head = width // HEADS
     bucket = rows // groups
-    scale = head ** (-0.5) * LOG2E
-    unscale = head**0.5
     gather = (
         lax.broadcasted_iota(jnp.int32, (width, LANES), 0) // head
         == lax.broadcasted_iota(jnp.int32, (width, LANES), 1)
     )
     gather = jnp.where(gather, 1.0, 0.0).astype(BF16)
+    queries = q_ref[...].astype(F32)
+    for j in range(MATCHINGS):
+        table = place_table(order_ref[j : j + 1, :], rows)
+        prod = queries * dot(table, rows_in_order(key_refs, j, bucket, 0, width))
+        high = prod.astype(BF16)
+        low = (prod - high.astype(F32)).astype(BF16)
+        score_ref[j] = dot(high, gather) + dot(low, gather) + bias_ref[j : j + 1, :] * head**0.5
+
+
+def weigh_kernel(groups, order_ref, acc_ref, stat_ref, score_ref, *refs):
+    val_refs = refs[: groups - 1]
+    part_ref, edge_ref = refs[groups - 1 :]
+    rows, width = part_ref.shape
+    head = width // HEADS
+    bucket = rows // groups
+    scale = head ** (-0.5) * LOG2E
     spread = (
         lax.broadcasted_iota(jnp.int32, (LANES, width), 1) // head
         == lax.broadcasted_iota(jnp.int32, (LANES, width), 0)
     )
     spread = jnp.where(spread, 1.0, 0.0).astype(BF16)
-    queries = q_ref[...].astype(F32)
     stat = stat_ref[...]
     lane = lax.broadcasted_iota(jnp.int32, stat.shape, 1)
     block_max = jnp.where(lane < HEADS, stat, 0.0)
     block_sum = jnp.where(lane < HEADS, jnp.roll(stat, -HEADS, axis=1), 1.0)
-    edge_scores = []
-    for j in range(MATCHINGS):
-        table = place_table(order_ref[j : j + 1, :], rows)
-        prod = queries * dot(table, rows_in_order(key_refs, j, bucket, 0, width))
-        high = prod.astype(BF16)
-        low = (prod - high.astype(F32)).astype(BF16)
-        edge = dot(high, gather) + dot(low, gather)
-        edge_scores.append(edge + bias_ref[j : j + 1, :] * unscale)
+    edge_scores = [score_ref[j] for j in range(MATCHINGS)]
     top = block_max
     for edge in edge_scores:
         top = jnp.maximum(top, edge)
@@ -264,7 +261,7 @@
     head = width // HEADS
     bucket = rows // groups
     params = pltpu.CompilerParams(vmem_limit_bytes=VMEM_BYTES)
-    tile_shape = jax.ShapeDtypeStruct((width + 2 * rows, width // 2), BF16)
+    tile_shape = jax.ShapeDtypeStruct((rows, 2 * width), BF16)
     relayed = loop_size == 8 and groups == 4
     kv_shape = jax.ShapeDtypeStruct((MATCHINGS * bucket, 2 * width), BF16)
     one_shape = jax.ShapeDtypeStruct((MATCHINGS * bucket, width), BF16)
@@ -276,8 +273,6 @@
         in_specs=[pl.BlockSpec(memory_space=pltpu.HBM)] * 3,
         out_specs=vmem_specs(1 + len(bucket_shapes)),
         scratch_shapes=[
-            pltpu.VMEM((rows, width), BF16),
-            pltpu.VMEM((rows, width), BF16),
             pltpu.VMEM(expander_order.shape, jnp.int32),
             pltpu.SemaphoreType.DMA((3,)),
         ],
@@ -315,10 +310,23 @@
             ],
             input_output_aliases=aliases,
             compiler_params=params,
-            cost_estimate=LONG if state is None else CHEAP,
+            cost_estimate=pl.CostEstimate(flops=1000, bytes_accessed=1000, transcendentals=0) if state is None else CHEAP,
             name="blocks" + "_".join(map(str, served)),
         )(tile_list, *served.values(), *others)
         return [pairs[0] if state is None else state[0], acc, stat]
+
+    bias = jnp.pad(expander_bias, ((0, 0), (0, LANES - HEADS)))
+
+    def score(key_parts):
+        return pl.pallas_call(
+            functools.partial(score_kernel, groups),
+            out_shape=jax.ShapeDtypeStruct((MATCHINGS, rows, LANES), F32),
+            in_specs=vmem_specs(3 + groups),
+            out_specs=pl.BlockSpec(memory_space=pltpu.VMEM),
+            compiler_params=params,
+            cost_estimate=CHEAP,
+            name="score",
+        )(queries, expander_order, bias, *key_parts)
 
     if relayed:
 
@@ -329,32 +337,34 @@
                 in_specs=vmem_specs(2),
                 out_specs=vmem_specs(2),
                 compiler_params=params,
-                cost_estimate=CHEAP,
+                cost_estimate=pl.CostEstimate(flops=10**10 if name == "relay_keys" else 2*10**9, bytes_accessed=1000, transcendentals=0),
                 name=name,
             )(order, full)
 
         full_k = over_grp(outgoing[2], 2)
         near = over_grp(outgoing[1], 1)
+        across = flipped(own_tile, 5)
         side = flipped(own_tile, 2)
-        across = flipped(own_tile, 5)
         twin = flipped(own_tile, 1)
         state = attend({0: own_tile}, None, False)
-        side, across, twin, state = fence((side, across, twin, state))
-        corner = flipped(side, 4)
-        corner_twin = flipped(across, 2)
-        side_twin = flipped(side, 1)
-        full_k, own_vals = fence((full_k, value_rows))
+        full_k, own_vals, state = fence((full_k, value_rows, state))
         full_v = over_grp(own_vals, 2)
         keys_2, passed = relay(full_k, full_k, "relay_keys")
+        across, side, twin, state, keys_2, passed = fence((across, side, twin, state, keys_2, passed))
+        corner_twin = flipped(across, 2)
+        corner = flipped(side, 4)
+        side_twin = flipped(side, 1)
         keys_3 = over_grp(passed, 1)
         state = attend({1: twin, 2: side, 4: across}, state, False)
         full_v, near, state = fence((full_v, near, state))
+        state = attend({3: side_twin}, state, False)
         vals_2, passed = relay(full_k, full_v, "relay_vals")
         vals_3 = over_grp(passed, 1)
-        key_parts = [outgoing[0], near, keys_2, keys_3]
         val_parts = [outgoing[0], near, vals_2, vals_3]
-        late = {3: side_twin, 5: corner, 6: corner_twin}
+        late = {5: corner, 6: corner_twin}
         _, acc, stat = attend(late, state, True)
+        keys_3, acc, stat = fence((keys_3, acc, stat))
+        scores = score([outgoing[0], near, keys_2, keys_3])
     else:
         tiles = {}
         for offset in range(-RADIUS, RADIUS + 1):
@@ -362,21 +372,21 @@
             tile = lax.ppermute(own_tile, "loop", pairs) if offset else own_tile
             tiles[offset + RADIUS] = tile
         _, acc, stat = attend(tiles, None, True)
-        key_parts = val_parts = [outgoing[0]] + [over_grp(outgoing[b], b) for b in range(1, groups)]
-
-    bias = jnp.pad(expander_bias, ((0, 0), (0, LANES - HEADS)))
+        val_parts = [outgoing[0]] + [over_grp(outgoing[b], b) for b in range(1, groups)]
+        scores = score(val_parts)
+
     part, edge = pl.pallas_call(
         functools.partial(weigh_kernel, groups),
         out_shape=[
             jax.ShapeDtypeStruct((rows, width), F32),
             jax.ShapeDtypeStruct((MATCHINGS, rows, width), F32),
         ],
-        in_specs=vmem_specs(4 + 2 * groups),
+        in_specs=vmem_specs(3 + groups),
         out_specs=vmem_specs(2),
         compiler_params=params,
         cost_estimate=CHEAP,
         name="weigh",
-    )(queries, expander_order, bias, acc, stat, *key_parts, *val_parts[:-1])
+    )(expander_order, acc, stat, scores, *val_parts[:-1])
     return pl.pallas_call(
         functools.partial(finish_kernel, groups),
         out_shape=jax.ShapeDtypeStruct((rows, width), BF16),

time: 44.6 us -> 43.7 us (0.980)
  starting transfers between devices: 14.3 us -> 11.7 us
  waiting for transfers between devices: 14 us -> 14.9 us
  Pallas kernels: 13.2 us -> 13.9 us
    ppermute x5, waiting for transfers between devices: 9.93 us -> 12 us  [over_grp(): return lax.ppermute(array, 'grp', [(i, i ^ b) for i in range(groups)])]
    ppermute x6, starting transfers between devices: 6.54 us -> 4.85 us  [flipped(): lax.ppermute(array, 'loop', [(i, i ^ bits) for i in range(loop_size)])]
    ppermute x6, waiting for transfers between devices: 4.08 us -> 2.88 us  [flipped(): lax.ppermute(array, 'loop', [(i, i ^ bits) for i in range(loop_size)])]
    pallas_call x0 -> x1, Pallas kernels: none -> 1.03 us  [score(): pl.pallas_call(functools.partial(score_kernel, groups), out_shape=jax.Sha...]
    ppermute x5, starting transfers between devices: 7.8 us -> 6.8 us  [over_grp(): return lax.ppermute(array, 'grp', [(i, i ^ b) for i in range(groups)])]
    pallas_call x1, Pallas kernels: 2.02 us -> 1.05 us  [shards(): pl.pallas_call(functools.partial(weigh_kernel, groups), out_shape=[jax.Sh...]
    pallas_call x3 -> x4, Pallas kernels: 6.6 us -> 7.54 us  [attend(): pl.pallas_call(functools.partial(blocks_kernel, loop_size, tuple(served),...]
  transfers between devices with their start and end apart: 11 -> 11, of which waited for: 5 -> 8; matrix products, arithmetic and copies ran while one was open for 0% -> 0% of each run, Pallas kernels for 21% -> 23%
where the time goes in v5:
time: 43.7 us; the launch traced here: 43.4 us
  waiting for transfers between devices  14.9 us (34%)
  Pallas kernels  13.9 us (32%)
  starting transfers between devices  11.7 us (27%)
  local copies, waits for them, and re-layouts  2.81 us (6%)
    ppermute x5, waiting for transfers between devices, over_grp(): return lax.ppermute(array, 'grp', [(i, i ^ b) for i in range(groups)])  12 us
    pallas_call x4, Pallas kernels, attend(): pl.pallas_call(functools.partial(blocks_kernel, loop_size, tuple(served),...  7.54 us
    ppermute x5, starting transfers between devices, over_grp(): return lax.ppermute(array, 'grp', [(i, i ^ b) for i in range(groups)])  6.8 us
    ppermute x6, starting transfers between devices, flipped(): lax.ppermute(array, 'loop', [(i, i ^ bits) for i in range(loop_size)])  4.85 us
    ppermute x6, waiting for transfers between devices, flipped(): lax.ppermute(array, 'loop', [(i, i ^ bits) for i in range(loop_size)])  2.88 us
    unnamed x18, local copies, waits for them, and re-layouts  2.81 us
    pallas_call x1, Pallas kernels, shards(): pl.pallas_call(functools.partial(prep_kernel, groups), out_shape=[tile_sh...  2.38 us
    pallas_call x1, Pallas kernels, shards(): pl.pallas_call(functools.partial(finish_kernel, groups), out_shape=jax.Sh...  1.37 us
  transfers between devices with their start and end apart: 11, of which 8 were waited for; matrix products, arithmetic and copies ran while one was open for 0% of the time, Pallas kernels for 23%

profile of v5, /device:TPU:0, one launch (start us, length us, event | category | flops | bytes accessed | tf_op | source)
XLA Modules:
  0.0 43.4 jit_solution(4127534284271672918)
XLA Ops:
  0.0 2.4 %prep.1 = (bf16[256,1024]{1,0:T(8,128)(2,1)}, bf16[192,1024]{1,0:T(8,128)(2,1)}, bf16[192,1024]{1,0:T(8,128)(2,1)}, bf16[272,512]{1,0:T(8,128)(2,1)}) custom-call(bf16[256,512]{1,0:T(8,128)(2,1)} %k_hbm.1, bf16[256,512]{1,0:T(8,128)(2,1)} %v_hbm.1, s32[3,256]{1,0:T(4,128)} %order_ref.5), custom_call_target="tpu_custom_call" | custom-call | tf_op jit(solution)/shard_map/prep/pallas_call | solution.py:270
  2.4 4.1 %collective-permute-start = (bf16[272,512]{1,0:T(8,128)(2,1)}, bf16[272,512]{1,0:T(8,128)(2,1)S(1)}, u32[]{:S(2)}, u32[]{:S(2)}) collective-permute-start(bf16[272,512]{1,0:T(8,128)(2,1)} %get-tuple-element.45), channel_id=1, source_target_pairs={{0,2},{1,3},{2,0},{3,1},{4,6},{5,7},{6,4},{7,5},{8,10},{9,11},{10,... | collective-permute-start | bytes 835592 | tf_op jit(solution)/shard_map/ppermute | solution.py:283
  6.5 0.7 %collective-permute-start.3 = (bf16[256,1024]{1,0:T(8,128)(2,1)}, bf16[256,1024]{1,0:T(8,128)(2,1)S(1)}, u32[]{:S(2)}, u32[]{:S(2)}) collective-permute-start(bf16[256,1024]{1,0:T(8,128)(2,1)} %get-tuple-element.46.refs_0_), channel_id=1, source_target_pairs={{0,20},{4,16},{8,28},{12,24},{16,4},{20,0},{24,12},{28,8},{1,21},{... | collective-permute-start | bytes 1572872 | tf_op jit(solution)/shard_map/ppermute | solution.py:286
  7.2 1.5 %collective-permute-start.4 = (bf16[256,1024]{1,0:T(8,128)(2,1)}, bf16[256,1024]{1,0:T(8,128)(2,1)S(1)}, u32[]{:S(2)}, u32[]{:S(2)}) collective-permute-start(bf16[256,1024]{1,0:T(8,128)(2,1)} %get-tuple-element.46.refs_0_), channel_id=1, source_target_pairs={{0,8},{4,12},{8,0},{12,4},{16,24},{20,28},{24,16},{28,20},{1,9},{5... | collective-permute-start | bytes 1572872 | tf_op jit(solution)/shard_map/ppermute | solution.py:286
  8.7 0.7 %collective-permute-start.5 = (bf16[256,1024]{1,0:T(8,128)(2,1)}, bf16[256,1024]{1,0:T(8,128)(2,1)S(1)}, u32[]{:S(2)}, u32[]{:S(2)}) collective-permute-start(bf16[256,1024]{1,0:T(8,128)(2,1)} %get-tuple-element.46.refs_0_), channel_id=1, source_target_pairs={{0,4},{4,0},{8,12},{12,8},{16,20},{20,16},{24,28},{28,24},{1,5},{5... | collective-permute-start | bytes 1572872 | tf_op jit(solution)/shard_map/ppermute | solution.py:286
  9.3 1.6 %collective-permute-start.2 = (bf16[192,1024]{1,0:T(8,128)(2,1)}, bf16[192,1024]{1,0:T(8,128)(2,1)S(1)}, u32[]{:S(2)}, u32[]{:S(2)}) collective-permute-start(bf16[192,1024]{1,0:T(8,128)(2,1)} %get-tuple-element.52), channel_id=1, source_target_pairs={{0,1},{1,0},{2,3},{3,2},{4,5},{5,4},{6,7},{7,6},{8,9},{9,8},{10,11... | collective-permute-start | bytes 1179656 | tf_op jit(solution)/shard_map/ppermute | solution.py:283
  10.9 0.0 copy-start.1
  10.9 0.9 %copy-done.1 = bf16[256,512]{1,0:T(8,128)(2,1)S(1)} copy-done((bf16[256,512]{1,0:T(8,128)(2,1)S(1)}, bf16[256,512]{1,0:T(8,128)(2,1)}, u32[]{:S(2)}) %copy-start.1) | copy-done | bytes 262168
  11.9 0.0 copy-start.3
  11.9 1.0 %copy-done.3 = bf16[256,1024]{1,0:T(8,128)(2,1)S(1)} copy-done((bf16[256,1024]{1,0:T(8,128)(2,1)S(1)}, bf16[256,1024]{1,0:T(8,128)(2,1)}, u32[]{:S(2)}) %copy-start.3) | copy-done | bytes 524312
  12.9 0.0 copy-start.6
  12.9 0.7 %copy-done.6 = s32[1,4]{1,0:T(1,128)S(1)} copy-done((s32[1,4]{1,0:T(1,128)S(1)}, s32[1,4]{1,0:T(1,128)}, u32[]{:S(2)}) %copy-start.6) | copy-done | bytes 40
  13.6 1.9 %blocks0.1 = (f32[512,256]{1,0:T(8,128)S(1)}, f32[16,256]{1,0:T(8,128)S(1)}, bf16[4,128,512]{2,1,0:T(8,128)(2,1)S(1)}) custom-call(s32[1,4]{1,0:T(1,128)S(1)} %copy-done.6, bf16[256,1024]{1,0:T(8,128)(2,1)S(1)} %copy-done.3, bf16[256,512]{1,0:T(8,128)(2,1)S(1)} %copy-done.1), custom_call_target="tpu_custom_call" | custom-call | flops 1000 | bytes 1000 | tf_op jit(solution)/shard_map/blocks0/pallas_call | solution.py:299
  15.4 4.0 %collective-permute-done.order_ref.rows_ref = bf16[272,512]{1,0:T(8,128)(2,1)S(1)} collective-permute-done((bf16[272,512]{1,0:T(8,128)(2,1)}, bf16[272,512]{1,0:T(8,128)(2,1)S(1)}, u32[]{:S(2)}, u32[]{:S(2)}) %collective-permute-start) | collective-permute-done | bytes 278560 | tf_op jit(solution)/shard_map/ppermute | solution.py:283
  19.4 0.0 copy-start.7
  19.4 0.0 collective-permute-start.1
  19.4 0.3 relay_keys.1
  19.7 1.1 %collective-permute-done.3.refs_2_ = bf16[256,1024]{1,0:T(8,128)(2,1)S(1)} collective-permute-done((bf16[256,1024]{1,0:T(8,128)(2,1)}, bf16[256,1024]{1,0:T(8,128)(2,1)S(1)}, u32[]{:S(2)}, u32[]{:S(2)}) %collective-permute-start.3) | collective-permute-done | bytes 524320 | tf_op jit(solution)/shard_map/ppermute | solution.py:286
  20.9 1.3 %collective-permute-done.4.refs_1_ = bf16[256,1024]{1,0:T(8,128)(2,1)S(1)} collective-permute-done((bf16[256,1024]{1,0:T(8,128)(2,1)}, bf16[256,1024]{1,0:T(8,128)(2,1)S(1)}, u32[]{:S(2)}, u32[]{:S(2)}) %collective-permute-start.4) | collective-permute-done | bytes 524320 | tf_op jit(solution)/shard_map/ppermute | solution.py:286
  22.2 0.0 collective-permute-done.5.refs_0_
  22.2 0.1 collective-permute-start.10
  22.3 0.4 collective-permute-start.8
  22.7 1.5 %collective-permute-start.9 = (bf16[256,1024]{1,0:T(8,128)(2,1)S(1)}, bf16[256,1024]{1,0:T(8,128)(2,1)S(1)}, u32[]{:S(2)}, u32[]{:S(2)}) collective-permute-start(bf16[256,1024]{1,0:T(8,128)(2,1)S(1)} %collective-permute-done.3.refs_2_), channel_id=1, source_target_pairs={{0,8},{4,12},{8,0},{12,4},{16,24},{20,28},{24,16},{28,20},{1,9},{5... | collective-permute-start | bytes 1572872 | tf_op jit(solution)/shard_map/ppermute | solution.py:286
  24.2 0.0 copy-done.7
  24.2 1.9 %blocks1_2_4.1 = (f32[512,256]{1,0:T(8,128)S(1)}, f32[16,256]{1,0:T(8,128)S(1)}) custom-call(s32[1,4]{1,0:T(1,128)S(1)} %copy-done.7, bf16[256,1024]{1,0:T(8,128)(2,1)S(1)} %collective-permute-done.5.refs_0_, bf16[256,1024]{1,0:T(8,128)(2,1)S(1)} %collective-permute-done.4.refs_1_, ...), custom_call_target="tpu_custom_call", output_to_operand_aliasing={{0}: (5, {}), {1}: (6, {})} | custom-call | flops 1000 | bytes 1000 | tf_op jit(solution)/shard_map/blocks1_2_4/pallas_call | solution.py:299
  26.0 1.0 %collective-permute-done.2.refs_1_ = bf16[192,1024]{1,0:T(8,128)(2,1)S(1)} collective-permute-done((bf16[192,1024]{1,0:T(8,128)(2,1)}, bf16[192,1024]{1,0:T(8,128)(2,1)S(1)}, u32[]{:S(2)}, u32[]{:S(2)}) %collective-permute-start.2) | collective-permute-done | bytes 393248 | tf_op jit(solution)/shard_map/ppermute | solution.py:283
  27.1 0.9 %collective-permute-start.7 = (bf16[192,512]{1,0:T(8,128)(2,1)S(1)}, bf16[192,512]{1,0:T(8,128)(2,1)S(1)}, u32[]{:S(2)}, u32[]{:S(2)}) collective-permute-start(bf16[192,512]{1,0:T(8,128)(2,1)S(1)} %get-tuple-element.68), channel_id=1, source_target_pairs={{0,1},{1,0},{2,3},{3,2},{4,5},{5,4},{6,7},{7,6},{8,9},{9,8},{10,11... | collective-permute-start | bytes 589832 | tf_op jit(solution)/shard_map/ppermute | solution.py:283
  27.9 5.8 %collective-permute-done.1.rows_ref = bf16[256,512]{1,0:T(8,128)(2,1)S(1)} collective-permute-done((bf16[256,512]{1,0:T(8,128)(2,1)}, bf16[256,512]{1,0:T(8,128)(2,1)S(1)}, u32[]{:S(2)}, u32[]{:S(2)}) %collective-permute-start.1) | collective-permute-done | bytes 262176 | tf_op jit(solution)/shard_map/ppermute | solution.py:283
  33.7 0.0 copy-start.8
  33.7 0.3 relay_vals.1
  34.0 0.2 collective-permute-start.6
  34.3 0.1 copy-done.8
  34.4 0.0 copy-start
  34.4 0.0 copy-start.2
  34.4 0.0 copy-start.5
  34.5 0.0 collective-permute-done.10.refs_0_
  34.5 1.8 %blocks3.1 = (f32[512,256]{1,0:T(8,128)S(1)}, f32[16,256]{1,0:T(8,128)S(1)}) custom-call(s32[1,4]{1,0:T(1,128)S(1)} %copy-done.7, bf16[256,1024]{1,0:T(8,128)(2,1)S(1)} %collective-permute-done.10.refs_0_, bf16[4,128,512]{2,1,0:T(8,128)(2,1)S(1)} %get-tuple-element.69.refs_3_.refs_1_.refs_2_, ...), custom_call_target="tpu_custom_call", output_to_operand_aliasing={{0}: (3, {}), {1}: (4, {})} | custom-call | flops 1000 | bytes 1000 | tf_op jit(solution)/shard_map/blocks3/pallas_call | solution.py:299
  36.3 0.2 collective-permute-done.8.refs_0_
  36.5 0.2 collective-permute-done.9.refs_1_
  36.7 2.0 %blocks5_6.1 = (f32[256,512]{1,0:T(8,128)S(1)}, f32[256,128]{1,0:T(8,128)S(1)}) custom-call(s32[1,4]{1,0:T(1,128)S(1)} %copy-done.7, bf16[256,1024]{1,0:T(8,128)(2,1)S(1)} %collective-permute-done.8.refs_0_, bf16[256,1024]{1,0:T(8,128)(2,1)S(1)} %collective-permute-done.9.refs_1_, bf16[4,128,512]{2,1,0:T(8,128)(2,1)S(1)} %get-tuple-element.69.refs_3_.refs_1_.refs_2_, ...), custom_call_target="tpu_custom_call" | custom-call | flops 1000 | bytes 1000 | tf_op jit(solution)/shard_map/blocks5_6/pallas_call | solution.py:299
  38.8 0.0 collective-permute-done.7.refs_3_
  38.8 0.0 copy-done
  38.8 0.0 copy-done.2
  38.8 0.0 copy-done.5
  38.8 0.0 copy-start.4
  38.8 1.0 %score.1.score_ref = f32[3,256,128]{2,1,0:T(8,128)S(1)} custom-call(bf16[256,512]{1,0:T(8,128)(2,1)S(1)} %copy-done.2, s32[3,256]{1,0:T(4,128)S(1)} %copy-done.5, f32[3,128]{1,0:T(4,128)S(1)} %pad.4.bias_ref, bf16[192,1024]{1,0:T(8,128)(2,1)S(1)} %copy-done, bf16[192,1024]{1,0:T(8,128)(2,1)S(1)} %collective-permute-done.2.refs_1_, ...), custom_call_target="tpu_custom_call" | custom-call | flops 1000 | bytes 1000 | tf_op jit(solution)/shard_map/score/pallas_call | solution.py:321
  39.8 1.1 %weigh.1 = (f32[256,512]{1,0:T(8,128)S(1)}, f32[3,256,512]{2,1,0:T(8,128)S(1)}) custom-call(s32[3,256]{1,0:T(4,128)S(1)} %copy-done.5, f32[256,512]{1,0:T(8,128)S(1)} %get-tuple-element.76.acc_ref, f32[256,128]{1,0:T(8,128)S(1)} %get-tuple-element.77.stat_ref, f32[3,256,128]{2,1,0:T(8,128)S(1)} %score.1.score_ref, bf16[192,1024]{1,0:T(8,128)(2,1)S(1)} %copy-done, ...), custom_call_target="tpu_custom_call" | custom-call | flops 1000 | bytes 1000 | tf_op jit(solution)/shard_map/weigh/pallas_call | solution.py:378
  40.9 1.2 %collective-permute-done.6.val_ref = bf16[192,512]{1,0:T(8,128)(2,1)S(1)} collective-permute-done((bf16[192,512]{1,0:T(8,128)(2,1)S(1)}, bf16[192,512]{1,0:T(8,128)(2,1)S(1)}, u32[]{:S(2)}, u32[]{:S(2)}) %collective-permute-start.6) | collective-permute-done | bytes 196640 | tf_op jit(solution)/shard_map/ppermute | solution.py:283
  42.1 0.0 copy-done.4
  42.1 1.4 %finish.1 = bf16[256,512]{1,0:T(8,128)(2,1)} custom-call(bf16[192,512]{1,0:T(8,128)(2,1)S(1)} %collective-permute-done.6.val_ref, s32[3,256]{1,0:T(4,128)S(1)} %copy-done.5, f32[256,512]{1,0:T(8,128)S(1)} %get-tuple-element.83.part_ref, f32[3,256,512]{2,1,0:T(8,128)S(1)} %get-tuple-element.84.edge_ref, bf16[512,512]{1,0:T(8,128)(2,1)S(1)} %copy-done.4), custom_call_target="tpu_custom_call" | custom-call | flops 1000 | bytes 1000 | tf_op jit(solution)/shard_map/finish/pallas_call | solution.py:390
  (1 shorter events, 0.0 us)
Async XLA Ops:
  2.4 17.0 %collective-permute-start = (bf16[272,512]{1,0:T(8,128)(2,1)}, bf16[272,512]{1,0:T(8,128)(2,1)S(1)}, u32[]{:S(2)}, u32[]{:S(2)}) collective-permute-start(bf16[272,512]{1,0:T(8,128)(2,1)} %get-tuple-element.45), channel_id=1, source_target_pairs={{0,2},{1,3},{2,0},{3,1},{4,6},{5,7},{6,4},{7,5},{8,10},{9,11},{10,... | collective-permute-start | bytes 835592 | tf_op jit(solution)/shard_map/ppermute | solution.py:283
  6.5 14.4 %collective-permute-start.3 = (bf16[256,1024]{1,0:T(8,128)(2,1)}, bf16[256,1024]{1,0:T(8,128)(2,1)S(1)}, u32[]{:S(2)}, u32[]{:S(2)}) collective-permute-start(bf16[256,1024]{1,0:T(8,128)(2,1)} %get-tuple-element.46.refs_0_), channel_id=1, source_target_pairs={{0,20},{4,16},{8,28},{12,24},{16,4},{20,0},{24,12},{28,8},{1,21},{... | collective-permute-start | bytes 1572872 | tf_op jit(solution)/shard_map/ppermute | solution.py:286
  7.2 15.0 %collective-permute-start.4 = (bf16[256,1024]{1,0:T(8,128)(2,1)}, bf16[256,1024]{1,0:T(8,128)(2,1)S(1)}, u32[]{:S(2)}, u32[]{:S(2)}) collective-permute-start(bf16[256,1024]{1,0:T(8,128)(2,1)} %get-tuple-element.46.refs_0_), channel_id=1, source_target_pairs={{0,8},{4,12},{8,0},{12,4},{16,24},{20,28},{24,16},{28,20},{1,9},{5... | collective-permute-start | bytes 1572872 | tf_op jit(solution)/shard_map/ppermute | solution.py:286
  8.7 13.5 %collective-permute-start.5 = (bf16[256,1024]{1,0:T(8,128)(2,1)}, bf16[256,1024]{1,0:T(8,128)(2,1)S(1)}, u32[]{:S(2)}, u32[]{:S(2)}) collective-permute-start(bf16[256,1024]{1,0:T(8,128)(2,1)} %get-tuple-element.46.refs_0_), channel_id=1, source_target_pairs={{0,4},{4,0},{8,12},{12,8},{16,20},{20,16},{24,28},{28,24},{1,5},{5... | collective-permute-start | bytes 1572872 | tf_op jit(solution)/shard_map/ppermute | solution.py:286
  9.3 17.7 %collective-permute-start.2 = (bf16[192,1024]{1,0:T(8,128)(2,1)}, bf16[192,1024]{1,0:T(8,128)(2,1)S(1)}, u32[]{:S(2)}, u32[]{:S(2)}) collective-permute-start(bf16[192,1024]{1,0:T(8,128)(2,1)} %get-tuple-element.52), channel_id=1, source_target_pairs={{0,1},{1,0},{2,3},{3,2},{4,5},{5,4},{6,7},{7,6},{8,9},{9,8},{10,11... | collective-permute-start | bytes 1179656 | tf_op jit(solution)/shard_map/ppermute | solution.py:283
  10.9 0.9 %copy-start.1 = (bf16[256,512]{1,0:T(8,128)(2,1)S(1)}, bf16[256,512]{1,0:T(8,128)(2,1)}, u32[]{:S(2)}) copy-start(bf16[256,512]{1,0:T(8,128)(2,1)} %q_ref.1) | copy-start | bytes 786436
  11.9 1.0 %copy-start.3 = (bf16[256,1024]{1,0:T(8,128)(2,1)S(1)}, bf16[256,1024]{1,0:T(8,128)(2,1)}, u32[]{:S(2)}) copy-start(bf16[256,1024]{1,0:T(8,128)(2,1)} %get-tuple-element.46.refs_0_) | copy-start | bytes 1572868
  12.9 0.7 %copy-start.6 = (s32[1,4]{1,0:T(1,128)S(1)}, s32[1,4]{1,0:T(1,128)}, u32[]{:S(2)}) copy-start(s32[1,4]{1,0:T(1,128)} %tiles_ref.7) | copy-start | bytes 52
  19.4 4.7 %copy-start.7 = (s32[1,4]{1,0:T(1,128)S(1)}, s32[1,4]{1,0:T(1,128)}, u32[]{:S(2)}) copy-start(s32[1,4]{1,0:T(1,128)} %tiles_ref.7) | copy-start | bytes 52
  19.4 14.3 %collective-permute-start.1 = (bf16[256,512]{1,0:T(8,128)(2,1)}, bf16[256,512]{1,0:T(8,128)(2,1)S(1)}, u32[]{:S(2)}, u32[]{:S(2)}) collective-permute-start(bf16[256,512]{1,0:T(8,128)(2,1)} %v_hbm.1), channel_id=1, source_target_pairs={{0,2},{1,3},{2,0},{3,1},{4,6},{5,7},{6,4},{7,5},{8,10},{9,11},{10,... | collective-permute-start | bytes 786440 | tf_op jit(solution)/shard_map/ppermute | solution.py:283
  22.2 12.3 %collective-permute-start.10 = (bf16[256,1024]{1,0:T(8,128)(2,1)S(1)}, bf16[256,1024]{1,0:T(8,128)(2,1)S(1)}, u32[]{:S(2)}, u32[]{:S(2)}) collective-permute-start(bf16[256,1024]{1,0:T(8,128)(2,1)S(1)} %collective-permute-done.4.refs_1_), channel_id=1, source_target_pairs={{0,4},{4,0},{8,12},{12,8},{16,20},{20,16},{24,28},{28,24},{1,5},{5... | collective-permute-start | bytes 1572872 | tf_op jit(solution)/shard_map/ppermute | solution.py:286
  22.3 14.3 %collective-permute-start.8 = (bf16[256,1024]{1,0:T(8,128)(2,1)S(1)}, bf16[256,1024]{1,0:T(8,128)(2,1)S(1)}, u32[]{:S(2)}, u32[]{:S(2)}) collective-permute-start(bf16[256,1024]{1,0:T(8,128)(2,1)S(1)} %collective-permute-done.4.refs_1_), channel_id=1, source_target_pairs={{0,16},{4,20},{8,24},{12,28},{16,0},{20,4},{24,8},{28,12},{1,17},{... | collective-permute-start | bytes 1572872 | tf_op jit(solution)/shard_map/ppermute | solution.py:286
  22.7 14.1 %collective-permute-start.9 = (bf16[256,1024]{1,0:T(8,128)(2,1)S(1)}, bf16[256,1024]{1,0:T(8,128)(2,1)S(1)}, u32[]{:S(2)}, u32[]{:S(2)}) collective-permute-start(bf16[256,1024]{1,0:T(8,128)(2,1)S(1)} %collective-permute-done.3.refs_2_), channel_id=1, source_target_pairs={{0,8},{4,12},{8,0},{12,4},{16,24},{20,28},{24,16},{28,20},{1,9},{5... | collective-permute-start | bytes 1572872 | tf_op jit(solution)/shard_map/ppermute | solution.py:286
  27.1 11.7 %collective-permute-start.7 = (bf16[192,512]{1,0:T(8,128)(2,1)S(1)}, bf16[192,512]{1,0:T(8,128)(2,1)S(1)}, u32[]{:S(2)}, u32[]{:S(2)}) collective-permute-start(bf16[192,512]{1,0:T(8,128)(2,1)S(1)} %get-tuple-element.68), channel_id=1, source_target_pairs={{0,1},{1,0},{2,3},{3,2},{4,5},{5,4},{6,7},{7,6},{8,9},{9,8},{10,11... | collective-permute-start | bytes 589832 | tf_op jit(solution)/shard_map/ppermute | solution.py:283
  33.7 0.7 %copy-start.8 = (f32[3,8]{1,0:T(4,128)S(1)}, f32[3,8]{1,0:T(4,128)}, u32[]{:S(2)}) copy-start(f32[3,8]{1,0:T(4,128)} %param.13) | copy-start | bytes 292
  34.0 8.0 %collective-permute-start.6 = (bf16[192,512]{1,0:T(8,128)(2,1)S(1)}, bf16[192,512]{1,0:T(8,128)(2,1)S(1)}, u32[]{:S(2)}, u32[]{:S(2)}) collective-permute-start(bf16[192,512]{1,0:T(8,128)(2,1)S(1)} %get-tuple-element.67), channel_id=1, source_target_pairs={{0,1},{1,0},{2,3},{3,2},{4,5},{5,4},{6,7},{7,6},{8,9},{9,8},{10,11... | collective-permute-start | bytes 589832 | tf_op jit(solution)/shard_map/ppermute | solution.py:283
  34.4 4.3 %copy-start = (bf16[192,1024]{1,0:T(8,128)(2,1)S(1)}, bf16[192,1024]{1,0:T(8,128)(2,1)}, u32[]{:S(2)}) copy-start(bf16[192,1024]{1,0:T(8,128)(2,1)} %get-tuple-element.78.refs_0_) | copy-start | bytes 1179652
  34.4 4.4 %copy-start.2 = (bf16[256,512]{1,0:T(8,128)(2,1)S(1)}, bf16[256,512]{1,0:T(8,128)(2,1)}, u32[]{:S(2)}) copy-start(bf16[256,512]{1,0:T(8,128)(2,1)} %q_ref.1) | copy-start | bytes 786436
  34.4 4.4 %copy-start.5 = (s32[3,256]{1,0:T(4,128)S(1)}, s32[3,256]{1,0:T(4,128)}, u32[]{:S(2)}) copy-start(s32[3,256]{1,0:T(4,128)} %order_ref.5) | copy-start | bytes 9220
  38.8 3.3 %copy-start.4 = (bf16[512,512]{1,0:T(8,128)(2,1)S(1)}, bf16[512,512]{1,0:T(8,128)(2,1)}, u32[]{:S(2)}) copy-start(bf16[512,512]{1,0:T(8,128)(2,1)} %w_ref.1) | copy-start | bytes 1572868

commit v6 on v5

--- a/solution.py
+++ b/solution.py
@@ -276,8 +276,9 @@
             pltpu.VMEM(expander_order.shape, jnp.int32),
             pltpu.SemaphoreType.DMA((3,)),
         ],
+        compiler_params=params,
         name="prep",
-    )(key_rows, value_rows, expander_order)
+    )(*[pltpu.with_memory_space_constraint(x, pltpu.HBM) for x in (key_rows, value_rows, expander_order)])
 
     def over_grp(array, b):
         return lax.ppermute(array, "grp", [(i, i ^ b) for i in range(groups)])

time: 43.7 us -> 42.5 us (0.973)
  local copies, waits for them, and re-layouts: 2.81 us -> 1.75 us
  starting transfers between devices: 11.7 us -> 12.7 us
  Pallas kernels: 13.9 us -> 13 us
    unnamed x18 -> x10, local copies, waits for them, and re-layouts: 2.81 us -> 1.74 us
    ppermute x5, starting transfers between devices: 6.8 us -> 7.83 us  [over_grp(): return lax.ppermute(array, 'grp', [(i, i ^ b) for i in range(groups)])]
    pallas_call x1, Pallas kernels: 2.38 us -> 1.46 us  [shards(): pl.pallas_call(functools.partial(prep_kernel, groups), out_shape=[tile_sh...]
  transfers between devices with their start and end apart: 11 -> 11, of which waited for: 8 -> 8; matrix products, arithmetic and copies ran while one was open for 0% -> 0% of each run, Pallas kernels for 23% -> 24%
where the time goes in v6:
time: 42.5 us; the launch traced here: 42.3 us
  waiting for transfers between devices  14.7 us (35%)
  Pallas kernels  13 us (31%)
  starting transfers between devices  12.7 us (30%)
  local copies, waits for them, and re-layouts  1.75 us (4%)
    ppermute x5, waiting for transfers between devices, over_grp(): return lax.ppermute(array, 'grp', [(i, i ^ b) for i in range(groups)])  11.8 us
    ppermute x5, starting transfers between devices, over_grp(): return lax.ppermute(array, 'grp', [(i, i ^ b) for i in range(groups)])  7.83 us
    pallas_call x4, Pallas kernels, attend(): pl.pallas_call(functools.partial(blocks_kernel, loop_size, tuple(served),...  7.53 us
    ppermute x6, starting transfers between devices, flipped(): lax.ppermute(array, 'loop', [(i, i ^ bits) for i in range(loop_size)])  4.85 us
    ppermute x6, waiting for transfers between devices, flipped(): lax.ppermute(array, 'loop', [(i, i ^ bits) for i in range(loop_size)])  2.92 us
    unnamed x10, local copies, waits for them, and re-layouts  1.74 us
    pallas_call x1, Pallas kernels, shards(): pl.pallas_call(functools.partial(prep_kernel, groups), out_shape=[tile_sh...  1.46 us
    pallas_call x1, Pallas kernels, shards(): pl.pallas_call(functools.partial(finish_kernel, groups), out_shape=jax.Sh...  1.38 us
  transfers between devices with their start and end apart: 11, of which 8 were waited for; matrix products, arithmetic and copies ran while one was open for 0% of the time, Pallas kernels for 24%

profile of v6, /device:TPU:0, one launch (start us, length us, event | category | flops | bytes accessed | tf_op | source)
XLA Modules:
  0.0 42.3 jit_solution(1195673965926969098)
XLA Ops:
  0.0 1.5 %prep.1 = (bf16[256,1024]{1,0:T(8,128)(2,1)S(1)}, bf16[192,1024]{1,0:T(8,128)(2,1)S(1)}, bf16[192,1024]{1,0:T(8,128)(2,1)S(1)}, bf16[272,512]{1,0:T(8,128)(2,1)S(1)}) custom-call(bf16[256,512]{1,0:T(8,128)(2,1)} %k_hbm.1, bf16[256,512]{1,0:T(8,128)(2,1)} %v_hbm.1, s32[3,256]{1,0:T(4,128)} %order_ref.5), custom_call_target="tpu_custom_call" | custom-call | tf_op jit(solution)/shard_map/prep/pallas_call | solution.py:270
  1.5 4.1 %collective-permute-start = (bf16[272,512]{1,0:T(8,128)(2,1)S(1)}, bf16[272,512]{1,0:T(8,128)(2,1)S(1)}, u32[]{:S(2)}, u32[]{:S(2)}) collective-permute-start(bf16[272,512]{1,0:T(8,128)(2,1)S(1)} %get-tuple-element.45), channel_id=1, source_target_pairs={{0,2},{1,3},{2,0},{3,1},{4,6},{5,7},{6,4},{7,5},{8,10},{9,11},{10,... | collective-permute-start | bytes 835592 | tf_op jit(solution)/shard_map/ppermute | solution.py:284
  5.6 0.7 %collective-permute-start.3 = (bf16[256,1024]{1,0:T(8,128)(2,1)S(1)}, bf16[256,1024]{1,0:T(8,128)(2,1)S(1)}, u32[]{:S(2)}, u32[]{:S(2)}) collective-permute-start(bf16[256,1024]{1,0:T(8,128)(2,1)S(1)} %get-tuple-element.46.refs_0_), channel_id=1, source_target_pairs={{0,20},{4,16},{8,28},{12,24},{16,4},{20,0},{24,12},{28,8},{1,21},{... | collective-permute-start | bytes 1572872 | tf_op jit(solution)/shard_map/ppermute | solution.py:287
  6.3 1.5 %collective-permute-start.4 = (bf16[256,1024]{1,0:T(8,128)(2,1)S(1)}, bf16[256,1024]{1,0:T(8,128)(2,1)S(1)}, u32[]{:S(2)}, u32[]{:S(2)}) collective-permute-start(bf16[256,1024]{1,0:T(8,128)(2,1)S(1)} %get-tuple-element.46.refs_0_), channel_id=1, source_target_pairs={{0,8},{4,12},{8,0},{12,4},{16,24},{20,28},{24,16},{28,20},{1,9},{5... | collective-permute-start | bytes 1572872 | tf_op jit(solution)/shard_map/ppermute | solution.py:287
  7.7 0.7 %collective-permute-start.5 = (bf16[256,1024]{1,0:T(8,128)(2,1)S(1)}, bf16[256,1024]{1,0:T(8,128)(2,1)S(1)}, u32[]{:S(2)}, u32[]{:S(2)}) collective-permute-start(bf16[256,1024]{1,0:T(8,128)(2,1)S(1)} %get-tuple-element.46.refs_0_), channel_id=1, source_target_pairs={{0,4},{4,0},{8,12},{12,8},{16,20},{20,16},{24,28},{28,24},{1,5},{5... | collective-permute-start | bytes 1572872 | tf_op jit(solution)/shard_map/ppermute | solution.py:287
  8.4 1.6 %collective-permute-start.2 = (bf16[192,1024]{1,0:T(8,128)(2,1)S(1)}, bf16[192,1024]{1,0:T(8,128)(2,1)S(1)}, u32[]{:S(2)}, u32[]{:S(2)}) collective-permute-start(bf16[192,1024]{1,0:T(8,128)(2,1)S(1)} %get-tuple-element.52), channel_id=1, source_target_pairs={{0,1},{1,0},{2,3},{3,2},{4,5},{5,4},{6,7},{7,6},{8,9},{9,8},{10,11... | collective-permute-start | bytes 1179656 | tf_op jit(solution)/shard_map/ppermute | solution.py:284
  10.0 0.0 copy-start
  10.0 0.9 %copy-done = bf16[256,512]{1,0:T(8,128)(2,1)S(1)} copy-done((bf16[256,512]{1,0:T(8,128)(2,1)S(1)}, bf16[256,512]{1,0:T(8,128)(2,1)}, u32[]{:S(2)}) %copy-start) | copy-done | bytes 262168
  10.9 0.0 copy-start.3
  11.0 0.7 %copy-done.3 = s32[1,4]{1,0:T(1,128)S(1)} copy-done((s32[1,4]{1,0:T(1,128)S(1)}, s32[1,4]{1,0:T(1,128)}, u32[]{:S(2)}) %copy-start.3) | copy-done | bytes 40
  11.6 1.9 %blocks0.1 = (f32[512,256]{1,0:T(8,128)S(1)}, f32[16,256]{1,0:T(8,128)S(1)}, bf16[4,128,512]{2,1,0:T(8,128)(2,1)S(1)}) custom-call(s32[1,4]{1,0:T(1,128)S(1)} %copy-done.3, bf16[256,1024]{1,0:T(8,128)(2,1)S(1)} %get-tuple-element.46.refs_0_, bf16[256,512]{1,0:T(8,128)(2,1)S(1)} %copy-done), custom_call_target="tpu_custom_call" | custom-call | flops 1000 | bytes 1000 | tf_op jit(solution)/shard_map/blocks0/pallas_call | solution.py:300
  13.5 4.8 %collective-permute-done.order_ref.rows_ref = bf16[272,512]{1,0:T(8,128)(2,1)S(1)} collective-permute-done((bf16[272,512]{1,0:T(8,128)(2,1)S(1)}, bf16[272,512]{1,0:T(8,128)(2,1)S(1)}, u32[]{:S(2)}, u32[]{:S(2)}) %collective-permute-start) | collective-permute-done | bytes 278560 | tf_op jit(solution)/shard_map/ppermute | solution.py:284
  18.3 0.0 collective-permute-start.1
  18.3 0.3 relay_keys.1
  18.6 1.1 %collective-permute-done.3.refs_2_ = bf16[256,1024]{1,0:T(8,128)(2,1)S(1)} collective-permute-done((bf16[256,1024]{1,0:T(8,128)(2,1)S(1)}, bf16[256,1024]{1,0:T(8,128)(2,1)S(1)}, u32[]{:S(2)}, u32[]{:S(2)}) %collective-permute-start.3) | collective-permute-done | bytes 524320 | tf_op jit(solution)/shard_map/ppermute | solution.py:287
  19.7 1.3 %collective-permute-done.4.refs_1_ = bf16[256,1024]{1,0:T(8,128)(2,1)S(1)} collective-permute-done((bf16[256,1024]{1,0:T(8,128)(2,1)S(1)}, bf16[256,1024]{1,0:T(8,128)(2,1)S(1)}, u32[]{:S(2)}, u32[]{:S(2)}) %collective-permute-start.4) | collective-permute-done | bytes 524320 | tf_op jit(solution)/shard_map/ppermute | solution.py:287
  21.0 0.0 collective-permute-done.5.refs_0_
  21.0 0.1 collective-permute-start.10
  21.1 0.4 collective-permute-start.8
  21.6 1.5 %collective-permute-start.9 = (bf16[256,1024]{1,0:T(8,128)(2,1)S(1)}, bf16[256,1024]{1,0:T(8,128)(2,1)S(1)}, u32[]{:S(2)}, u32[]{:S(2)}) collective-permute-start(bf16[256,1024]{1,0:T(8,128)(2,1)S(1)} %collective-permute-done.3.refs_2_), channel_id=1, source_target_pairs={{0,8},{4,12},{8,0},{12,4},{16,24},{20,28},{24,16},{28,20},{1,9},{5... | collective-permute-start | bytes 1572872 | tf_op jit(solution)/shard_map/ppermute | solution.py:287
  23.0 1.9 %blocks1_2_4.1 = (f32[512,256]{1,0:T(8,128)S(1)}, f32[16,256]{1,0:T(8,128)S(1)}) custom-call(s32[1,4]{1,0:T(1,128)S(1)} %copy-done.3, bf16[256,1024]{1,0:T(8,128)(2,1)S(1)} %collective-permute-done.5.refs_0_, bf16[256,1024]{1,0:T(8,128)(2,1)S(1)} %collective-permute-done.4.refs_1_, ...), custom_call_target="tpu_custom_call", output_to_operand_aliasing={{0}: (5, {}), {1}: (6, {})} | custom-call | flops 1000 | bytes 1000 | tf_op jit(solution)/shard_map/blocks1_2_4/pallas_call | solution.py:300
  24.9 1.0 %collective-permute-done.2.refs_1_ = bf16[192,1024]{1,0:T(8,128)(2,1)S(1)} collective-permute-done((bf16[192,1024]{1,0:T(8,128)(2,1)S(1)}, bf16[192,1024]{1,0:T(8,128)(2,1)S(1)}, u32[]{:S(2)}, u32[]{:S(2)}) %collective-permute-start.2) | collective-permute-done | bytes 393248 | tf_op jit(solution)/shard_map/ppermute | solution.py:284
  25.9 1.9 %collective-permute-start.7 = (bf16[192,512]{1,0:T(8,128)(2,1)S(1)}, bf16[192,512]{1,0:T(8,128)(2,1)S(1)}, u32[]{:S(2)}, u32[]{:S(2)}) collective-permute-start(bf16[192,512]{1,0:T(8,128)(2,1)S(1)} %get-tuple-element.68), channel_id=1, source_target_pairs={{0,1},{1,0},{2,3},{3,2},{4,5},{5,4},{6,7},{7,6},{8,9},{9,8},{10,11... | collective-permute-start | bytes 589832 | tf_op jit(solution)/shard_map/ppermute | solution.py:284
  27.8 4.8 %collective-permute-done.1.rows_ref = bf16[256,512]{1,0:T(8,128)(2,1)S(1)} collective-permute-done((bf16[256,512]{1,0:T(8,128)(2,1)}, bf16[256,512]{1,0:T(8,128)(2,1)S(1)}, u32[]{:S(2)}, u32[]{:S(2)}) %collective-permute-start.1) | collective-permute-done | bytes 262176 | tf_op jit(solution)/shard_map/ppermute | solution.py:284
  32.6 0.0 copy-start.4
  32.6 0.3 relay_vals.1
  32.9 0.3 collective-permute-start.6
  33.2 0.1 copy-done.4
  33.3 0.0 copy-start.2
  33.3 0.0 collective-permute-done.10.refs_0_
  33.3 1.8 %blocks3.1 = (f32[512,256]{1,0:T(8,128)S(1)}, f32[16,256]{1,0:T(8,128)S(1)}) custom-call(s32[1,4]{1,0:T(1,128)S(1)} %copy-done.3, bf16[256,1024]{1,0:T(8,128)(2,1)S(1)} %collective-permute-done.10.refs_0_, bf16[4,128,512]{2,1,0:T(8,128)(2,1)S(1)} %get-tuple-element.69.refs_3_.refs_1_.refs_2_, ...), custom_call_target="tpu_custom_call", output_to_operand_aliasing={{0}: (3, {}), {1}: (4, {})} | custom-call | flops 1000 | bytes 1000 | tf_op jit(solution)/shard_map/blocks3/pallas_call | solution.py:300
  35.1 0.3 collective-permute-done.8.refs_0_
  35.4 0.2 collective-permute-done.9.refs_1_
  35.6 2.0 %blocks5_6.1 = (f32[256,512]{1,0:T(8,128)S(1)}, f32[256,128]{1,0:T(8,128)S(1)}) custom-call(s32[1,4]{1,0:T(1,128)S(1)} %copy-done.3, bf16[256,1024]{1,0:T(8,128)(2,1)S(1)} %collective-permute-done.8.refs_0_, bf16[256,1024]{1,0:T(8,128)(2,1)S(1)} %collective-permute-done.9.refs_1_, bf16[4,128,512]{2,1,0:T(8,128)(2,1)S(1)} %get-tuple-element.69.refs_3_.refs_1_.refs_2_, ...), custom_call_target="tpu_custom_call" | custom-call | flops 1000 | bytes 1000 | tf_op jit(solution)/shard_map/blocks5_6/pallas_call | solution.py:300
  37.6 0.0 collective-permute-done.7.refs_3_
  37.6 0.0 copy-done.2
  37.7 0.0 copy-start.1
  37.7 1.0 %score.1.score_ref = f32[3,256,128]{2,1,0:T(8,128)S(1)} custom-call(bf16[256,512]{1,0:T(8,128)(2,1)S(1)} %copy-done, s32[3,256]{1,0:T(4,128)S(1)} %copy-done.2, f32[3,128]{1,0:T(4,128)S(1)} %pad.4.bias_ref, bf16[192,1024]{1,0:T(8,128)(2,1)S(1)} %get-tuple-element.78.refs_0_, bf16[192,1024]{1,0:T(8,128)(2,1)S(1)} %collective-permute-done.2.refs_1_, ...), custom_call_target="tpu_custom_call" | custom-call | flops 1000 | bytes 1000 | tf_op jit(solution)/shard_map/score/pallas_call | solution.py:322
  38.7 1.1 %weigh.1 = (f32[256,512]{1,0:T(8,128)S(1)}, f32[3,256,512]{2,1,0:T(8,128)S(1)}) custom-call(s32[3,256]{1,0:T(4,128)S(1)} %copy-done.2, f32[256,512]{1,0:T(8,128)S(1)} %get-tuple-element.76.acc_ref, f32[256,128]{1,0:T(8,128)S(1)} %get-tuple-element.77.stat_ref, f32[3,256,128]{2,1,0:T(8,128)S(1)} %score.1.score_ref, ...), custom_call_target="tpu_custom_call" | custom-call | flops 1000 | bytes 1000 | tf_op jit(solution)/shard_map/weigh/pallas_call | solution.py:379
  39.8 1.2 %collective-permute-done.6.val_ref = bf16[192,512]{1,0:T(8,128)(2,1)S(1)} collective-permute-done((bf16[192,512]{1,0:T(8,128)(2,1)S(1)}, bf16[192,512]{1,0:T(8,128)(2,1)S(1)}, u32[]{:S(2)}, u32[]{:S(2)}) %collective-permute-start.6) | collective-permute-done | bytes 196640 | tf_op jit(solution)/shard_map/ppermute | solution.py:284
  40.9 0.0 copy-done.1
  40.9 1.4 %finish.1 = bf16[256,512]{1,0:T(8,128)(2,1)} custom-call(bf16[192,512]{1,0:T(8,128)(2,1)S(1)} %collective-permute-done.6.val_ref, s32[3,256]{1,0:T(4,128)S(1)} %copy-done.2, f32[256,512]{1,0:T(8,128)S(1)} %get-tuple-element.83.part_ref, f32[3,256,512]{2,1,0:T(8,128)S(1)} %get-tuple-element.84.edge_ref, bf16[512,512]{1,0:T(8,128)(2,1)S(1)} %copy-done.1), custom_call_target="tpu_custom_call" | custom-call | flops 1000 | bytes 1000 | tf_op jit(solution)/shard_map/finish/pallas_call | solution.py:391
  (1 shorter events, 0.0 us)
Async XLA Ops:
  1.5 16.8 %collective-permute-start = (bf16[272,512]{1,0:T(8,128)(2,1)S(1)}, bf16[272,512]{1,0:T(8,128)(2,1)S(1)}, u32[]{:S(2)}, u32[]{:S(2)}) collective-permute-start(bf16[272,512]{1,0:T(8,128)(2,1)S(1)} %get-tuple-element.45), channel_id=1, source_target_pairs={{0,2},{1,3},{2,0},{3,1},{4,6},{5,7},{6,4},{7,5},{8,10},{9,11},{10,... | collective-permute-start | bytes 835592 | tf_op jit(solution)/shard_map/ppermute | solution.py:284
  5.6 14.2 %collective-permute-start.3 = (bf16[256,1024]{1,0:T(8,128)(2,1)S(1)}, bf16[256,1024]{1,0:T(8,128)(2,1)S(1)}, u32[]{:S(2)}, u32[]{:S(2)}) collective-permute-start(bf16[256,1024]{1,0:T(8,128)(2,1)S(1)} %get-tuple-element.46.refs_0_), channel_id=1, source_target_pairs={{0,20},{4,16},{8,28},{12,24},{16,4},{20,0},{24,12},{28,8},{1,21},{... | collective-permute-start | bytes 1572872 | tf_op jit(solution)/shard_map/ppermute | solution.py:287
  6.3 14.8 %collective-permute-start.4 = (bf16[256,1024]{1,0:T(8,128)(2,1)S(1)}, bf16[256,1024]{1,0:T(8,128)(2,1)S(1)}, u32[]{:S(2)}, u32[]{:S(2)}) collective-permute-start(bf16[256,1024]{1,0:T(8,128)(2,1)S(1)} %get-tuple-element.46.refs_0_), channel_id=1, source_target_pairs={{0,8},{4,12},{8,0},{12,4},{16,24},{20,28},{24,16},{28,20},{1,9},{5... | collective-permute-start | bytes 1572872 | tf_op jit(solution)/shard_map/ppermute | solution.py:287
  7.7 13.3 %collective-permute-start.5 = (bf16[256,1024]{1,0:T(8,128)(2,1)S(1)}, bf16[256,1024]{1,0:T(8,128)(2,1)S(1)}, u32[]{:S(2)}, u32[]{:S(2)}) collective-permute-start(bf16[256,1024]{1,0:T(8,128)(2,1)S(1)} %get-tuple-element.46.refs_0_), channel_id=1, source_target_pairs={{0,4},{4,0},{8,12},{12,8},{16,20},{20,16},{24,28},{28,24},{1,5},{5... | collective-permute-start | bytes 1572872 | tf_op jit(solution)/shard_map/ppermute | solution.py:287
  8.4 17.5 %collective-permute-start.2 = (bf16[192,1024]{1,0:T(8,128)(2,1)S(1)}, bf16[192,1024]{1,0:T(8,128)(2,1)S(1)}, u32[]{:S(2)}, u32[]{:S(2)}) collective-permute-start(bf16[192,1024]{1,0:T(8,128)(2,1)S(1)} %get-tuple-element.52), channel_id=1, source_target_pairs={{0,1},{1,0},{2,3},{3,2},{4,5},{5,4},{6,7},{7,6},{8,9},{9,8},{10,11... | collective-permute-start | bytes 1179656 | tf_op jit(solution)/shard_map/ppermute | solution.py:284
  10.0 0.9 %copy-start = (bf16[256,512]{1,0:T(8,128)(2,1)S(1)}, bf16[256,512]{1,0:T(8,128)(2,1)}, u32[]{:S(2)}) copy-start(bf16[256,512]{1,0:T(8,128)(2,1)} %q_ref.1) | copy-start | bytes 786436
  10.9 0.7 %copy-start.3 = (s32[1,4]{1,0:T(1,128)S(1)}, s32[1,4]{1,0:T(1,128)}, u32[]{:S(2)}) copy-start(s32[1,4]{1,0:T(1,128)} %tiles_ref.7) | copy-start | bytes 52
  18.3 14.3 %collective-permute-start.1 = (bf16[256,512]{1,0:T(8,128)(2,1)}, bf16[256,512]{1,0:T(8,128)(2,1)S(1)}, u32[]{:S(2)}, u32[]{:S(2)}) collective-permute-start(bf16[256,512]{1,0:T(8,128)(2,1)} %v_hbm.1), channel_id=1, source_target_pairs={{0,2},{1,3},{2,0},{3,1},{4,6},{5,7},{6,4},{7,5},{8,10},{9,11},{10,... | collective-permute-start | bytes 786440 | tf_op jit(solution)/shard_map/ppermute | solution.py:284
  21.0 12.3 %collective-permute-start.10 = (bf16[256,1024]{1,0:T(8,128)(2,1)S(1)}, bf16[256,1024]{1,0:T(8,128)(2,1)S(1)}, u32[]{:S(2)}, u32[]{:S(2)}) collective-permute-start(bf16[256,1024]{1,0:T(8,128)(2,1)S(1)} %collective-permute-done.4.refs_1_), channel_id=1, source_target_pairs={{0,4},{4,0},{8,12},{12,8},{16,20},{20,16},{24,28},{28,24},{1,5},{5... | collective-permute-start | bytes 1572872 | tf_op jit(solution)/shard_map/ppermute | solution.py:287
  21.1 14.3 %collective-permute-start.8 = (bf16[256,1024]{1,0:T(8,128)(2,1)S(1)}, bf16[256,1024]{1,0:T(8,128)(2,1)S(1)}, u32[]{:S(2)}, u32[]{:S(2)}) collective-permute-start(bf16[256,1024]{1,0:T(8,128)(2,1)S(1)} %collective-permute-done.4.refs_1_), channel_id=1, source_target_pairs={{0,16},{4,20},{8,24},{12,28},{16,0},{20,4},{24,8},{28,12},{1,17},{... | collective-permute-start | bytes 1572872 | tf_op jit(solution)/shard_map/ppermute | solution.py:287
  21.6 14.1 %collective-permute-start.9 = (bf16[256,1024]{1,0:T(8,128)(2,1)S(1)}, bf16[256,1024]{1,0:T(8,128)(2,1)S(1)}, u32[]{:S(2)}, u32[]{:S(2)}) collective-permute-start(bf16[256,1024]{1,0:T(8,128)(2,1)S(1)} %collective-permute-done.3.refs_2_), channel_id=1, source_target_pairs={{0,8},{4,12},{8,0},{12,4},{16,24},{20,28},{24,16},{28,20},{1,9},{5... | collective-permute-start | bytes 1572872 | tf_op jit(solution)/shard_map/ppermute | solution.py:287
  25.9 11.7 %collective-permute-start.7 = (bf16[192,512]{1,0:T(8,128)(2,1)S(1)}, bf16[192,512]{1,0:T(8,128)(2,1)S(1)}, u32[]{:S(2)}, u32[]{:S(2)}) collective-permute-start(bf16[192,512]{1,0:T(8,128)(2,1)S(1)} %get-tuple-element.68), channel_id=1, source_target_pairs={{0,1},{1,0},{2,3},{3,2},{4,5},{5,4},{6,7},{7,6},{8,9},{9,8},{10,11... | collective-permute-start | bytes 589832 | tf_op jit(solution)/shard_map/ppermute | solution.py:284
  32.6 0.7 %copy-start.4 = (f32[3,8]{1,0:T(4,128)S(1)}, f32[3,8]{1,0:T(4,128)}, u32[]{:S(2)}) copy-start(f32[3,8]{1,0:T(4,128)} %param.13) | copy-start | bytes 292
  32.9 8.0 %collective-permute-start.6 = (bf16[192,512]{1,0:T(8,128)(2,1)S(1)}, bf16[192,512]{1,0:T(8,128)(2,1)S(1)}, u32[]{:S(2)}, u32[]{:S(2)}) collective-permute-start(bf16[192,512]{1,0:T(8,128)(2,1)S(1)} %get-tuple-element.67), channel_id=1, source_target_pairs={{0,1},{1,0},{2,3},{3,2},{4,5},{5,4},{6,7},{7,6},{8,9},{9,8},{10,11... | collective-permute-start | bytes 589832 | tf_op jit(solution)/shard_map/ppermute | solution.py:284
  33.3 4.3 %copy-start.2 = (s32[3,256]{1,0:T(4,128)S(1)}, s32[3,256]{1,0:T(4,128)}, u32[]{:S(2)}) copy-start(s32[3,256]{1,0:T(4,128)} %order_ref.5) | copy-start | bytes 9220
  37.7 3.3 %copy-start.1 = (bf16[512,512]{1,0:T(8,128)(2,1)S(1)}, bf16[512,512]{1,0:T(8,128)(2,1)}, u32[]{:S(2)}) copy-start(bf16[512,512]{1,0:T(8,128)(2,1)} %w_ref.1) | copy-start | bytes 1572868

commit v7 on v6

--- a/solution.py
+++ b/solution.py
@@ -31,7 +31,23 @@
     return jnp.where(row_ids == order_row, 1.0, 0.0).astype(BF16)
 
 
-def prep_kernel(groups, k_hbm, v_hbm, order_hbm, tile_ref, *refs):
+def bucket_table(order, bucket, lowest, count):
+    lane = lax.broadcasted_iota(jnp.int32, order.shape, 1)
+    swapped = jnp.where(lane % 2 == 0, jnp.roll(order, -1, axis=1), jnp.roll(order, 1, axis=1))
+    wanted = jnp.where(lane < bucket, swapped, order)
+    chosen = slice(lowest * bucket, (lowest + count) * bucket)
+    tables = [place_table(wanted[j : j + 1, :], order.shape[1])[:, chosen] for j in range(MATCHINGS)]
+    return jnp.concatenate(tables, axis=1)
+
+
+def put_buckets(ordered, bucket, out_refs):
+    for j in range(MATCHINGS):
+        for i, out_ref in enumerate(out_refs):
+            first = (j * len(out_refs) + i) * bucket
+            out_ref[j * bucket : (j + 1) * bucket, :] = ordered[first : first + bucket]
+
+
+def prep_kernel(groups, lowest, k_hbm, v_hbm, order_hbm, tile_ref, *refs):
     out_refs, (order_ref, sems) = refs[:-2], refs[-2:]
     rows, width = k_hbm.shape
     bucket = rows // groups
@@ -41,13 +57,8 @@
         copy.start()
     copies[0].wait()
     order = order_ref[...]
-    lane = lax.broadcasted_iota(jnp.int32, order.shape, 1)
-    swapped = jnp.where(lane % 2 == 0, jnp.roll(order, -1, axis=1), jnp.roll(order, 1, axis=1))
-    wanted = jnp.where(lane < bucket, swapped, order)
     paired = [ref for ref in out_refs if ref.shape[1] == 2 * width]
-    n_slots = len(paired) * bucket
-    tables = [place_table(wanted[j : j + 1, :], rows)[:, :n_slots] for j in range(MATCHINGS)]
-    table = jnp.concatenate(tables, axis=1)
+    table = bucket_table(order, bucket, lowest, len(paired))
     for copy in copies[1:]:
         copy.wait()
     tile = tile_ref[...]
@@ -56,11 +67,13 @@
         padded = jnp.concatenate([order, jnp.zeros((ORDER_ROWS - MATCHINGS, rows), jnp.int32)], axis=0)
         ref[rows:, :rows] = padded.astype(F32).astype(BF16)
         ref[rows:, rows:] = jnp.zeros((ORDER_ROWS, width - rows), BF16)
-    ordered = dot(table, tile, ((0,), (0,))).astype(BF16)
-    for j in range(MATCHINGS):
-        mine = slice(j * bucket, (j + 1) * bucket)
-        for b, out_ref in enumerate(paired):
-            out_ref[mine, :] = ordered[j * n_slots + b * bucket : j * n_slots + (b + 1) * bucket]
+    put_buckets(dot(table, tile, ((0,), (0,))).astype(BF16), bucket, paired)
+
+
+def own_bucket_kernel(groups, tile_ref, order_ref, out_ref):
+    bucket = tile_ref.shape[0] // groups
+    table = bucket_table(order_ref[...], bucket, 0, 1)
+    put_buckets(dot(table, tile_ref[...], ((0,), (0,))).astype(BF16), bucket, [out_ref])
 
 
 def relay_kernel(groups, order_ref, rows_ref, mine_ref, next_ref):
@@ -232,21 +245,27 @@
 
     numer = acc_ref[...] * wide(keep * inv)
     for j in range(MATCHINGS):
-        table = place_table(order_ref[j : j + 1, :], rows)[:, : rows - bucket]
-        edge = wide(edge_w[j].astype(BF16).astype(F32) * inv)
-        edge_ref[j] = edge
-        numer = numer + edge * dot(table, rows_in_order(val_refs, j, bucket, width, width))
+        table = place_table(order_ref[j : j + 1, :], rows)
+        share = edge_w[j].astype(BF16).astype(F32) * inv
+        numer = numer + wide(share) * dot(table[:, : rows - bucket], rows_in_order(val_refs, j, bucket, width, width))
+        high = share.astype(BF16)
+        low = (share - high.astype(F32)).astype(BF16)
+        last = table[:, rows - bucket :]
+        in_order = dot(last, high, ((0,), (0,))) + dot(last, low, ((0,), (0,)))
+        edge_ref[j * bucket : (j + 1) * bucket, :] = wide(in_order)
     part_ref[...] = numer
 
 
 def finish_kernel(groups, val_ref, order_ref, part_ref, edge_ref, w_ref, out_ref):
     rows, width = part_ref.shape
     bucket = rows // groups
-    numer = part_ref[...]
-    for j in range(MATCHINGS):
-        table = place_table(order_ref[j : j + 1, :], rows)[:, rows - bucket :]
-        numer = numer + edge_ref[j] * dot(table, rows_in_order([val_ref], j, bucket, width, width))
-    out_ref[...] = dot(numer.astype(BF16), w_ref[...]).astype(BF16)
+    weighed = edge_ref[...] * val_ref[:, val_ref.shape[1] - width :].astype(F32)
+    high = weighed.astype(BF16)
+    low = (weighed - high.astype(F32)).astype(BF16)
+    tables = [place_table(order_ref[j : j + 1, :], rows)[:, rows - bucket :] for j in range(MATCHINGS)]
+    table = jnp.concatenate(tables, axis=1)
+    attended = part_ref[...] + dot(table, high) + dot(table, low)
+    out_ref[...] = dot(attended.astype(BF16), w_ref[...]).astype(BF16)
 
 
 fence = lax.optimization_barrier
@@ -266,9 +285,9 @@
     kv_shape = jax.ShapeDtypeStruct((MATCHINGS * bucket, 2 * width), BF16)
     one_shape = jax.ShapeDtypeStruct((MATCHINGS * bucket, width), BF16)
     full_shape = jax.ShapeDtypeStruct((rows + ORDER_ROWS, width), BF16)
-    bucket_shapes = [kv_shape, kv_shape, full_shape] if relayed else [kv_shape] * groups
+    bucket_shapes = [kv_shape, full_shape] if relayed else [kv_shape] * groups
     own_tile, *outgoing = pl.pallas_call(
-        functools.partial(prep_kernel, groups),
+        functools.partial(prep_kernel, groups, 1 if relayed else 0),
         out_shape=[tile_shape] + bucket_shapes,
         in_specs=[pl.BlockSpec(memory_space=pltpu.HBM)] * 3,
         out_specs=vmem_specs(1 + len(bucket_shapes)),
@@ -342,8 +361,8 @@
                 name=name,
             )(order, full)
 
-        full_k = over_grp(outgoing[2], 2)
-        near = over_grp(outgoing[1], 1)
+        full_k = over_grp(outgoing[1], 2)
+        near = over_grp(outgoing[0], 1)
         across = flipped(own_tile, 5)
         side = flipped(own_tile, 2)
         twin = flipped(own_tile, 1)
@@ -357,15 +376,24 @@
         side_twin = flipped(side, 1)
         keys_3 = over_grp(passed, 1)
         state = attend({1: twin, 2: side, 4: across}, state, False)
-        full_v, near, state = fence((full_v, near, state))
+        own_bucket = pl.pallas_call(
+            functools.partial(own_bucket_kernel, groups),
+            out_shape=kv_shape,
+            in_specs=vmem_specs(2),
+            out_specs=pl.BlockSpec(memory_space=pltpu.VMEM),
+            compiler_params=params,
+            cost_estimate=CHEAP,
+            name="own_bucket",
+        )(own_tile, expander_order)
+        full_v, near, state, own_bucket = fence((full_v, near, state, own_bucket))
         state = attend({3: side_twin}, state, False)
         vals_2, passed = relay(full_k, full_v, "relay_vals")
         vals_3 = over_grp(passed, 1)
-        val_parts = [outgoing[0], near, vals_2, vals_3]
+        val_parts = [own_bucket, near, vals_2, vals_3]
         late = {5: corner, 6: corner_twin}
         _, acc, stat = attend(late, state, True)
         keys_3, acc, stat = fence((keys_3, acc, stat))
-        scores = score([outgoing[0], near, keys_2, keys_3])
+        scores = score([own_bucket, near, keys_2, keys_3])
     else:
         tiles = {}
         for offset in range(-RADIUS, RADIUS + 1):
@@ -380,7 +408,7 @@
         functools.partial(weigh_kernel, groups),
         out_shape=[
             jax.ShapeDtypeStruct((rows, width), F32),
-            jax.ShapeDtypeStruct((MATCHINGS, rows, width), F32),
+            jax.ShapeDtypeStruct((MATCHINGS * bucket, width), F32),
         ],
         in_specs=vmem_specs(3 + groups),
         out_specs=vmem_specs(2),

time: 42.5 us -> 42.1 us (level)
  local copies, waits for them, and re-layouts: 1.75 us -> 0.1 us
  waiting for transfers between devices: 14.7 us -> 15.8 us
  Pallas kernels: 13 us -> 13.8 us
  starting transfers between devices: 12.7 us -> 12.2 us
    unnamed x10 -> x12, local copies, waits for them, and re-layouts: 1.74 us -> 0.09 us
    ppermute x5, waiting for transfers between devices: 11.8 us -> 12.7 us  [over_grp(): return lax.ppermute(array, 'grp', [(i, i ^ b) for i in range(groups)])]
    ppermute x5, starting transfers between devices: 7.83 us -> 7.3 us  [over_grp(): return lax.ppermute(array, 'grp', [(i, i ^ b) for i in range(groups)])]
    pallas_call x1, Pallas kernels: 1.05 us -> 1.52 us  [shards(): pl.pallas_call(functools.partial(weigh_kernel, groups), out_shape=[jax.Sh...]
    pallas_call x1 -> x2, Pallas kernels: 1.46 us -> 1.83 us  [the longest x1 1.4 us: shards(): pl.pallas_call(functools.partial(prep_kernel, groups, 1 if relayed else 0...]
  transfers between devices with their start and end apart: 11 -> 11, of which waited for: 8 -> 8; matrix products, arithmetic and copies ran while one was open for 0% -> 0% of each run, Pallas kernels for 24% -> 26%
where the time goes in v7:
time: 42.1 us; the launch traced here: 41.9 us
  waiting for transfers between devices  15.8 us (38%)
  Pallas kernels  13.8 us (33%)
  starting transfers between devices  12.2 us (29%)
    ppermute x5, waiting for transfers between devices, over_grp(): return lax.ppermute(array, 'grp', [(i, i ^ b) for i in range(groups)])  12.7 us
    pallas_call x4, Pallas kernels, attend(): pl.pallas_call(functools.partial(blocks_kernel, loop_size, tuple(served),...  7.54 us
    ppermute x5, starting transfers between devices, over_grp(): return lax.ppermute(array, 'grp', [(i, i ^ b) for i in range(groups)])  7.3 us
    ppermute x6, starting transfers between devices, flipped(): lax.ppermute(array, 'loop', [(i, i ^ bits) for i in range(loop_size)])  4.85 us
    ppermute x6, waiting for transfers between devices, flipped(): lax.ppermute(array, 'loop', [(i, i ^ bits) for i in range(loop_size)])  3.12 us
    pallas_call x1, Pallas kernels, shards(): pl.pallas_call(functools.partial(weigh_kernel, groups), out_shape=[jax.Sh...  1.52 us
    pallas_call x1, Pallas kernels, shards(): pl.pallas_call(functools.partial(prep_kernel, groups, 1 if relayed else 0...  1.4 us
    pallas_call x1, Pallas kernels, shards(): pl.pallas_call(functools.partial(finish_kernel, groups), out_shape=jax.Sh...  1.27 us
  transfers between devices with their start and end apart: 11, of which 8 were waited for; matrix products, arithmetic and copies ran while one was open for 0% of the time, Pallas kernels for 26%

profile of v7, /device:TPU:0, one launch (start us, length us, event | category | flops | bytes accessed | tf_op | source)
XLA Modules:
  0.0 41.9 jit_solution(15947499519429006989)
XLA Ops:
  0.0 0.0 copy-start
  0.0 1.4 %prep.1 = (bf16[256,1024]{1,0:T(8,128)(2,1)S(1)}, bf16[192,1024]{1,0:T(8,128)(2,1)S(1)}, bf16[272,512]{1,0:T(8,128)(2,1)S(1)}) custom-call(bf16[256,512]{1,0:T(8,128)(2,1)} %k_hbm.1, bf16[256,512]{1,0:T(8,128)(2,1)} %v_hbm.1, s32[3,256]{1,0:T(4,128)} %order_ref.7), custom_call_target="tpu_custom_call" | custom-call | tf_op jit(solution)/shard_map/prep/pallas_call | solution.py:289
  1.4 4.1 %collective-permute-start = (bf16[272,512]{1,0:T(8,128)(2,1)S(1)}, bf16[272,512]{1,0:T(8,128)(2,1)S(1)}, u32[]{:S(2)}, u32[]{:S(2)}) collective-permute-start(bf16[272,512]{1,0:T(8,128)(2,1)S(1)} %get-tuple-element.45), channel_id=1, source_target_pairs={{0,2},{1,3},{2,0},{3,1},{4,6},{5,7},{6,4},{7,5},{8,10},{9,11},{10,... | collective-permute-start | bytes 835592 | tf_op jit(solution)/shard_map/ppermute | solution.py:303
  5.5 0.0 copy-start.3
  5.5 0.7 %collective-permute-start.3 = (bf16[256,1024]{1,0:T(8,128)(2,1)S(1)}, bf16[256,1024]{1,0:T(8,128)(2,1)S(1)}, u32[]{:S(2)}, u32[]{:S(2)}) collective-permute-start(bf16[256,1024]{1,0:T(8,128)(2,1)S(1)} %get-tuple-element.46.refs_0_.tile_ref), channel_id=1, source_target_pairs={{0,20},{4,16},{8,28},{12,24},{16,4},{20,0},{24,12},{28,8},{1,21},{... | collective-permute-start | bytes 1572872 | tf_op jit(solution)/shard_map/ppermute | solution.py:306
  6.2 1.5 %collective-permute-start.4 = (bf16[256,1024]{1,0:T(8,128)(2,1)S(1)}, bf16[256,1024]{1,0:T(8,128)(2,1)S(1)}, u32[]{:S(2)}, u32[]{:S(2)}) collective-permute-start(bf16[256,1024]{1,0:T(8,128)(2,1)S(1)} %get-tuple-element.46.refs_0_.tile_ref), channel_id=1, source_target_pairs={{0,8},{4,12},{8,0},{12,4},{16,24},{20,28},{24,16},{28,20},{1,9},{5... | collective-permute-start | bytes 1572872 | tf_op jit(solution)/shard_map/ppermute | solution.py:306
  7.7 0.7 %collective-permute-start.5 = (bf16[256,1024]{1,0:T(8,128)(2,1)S(1)}, bf16[256,1024]{1,0:T(8,128)(2,1)S(1)}, u32[]{:S(2)}, u32[]{:S(2)}) collective-permute-start(bf16[256,1024]{1,0:T(8,128)(2,1)S(1)} %get-tuple-element.46.refs_0_.tile_ref), channel_id=1, source_target_pairs={{0,4},{4,0},{8,12},{12,8},{16,20},{20,16},{24,28},{28,24},{1,5},{5... | collective-permute-start | bytes 1572872 | tf_op jit(solution)/shard_map/ppermute | solution.py:306
  8.4 0.0 copy-start.4
  8.4 1.6 %collective-permute-start.2 = (bf16[192,1024]{1,0:T(8,128)(2,1)S(1)}, bf16[192,1024]{1,0:T(8,128)(2,1)S(1)}, u32[]{:S(2)}, u32[]{:S(2)}) collective-permute-start(bf16[192,1024]{1,0:T(8,128)(2,1)S(1)} %get-tuple-element.52), channel_id=1, source_target_pairs={{0,1},{1,0},{2,3},{3,2},{4,5},{5,4},{6,7},{7,6},{8,9},{9,8},{10,11... | collective-permute-start | bytes 1179656 | tf_op jit(solution)/shard_map/ppermute | solution.py:303
  9.9 0.0 copy-done
  9.9 0.0 copy-done.3
  9.9 1.9 %blocks0.1 = (f32[512,256]{1,0:T(8,128)S(1)}, f32[16,256]{1,0:T(8,128)S(1)}, bf16[4,128,512]{2,1,0:T(8,128)(2,1)S(1)}) custom-call(s32[1,4]{1,0:T(1,128)S(1)} %copy-done.3, bf16[256,1024]{1,0:T(8,128)(2,1)S(1)} %get-tuple-element.46.refs_0_.tile_ref, bf16[256,512]{1,0:T(8,128)(2,1)S(1)} %copy-done), custom_call_target="tpu_custom_call" | custom-call | flops 1000 | bytes 1000 | tf_op jit(solution)/shard_map/blocks0/pallas_call | solution.py:319
  11.8 6.4 %collective-permute-done.order_ref.rows_ref = bf16[272,512]{1,0:T(8,128)(2,1)S(1)} collective-permute-done((bf16[272,512]{1,0:T(8,128)(2,1)S(1)}, bf16[272,512]{1,0:T(8,128)(2,1)S(1)}, u32[]{:S(2)}, u32[]{:S(2)}) %collective-permute-start) | collective-permute-done | bytes 278560 | tf_op jit(solution)/shard_map/ppermute | solution.py:303
  18.2 0.0 copy-done.4
  18.2 0.0 collective-permute-start.1
  18.3 0.0 copy-start.2
  18.3 0.3 relay_keys.1
  18.6 1.1 %collective-permute-done.3.refs_2_ = bf16[256,1024]{1,0:T(8,128)(2,1)S(1)} collective-permute-done((bf16[256,1024]{1,0:T(8,128)(2,1)S(1)}, bf16[256,1024]{1,0:T(8,128)(2,1)S(1)}, u32[]{:S(2)}, u32[]{:S(2)}) %collective-permute-start.3) | collective-permute-done | bytes 524320 | tf_op jit(solution)/shard_map/ppermute | solution.py:306
  19.7 1.3 %collective-permute-done.4.refs_1_ = bf16[256,1024]{1,0:T(8,128)(2,1)S(1)} collective-permute-done((bf16[256,1024]{1,0:T(8,128)(2,1)S(1)}, bf16[256,1024]{1,0:T(8,128)(2,1)S(1)}, u32[]{:S(2)}, u32[]{:S(2)}) %collective-permute-start.4) | collective-permute-done | bytes 524320 | tf_op jit(solution)/shard_map/ppermute | solution.py:306
  21.0 0.0 collective-permute-done.5.refs_0_
  21.0 0.1 collective-permute-start.10
  21.1 0.4 collective-permute-start.8
  21.5 1.5 %collective-permute-start.9 = (bf16[256,1024]{1,0:T(8,128)(2,1)S(1)}, bf16[256,1024]{1,0:T(8,128)(2,1)S(1)}, u32[]{:S(2)}, u32[]{:S(2)}) collective-permute-start(bf16[256,1024]{1,0:T(8,128)(2,1)S(1)} %collective-permute-done.3.refs_2_), channel_id=1, source_target_pairs={{0,8},{4,12},{8,0},{12,4},{16,24},{20,28},{24,16},{28,20},{1,9},{5... | collective-permute-start | bytes 1572872 | tf_op jit(solution)/shard_map/ppermute | solution.py:306
  23.0 0.0 copy-done.2
  23.0 0.4 %own_bucket.1.refs_0_ = bf16[192,1024]{1,0:T(8,128)(2,1)S(1)} custom-call(bf16[256,1024]{1,0:T(8,128)(2,1)S(1)} %get-tuple-element.46.refs_0_.tile_ref, s32[3,256]{1,0:T(4,128)S(1)} %copy-done.2), custom_call_target="tpu_custom_call" | custom-call | flops 1000 | bytes 1000 | tf_op jit(solution)/shard_map/own_bucket/pallas_call | solution.py:379
  23.4 1.9 %blocks1_2_4.1 = (f32[512,256]{1,0:T(8,128)S(1)}, f32[16,256]{1,0:T(8,128)S(1)}) custom-call(s32[1,4]{1,0:T(1,128)S(1)} %copy-done.3, bf16[256,1024]{1,0:T(8,128)(2,1)S(1)} %collective-permute-done.5.refs_0_, bf16[256,1024]{1,0:T(8,128)(2,1)S(1)} %collective-permute-done.4.refs_1_, ...), custom_call_target="tpu_custom_call", output_to_operand_aliasing={{0}: (5, {}), {1}: (6, {})} | custom-call | flops 1000 | bytes 1000 | tf_op jit(solution)/shard_map/blocks1_2_4/pallas_call | solution.py:319
  25.3 0.6 %collective-permute-done.2.refs_1_ = bf16[192,1024]{1,0:T(8,128)(2,1)S(1)} collective-permute-done((bf16[192,1024]{1,0:T(8,128)(2,1)S(1)}, bf16[192,1024]{1,0:T(8,128)(2,1)S(1)}, u32[]{:S(2)}, u32[]{:S(2)}) %collective-permute-start.2) | collective-permute-done | bytes 393248 | tf_op jit(solution)/shard_map/ppermute | solution.py:303
  25.9 1.3 %collective-permute-start.7 = (bf16[192,512]{1,0:T(8,128)(2,1)S(1)}, bf16[192,512]{1,0:T(8,128)(2,1)S(1)}, u32[]{:S(2)}, u32[]{:S(2)}) collective-permute-start(bf16[192,512]{1,0:T(8,128)(2,1)S(1)} %get-tuple-element.68), channel_id=1, source_target_pairs={{0,1},{1,0},{2,3},{3,2},{4,5},{5,4},{6,7},{7,6},{8,9},{9,8},{10,11... | collective-permute-start | bytes 589832 | tf_op jit(solution)/shard_map/ppermute | solution.py:303
  27.2 5.2 %collective-permute-done.1.rows_ref = bf16[256,512]{1,0:T(8,128)(2,1)S(1)} collective-permute-done((bf16[256,512]{1,0:T(8,128)(2,1)S(1)}, bf16[256,512]{1,0:T(8,128)(2,1)S(1)}, u32[]{:S(2)}, u32[]{:S(2)}) %collective-permute-start.1) | collective-permute-done | bytes 262176 | tf_op jit(solution)/shard_map/ppermute | solution.py:303
  32.3 0.0 copy-start.5
  32.4 0.3 relay_vals.1
  32.6 0.3 collective-permute-start.6
  33.0 0.1 copy-done.5
  33.0 0.0 collective-permute-done.10.refs_0_
  33.0 1.8 %blocks3.1 = (f32[512,256]{1,0:T(8,128)S(1)}, f32[16,256]{1,0:T(8,128)S(1)}) custom-call(s32[1,4]{1,0:T(1,128)S(1)} %copy-done.3, bf16[256,1024]{1,0:T(8,128)(2,1)S(1)} %collective-permute-done.10.refs_0_, bf16[4,128,512]{2,1,0:T(8,128)(2,1)S(1)} %get-tuple-element.69.refs_3_.refs_1_.refs_2_, ...), custom_call_target="tpu_custom_call", output_to_operand_aliasing={{0}: (3, {}), {1}: (4, {})} | custom-call | flops 1000 | bytes 1000 | tf_op jit(solution)/shard_map/blocks3/pallas_call | solution.py:319
  34.9 0.5 %collective-permute-done.8.refs_0_ = bf16[256,1024]{1,0:T(8,128)(2,1)S(1)} collective-permute-done((bf16[256,1024]{1,0:T(8,128)(2,1)S(1)}, bf16[256,1024]{1,0:T(8,128)(2,1)S(1)}, u32[]{:S(2)}, u32[]{:S(2)}) %collective-permute-start.8) | collective-permute-done | bytes 524320 | tf_op jit(solution)/shard_map/ppermute | solution.py:306
  35.3 0.2 collective-permute-done.9.refs_1_
  35.6 2.0 %blocks5_6.1 = (f32[256,512]{1,0:T(8,128)S(1)}, f32[256,128]{1,0:T(8,128)S(1)}) custom-call(s32[1,4]{1,0:T(1,128)S(1)} %copy-done.3, bf16[256,1024]{1,0:T(8,128)(2,1)S(1)} %collective-permute-done.8.refs_0_, bf16[256,1024]{1,0:T(8,128)(2,1)S(1)} %collective-permute-done.9.refs_1_, bf16[4,128,512]{2,1,0:T(8,128)(2,1)S(1)} %get-tuple-element.69.refs_3_.refs_1_.refs_2_, ...), custom_call_target="tpu_custom_call" | custom-call | flops 1000 | bytes 1000 | tf_op jit(solution)/shard_map/blocks5_6/pallas_call | solution.py:319
  37.6 0.0 collective-permute-done.7.refs_3_
  37.6 1.0 %score.1.score_ref = f32[3,256,128]{2,1,0:T(8,128)S(1)} custom-call(bf16[256,512]{1,0:T(8,128)(2,1)S(1)} %copy-done, s32[3,256]{1,0:T(4,128)S(1)} %copy-done.2, f32[3,128]{1,0:T(4,128)S(1)} %pad.4.bias_ref, bf16[192,1024]{1,0:T(8,128)(2,1)S(1)} %own_bucket.1.refs_0_, bf16[192,1024]{1,0:T(8,128)(2,1)S(1)} %collective-permute-done.2.refs_1_, ...), custom_call_target="tpu_custom_call" | custom-call | flops 1000 | bytes 1000 | tf_op jit(solution)/shard_map/score/pallas_call | solution.py:341
  38.6 0.0 copy-start.1
  38.6 1.5 %weigh.1 = (f32[256,512]{1,0:T(8,128)S(1)}, f32[192,512]{1,0:T(8,128)S(1)}) custom-call(s32[3,256]{1,0:T(4,128)S(1)} %copy-done.2, f32[256,512]{1,0:T(8,128)S(1)} %get-tuple-element.76.acc_ref, f32[256,128]{1,0:T(8,128)S(1)} %get-tuple-element.77.stat_ref, f32[3,256,128]{2,1,0:T(8,128)S(1)} %score.1.score_ref, bf16[192,1024]{1,0:T(8,128)(2,1)S(1)} %own_bucket.1.refs_0_, ...), custom_call_target="tpu_custom_call" | custom-call | flops 1000 | bytes 1000 | tf_op jit(solution)/shard_map/weigh/pallas_call | solution.py:407
  40.2 0.5 %collective-permute-done.6.val_ref = bf16[192,512]{1,0:T(8,128)(2,1)S(1)} collective-permute-done((bf16[192,512]{1,0:T(8,128)(2,1)S(1)}, bf16[192,512]{1,0:T(8,128)(2,1)S(1)}, u32[]{:S(2)}, u32[]{:S(2)}) %collective-permute-start.6) | collective-permute-done | bytes 196640 | tf_op jit(solution)/shard_map/ppermute | solution.py:303
  40.6 0.0 copy-done.1
  40.6 1.3 %finish.1 = bf16[256,512]{1,0:T(8,128)(2,1)} custom-call(bf16[192,512]{1,0:T(8,128)(2,1)S(1)} %collective-permute-done.6.val_ref, s32[3,256]{1,0:T(4,128)S(1)} %copy-done.2, f32[256,512]{1,0:T(8,128)S(1)} %get-tuple-element.83.part_ref, f32[192,512]{1,0:T(8,128)S(1)} %get-tuple-element.84.edge_ref, bf16[512,512]{1,0:T(8,128)(2,1)S(1)} %copy-done.1), custom_call_target="tpu_custom_call" | custom-call | flops 1000 | bytes 1000 | tf_op jit(solution)/shard_map/finish/pallas_call | solution.py:419
  (1 shorter events, 0.0 us)
Async XLA Ops:
  0.0 9.9 %copy-start = (bf16[256,512]{1,0:T(8,128)(2,1)S(1)}, bf16[256,512]{1,0:T(8,128)(2,1)}, u32[]{:S(2)}) copy-start(bf16[256,512]{1,0:T(8,128)(2,1)} %q_ref.1) | copy-start | bytes 786436
  1.4 16.8 %collective-permute-start = (bf16[272,512]{1,0:T(8,128)(2,1)S(1)}, bf16[272,512]{1,0:T(8,128)(2,1)S(1)}, u32[]{:S(2)}, u32[]{:S(2)}) collective-permute-start(bf16[272,512]{1,0:T(8,128)(2,1)S(1)} %get-tuple-element.45), channel_id=1, source_target_pairs={{0,2},{1,3},{2,0},{3,1},{4,6},{5,7},{6,4},{7,5},{8,10},{9,11},{10,... | collective-permute-start | bytes 835592 | tf_op jit(solution)/shard_map/ppermute | solution.py:303
  5.5 4.4 %copy-start.3 = (s32[1,4]{1,0:T(1,128)S(1)}, s32[1,4]{1,0:T(1,128)}, u32[]{:S(2)}) copy-start(s32[1,4]{1,0:T(1,128)} %tiles_ref.7) | copy-start | bytes 52
  5.5 14.2 %collective-permute-start.3 = (bf16[256,1024]{1,0:T(8,128)(2,1)S(1)}, bf16[256,1024]{1,0:T(8,128)(2,1)S(1)}, u32[]{:S(2)}, u32[]{:S(2)}) collective-permute-start(bf16[256,1024]{1,0:T(8,128)(2,1)S(1)} %get-tuple-element.46.refs_0_.tile_ref), channel_id=1, source_target_pairs={{0,20},{4,16},{8,28},{12,24},{16,4},{20,0},{24,12},{28,8},{1,21},{... | collective-permute-start | bytes 1572872 | tf_op jit(solution)/shard_map/ppermute | solution.py:306
  6.2 14.8 %collective-permute-start.4 = (bf16[256,1024]{1,0:T(8,128)(2,1)S(1)}, bf16[256,1024]{1,0:T(8,128)(2,1)S(1)}, u32[]{:S(2)}, u32[]{:S(2)}) collective-permute-start(bf16[256,1024]{1,0:T(8,128)(2,1)S(1)} %get-tuple-element.46.refs_0_.tile_ref), channel_id=1, source_target_pairs={{0,8},{4,12},{8,0},{12,4},{16,24},{20,28},{24,16},{28,20},{1,9},{5... | collective-permute-start | bytes 1572872 | tf_op jit(solution)/shard_map/ppermute | solution.py:306
  7.7 13.3 %collective-permute-start.5 = (bf16[256,1024]{1,0:T(8,128)(2,1)S(1)}, bf16[256,1024]{1,0:T(8,128)(2,1)S(1)}, u32[]{:S(2)}, u32[]{:S(2)}) collective-permute-start(bf16[256,1024]{1,0:T(8,128)(2,1)S(1)} %get-tuple-element.46.refs_0_.tile_ref), channel_id=1, source_target_pairs={{0,4},{4,0},{8,12},{12,8},{16,20},{20,16},{24,28},{28,24},{1,5},{5... | collective-permute-start | bytes 1572872 | tf_op jit(solution)/shard_map/ppermute | solution.py:306
  8.4 9.9 %copy-start.4 = (bf16[256,512]{1,0:T(8,128)(2,1)S(1)}, bf16[256,512]{1,0:T(8,128)(2,1)}, u32[]{:S(2)}) copy-start(bf16[256,512]{1,0:T(8,128)(2,1)} %v_hbm.1) | copy-start | bytes 786436
  8.4 17.5 %collective-permute-start.2 = (bf16[192,1024]{1,0:T(8,128)(2,1)S(1)}, bf16[192,1024]{1,0:T(8,128)(2,1)S(1)}, u32[]{:S(2)}, u32[]{:S(2)}) collective-permute-start(bf16[192,1024]{1,0:T(8,128)(2,1)S(1)} %get-tuple-element.52), channel_id=1, source_target_pairs={{0,1},{1,0},{2,3},{3,2},{4,5},{5,4},{6,7},{7,6},{8,9},{9,8},{10,11... | collective-permute-start | bytes 1179656 | tf_op jit(solution)/shard_map/ppermute | solution.py:303
  18.2 14.1 %collective-permute-start.1 = (bf16[256,512]{1,0:T(8,128)(2,1)S(1)}, bf16[256,512]{1,0:T(8,128)(2,1)S(1)}, u32[]{:S(2)}, u32[]{:S(2)}) collective-permute-start(bf16[256,512]{1,0:T(8,128)(2,1)S(1)} %copy-done.4), channel_id=1, source_target_pairs={{0,2},{1,3},{2,0},{3,1},{4,6},{5,7},{6,4},{7,5},{8,10},{9,11},{10,... | collective-permute-start | bytes 786440 | tf_op jit(solution)/shard_map/ppermute | solution.py:303
  18.3 4.7 %copy-start.2 = (s32[3,256]{1,0:T(4,128)S(1)}, s32[3,256]{1,0:T(4,128)}, u32[]{:S(2)}) copy-start(s32[3,256]{1,0:T(4,128)} %order_ref.7) | copy-start | bytes 9220
  21.0 12.1 %collective-permute-start.10 = (bf16[256,1024]{1,0:T(8,128)(2,1)S(1)}, bf16[256,1024]{1,0:T(8,128)(2,1)S(1)}, u32[]{:S(2)}, u32[]{:S(2)}) collective-permute-start(bf16[256,1024]{1,0:T(8,128)(2,1)S(1)} %collective-permute-done.4.refs_1_), channel_id=1, source_target_pairs={{0,4},{4,0},{8,12},{12,8},{16,20},{20,16},{24,28},{28,24},{1,5},{5... | collective-permute-start | bytes 1572872 | tf_op jit(solution)/shard_map/ppermute | solution.py:306
  21.1 14.3 %collective-permute-start.8 = (bf16[256,1024]{1,0:T(8,128)(2,1)S(1)}, bf16[256,1024]{1,0:T(8,128)(2,1)S(1)}, u32[]{:S(2)}, u32[]{:S(2)}) collective-permute-start(bf16[256,1024]{1,0:T(8,128)(2,1)S(1)} %collective-permute-done.4.refs_1_), channel_id=1, source_target_pairs={{0,16},{4,20},{8,24},{12,28},{16,0},{20,4},{24,8},{28,12},{1,17},{... | collective-permute-start | bytes 1572872 | tf_op jit(solution)/shard_map/ppermute | solution.py:306
  21.5 14.1 %collective-permute-start.9 = (bf16[256,1024]{1,0:T(8,128)(2,1)S(1)}, bf16[256,1024]{1,0:T(8,128)(2,1)S(1)}, u32[]{:S(2)}, u32[]{:S(2)}) collective-permute-start(bf16[256,1024]{1,0:T(8,128)(2,1)S(1)} %collective-permute-done.3.refs_2_), channel_id=1, source_target_pairs={{0,8},{4,12},{8,0},{12,4},{16,24},{20,28},{24,16},{28,20},{1,9},{5... | collective-permute-start | bytes 1572872 | tf_op jit(solution)/shard_map/ppermute | solution.py:306
  25.9 11.7 %collective-permute-start.7 = (bf16[192,512]{1,0:T(8,128)(2,1)S(1)}, bf16[192,512]{1,0:T(8,128)(2,1)S(1)}, u32[]{:S(2)}, u32[]{:S(2)}) collective-permute-start(bf16[192,512]{1,0:T(8,128)(2,1)S(1)} %get-tuple-element.68), channel_id=1, source_target_pairs={{0,1},{1,0},{2,3},{3,2},{4,5},{5,4},{6,7},{7,6},{8,9},{9,8},{10,11... | collective-permute-start | bytes 589832 | tf_op jit(solution)/shard_map/ppermute | solution.py:303
  32.3 0.7 %copy-start.5 = (f32[3,8]{1,0:T(4,128)S(1)}, f32[3,8]{1,0:T(4,128)}, u32[]{:S(2)}) copy-start(f32[3,8]{1,0:T(4,128)} %param.13) | copy-start | bytes 292
  32.6 8.0 %collective-permute-start.6 = (bf16[192,512]{1,0:T(8,128)(2,1)S(1)}, bf16[192,512]{1,0:T(8,128)(2,1)S(1)}, u32[]{:S(2)}, u32[]{:S(2)}) collective-permute-start(bf16[192,512]{1,0:T(8,128)(2,1)S(1)} %get-tuple-element.67), channel_id=1, source_target_pairs={{0,1},{1,0},{2,3},{3,2},{4,5},{5,4},{6,7},{7,6},{8,9},{9,8},{10,11... | collective-permute-start | bytes 589832 | tf_op jit(solution)/shard_map/ppermute | solution.py:303
  38.6 2.0 %copy-start.1 = (bf16[512,512]{1,0:T(8,128)(2,1)S(1)}, bf16[512,512]{1,0:T(8,128)(2,1)}, u32[]{:S(2)}) copy-start(bf16[512,512]{1,0:T(8,128)(2,1)} %w_ref.1) | copy-start | bytes 1572868

commit v8 on v7

--- a/solution.py
+++ b/solution.py
@@ -263,8 +263,8 @@
     high = weighed.astype(BF16)
     low = (weighed - high.astype(F32)).astype(BF16)
     tables = [place_table(order_ref[j : j + 1, :], rows)[:, rows - bucket :] for j in range(MATCHINGS)]
-    table = jnp.concatenate(tables, axis=1)
-    attended = part_ref[...] + dot(table, high) + dot(table, low)
+    table = jnp.concatenate(tables + tables, axis=1)
+    attended = part_ref[...] + dot(table, jnp.concatenate([high, low], axis=0))
     out_ref[...] = dot(attended.astype(BF16), w_ref[...]).astype(BF16)
 
 

time: 42.1 us -> 42.1 us (level)
  starting transfers between devices: 12.2 us -> 13.2 us
  waiting for transfers between devices: 15.8 us -> 14.8 us
    ppermute x5, starting transfers between devices: 7.3 us -> 8.32 us  [over_grp(): return lax.ppermute(array, 'grp', [(i, i ^ b) for i in range(groups)])]
    ppermute x5, waiting for transfers between devices: 12.7 us -> 11.7 us  [over_grp(): return lax.ppermute(array, 'grp', [(i, i ^ b) for i in range(groups)])]
where the time goes in v8:
time: 42.1 us; the launch traced here: 41.9 us
  waiting for transfers between devices  14.8 us (35%)
  Pallas kernels  13.8 us (33%)
  starting transfers between devices  13.2 us (31%)
    ppermute x5, waiting for transfers between devices, over_grp(): return lax.ppermute(array, 'grp', [(i, i ^ b) for i in range(groups)])  11.7 us
    ppermute x5, starting transfers between devices, over_grp(): return lax.ppermute(array, 'grp', [(i, i ^ b) for i in range(groups)])  8.32 us
    pallas_call x4, Pallas kernels, attend(): pl.pallas_call(functools.partial(blocks_kernel, loop_size, tuple(served),...  7.54 us
    ppermute x6, starting transfers between devices, flipped(): lax.ppermute(array, 'loop', [(i, i ^ bits) for i in range(loop_size)])  4.85 us
    ppermute x6, waiting for transfers between devices, flipped(): lax.ppermute(array, 'loop', [(i, i ^ bits) for i in range(loop_size)])  3.12 us
    pallas_call x1, Pallas kernels, shards(): pl.pallas_call(functools.partial(weigh_kernel, groups), out_shape=[jax.Sh...  1.52 us
    pallas_call x1, Pallas kernels, shards(): pl.pallas_call(functools.partial(prep_kernel, groups, 1 if relayed else 0...  1.4 us
    pallas_call x1, Pallas kernels, shards(): pl.pallas_call(functools.partial(finish_kernel, groups), out_shape=jax.Sh...  1.27 us
  transfers between devices with their start and end apart: 11, of which 8 were waited for; matrix products, arithmetic and copies ran while one was open for 0% of the time, Pallas kernels for 26%

profile of v8, /device:TPU:0, one launch (start us, length us, event | category | flops | bytes accessed | tf_op | source)
XLA Modules:
  0.0 41.9 jit_solution(7599417295343456535)
XLA Ops:
  0.0 0.0 copy-start
  0.0 1.4 %prep.1 = (bf16[256,1024]{1,0:T(8,128)(2,1)S(1)}, bf16[192,1024]{1,0:T(8,128)(2,1)S(1)}, bf16[272,512]{1,0:T(8,128)(2,1)S(1)}) custom-call(bf16[256,512]{1,0:T(8,128)(2,1)} %k_hbm.1, bf16[256,512]{1,0:T(8,128)(2,1)} %v_hbm.1, s32[3,256]{1,0:T(4,128)} %order_ref.7), custom_call_target="tpu_custom_call" | custom-call | tf_op jit(solution)/shard_map/prep/pallas_call | solution.py:289
  1.4 4.1 %collective-permute-start = (bf16[272,512]{1,0:T(8,128)(2,1)S(1)}, bf16[272,512]{1,0:T(8,128)(2,1)S(1)}, u32[]{:S(2)}, u32[]{:S(2)}) collective-permute-start(bf16[272,512]{1,0:T(8,128)(2,1)S(1)} %get-tuple-element.45), channel_id=1, source_target_pairs={{0,2},{1,3},{2,0},{3,1},{4,6},{5,7},{6,4},{7,5},{8,10},{9,11},{10,... | collective-permute-start | bytes 835592 | tf_op jit(solution)/shard_map/ppermute | solution.py:303
  5.5 0.0 copy-start.3
  5.5 0.7 %collective-permute-start.3 = (bf16[256,1024]{1,0:T(8,128)(2,1)S(1)}, bf16[256,1024]{1,0:T(8,128)(2,1)S(1)}, u32[]{:S(2)}, u32[]{:S(2)}) collective-permute-start(bf16[256,1024]{1,0:T(8,128)(2,1)S(1)} %get-tuple-element.46.refs_0_.tile_ref), channel_id=1, source_target_pairs={{0,20},{4,16},{8,28},{12,24},{16,4},{20,0},{24,12},{28,8},{1,21},{... | collective-permute-start | bytes 1572872 | tf_op jit(solution)/shard_map/ppermute | solution.py:306
  6.2 1.5 %collective-permute-start.4 = (bf16[256,1024]{1,0:T(8,128)(2,1)S(1)}, bf16[256,1024]{1,0:T(8,128)(2,1)S(1)}, u32[]{:S(2)}, u32[]{:S(2)}) collective-permute-start(bf16[256,1024]{1,0:T(8,128)(2,1)S(1)} %get-tuple-element.46.refs_0_.tile_ref), channel_id=1, source_target_pairs={{0,8},{4,12},{8,0},{12,4},{16,24},{20,28},{24,16},{28,20},{1,9},{5... | collective-permute-start | bytes 1572872 | tf_op jit(solution)/shard_map/ppermute | solution.py:306
  7.7 0.7 %collective-permute-start.5 = (bf16[256,1024]{1,0:T(8,128)(2,1)S(1)}, bf16[256,1024]{1,0:T(8,128)(2,1)S(1)}, u32[]{:S(2)}, u32[]{:S(2)}) collective-permute-start(bf16[256,1024]{1,0:T(8,128)(2,1)S(1)} %get-tuple-element.46.refs_0_.tile_ref), channel_id=1, source_target_pairs={{0,4},{4,0},{8,12},{12,8},{16,20},{20,16},{24,28},{28,24},{1,5},{5... | collective-permute-start | bytes 1572872 | tf_op jit(solution)/shard_map/ppermute | solution.py:306
  8.4 0.0 copy-start.4
  8.4 1.6 %collective-permute-start.2 = (bf16[192,1024]{1,0:T(8,128)(2,1)S(1)}, bf16[192,1024]{1,0:T(8,128)(2,1)S(1)}, u32[]{:S(2)}, u32[]{:S(2)}) collective-permute-start(bf16[192,1024]{1,0:T(8,128)(2,1)S(1)} %get-tuple-element.52), channel_id=1, source_target_pairs={{0,1},{1,0},{2,3},{3,2},{4,5},{5,4},{6,7},{7,6},{8,9},{9,8},{10,11... | collective-permute-start | bytes 1179656 | tf_op jit(solution)/shard_map/ppermute | solution.py:303
  9.9 0.0 copy-done
  9.9 0.0 copy-done.3
  9.9 1.9 %blocks0.1 = (f32[512,256]{1,0:T(8,128)S(1)}, f32[16,256]{1,0:T(8,128)S(1)}, bf16[4,128,512]{2,1,0:T(8,128)(2,1)S(1)}) custom-call(s32[1,4]{1,0:T(1,128)S(1)} %copy-done.3, bf16[256,1024]{1,0:T(8,128)(2,1)S(1)} %get-tuple-element.46.refs_0_.tile_ref, bf16[256,512]{1,0:T(8,128)(2,1)S(1)} %copy-done), custom_call_target="tpu_custom_call" | custom-call | flops 1000 | bytes 1000 | tf_op jit(solution)/shard_map/blocks0/pallas_call | solution.py:319
  11.8 6.4 %collective-permute-done.order_ref.rows_ref = bf16[272,512]{1,0:T(8,128)(2,1)S(1)} collective-permute-done((bf16[272,512]{1,0:T(8,128)(2,1)S(1)}, bf16[272,512]{1,0:T(8,128)(2,1)S(1)}, u32[]{:S(2)}, u32[]{:S(2)}) %collective-permute-start) | collective-permute-done | bytes 278560 | tf_op jit(solution)/shard_map/ppermute | solution.py:303
  18.2 0.0 copy-done.4
  18.2 0.0 collective-permute-start.1
  18.3 0.0 copy-start.2
  18.3 0.3 relay_keys.1
  18.6 1.1 %collective-permute-done.3.refs_2_ = bf16[256,1024]{1,0:T(8,128)(2,1)S(1)} collective-permute-done((bf16[256,1024]{1,0:T(8,128)(2,1)S(1)}, bf16[256,1024]{1,0:T(8,128)(2,1)S(1)}, u32[]{:S(2)}, u32[]{:S(2)}) %collective-permute-start.3) | collective-permute-done | bytes 524320 | tf_op jit(solution)/shard_map/ppermute | solution.py:306
  19.7 1.3 %collective-permute-done.4.refs_1_ = bf16[256,1024]{1,0:T(8,128)(2,1)S(1)} collective-permute-done((bf16[256,1024]{1,0:T(8,128)(2,1)S(1)}, bf16[256,1024]{1,0:T(8,128)(2,1)S(1)}, u32[]{:S(2)}, u32[]{:S(2)}) %collective-permute-start.4) | collective-permute-done | bytes 524320 | tf_op jit(solution)/shard_map/ppermute | solution.py:306
  21.0 0.0 collective-permute-done.5.refs_0_
  21.0 0.1 collective-permute-start.10
  21.1 0.4 collective-permute-start.8
  21.5 1.5 %collective-permute-start.9 = (bf16[256,1024]{1,0:T(8,128)(2,1)S(1)}, bf16[256,1024]{1,0:T(8,128)(2,1)S(1)}, u32[]{:S(2)}, u32[]{:S(2)}) collective-permute-start(bf16[256,1024]{1,0:T(8,128)(2,1)S(1)} %collective-permute-done.3.refs_2_), channel_id=1, source_target_pairs={{0,8},{4,12},{8,0},{12,4},{16,24},{20,28},{24,16},{28,20},{1,9},{5... | collective-permute-start | bytes 1572872 | tf_op jit(solution)/shard_map/ppermute | solution.py:306
  23.0 0.0 copy-done.2
  23.0 0.4 %own_bucket.1.refs_0_ = bf16[192,1024]{1,0:T(8,128)(2,1)S(1)} custom-call(bf16[256,1024]{1,0:T(8,128)(2,1)S(1)} %get-tuple-element.46.refs_0_.tile_ref, s32[3,256]{1,0:T(4,128)S(1)} %copy-done.2), custom_call_target="tpu_custom_call" | custom-call | flops 1000 | bytes 1000 | tf_op jit(solution)/shard_map/own_bucket/pallas_call | solution.py:379
  23.4 1.9 %blocks1_2_4.1 = (f32[512,256]{1,0:T(8,128)S(1)}, f32[16,256]{1,0:T(8,128)S(1)}) custom-call(s32[1,4]{1,0:T(1,128)S(1)} %copy-done.3, bf16[256,1024]{1,0:T(8,128)(2,1)S(1)} %collective-permute-done.5.refs_0_, bf16[256,1024]{1,0:T(8,128)(2,1)S(1)} %collective-permute-done.4.refs_1_, ...), custom_call_target="tpu_custom_call", output_to_operand_aliasing={{0}: (5, {}), {1}: (6, {})} | custom-call | flops 1000 | bytes 1000 | tf_op jit(solution)/shard_map/blocks1_2_4/pallas_call | solution.py:319
  25.3 0.6 %collective-permute-done.2.refs_1_ = bf16[192,1024]{1,0:T(8,128)(2,1)S(1)} collective-permute-done((bf16[192,1024]{1,0:T(8,128)(2,1)S(1)}, bf16[192,1024]{1,0:T(8,128)(2,1)S(1)}, u32[]{:S(2)}, u32[]{:S(2)}) %collective-permute-start.2) | collective-permute-done | bytes 393248 | tf_op jit(solution)/shard_map/ppermute | solution.py:303
  25.9 2.3 %collective-permute-start.7 = (bf16[192,512]{1,0:T(8,128)(2,1)S(1)}, bf16[192,512]{1,0:T(8,128)(2,1)S(1)}, u32[]{:S(2)}, u32[]{:S(2)}) collective-permute-start(bf16[192,512]{1,0:T(8,128)(2,1)S(1)} %get-tuple-element.68), channel_id=1, source_target_pairs={{0,1},{1,0},{2,3},{3,2},{4,5},{5,4},{6,7},{7,6},{8,9},{9,8},{10,11... | collective-permute-start | bytes 589832 | tf_op jit(solution)/shard_map/ppermute | solution.py:303
  28.2 4.1 %collective-permute-done.1.rows_ref = bf16[256,512]{1,0:T(8,128)(2,1)S(1)} collective-permute-done((bf16[256,512]{1,0:T(8,128)(2,1)S(1)}, bf16[256,512]{1,0:T(8,128)(2,1)S(1)}, u32[]{:S(2)}, u32[]{:S(2)}) %collective-permute-start.1) | collective-permute-done | bytes 262176 | tf_op jit(solution)/shard_map/ppermute | solution.py:303
  32.3 0.0 copy-start.5
  32.4 0.3 relay_vals.1
  32.6 0.3 collective-permute-start.6
  33.0 0.1 copy-done.5
  33.0 0.0 collective-permute-done.10.refs_0_
  33.0 1.8 %blocks3.1 = (f32[512,256]{1,0:T(8,128)S(1)}, f32[16,256]{1,0:T(8,128)S(1)}) custom-call(s32[1,4]{1,0:T(1,128)S(1)} %copy-done.3, bf16[256,1024]{1,0:T(8,128)(2,1)S(1)} %collective-permute-done.10.refs_0_, bf16[4,128,512]{2,1,0:T(8,128)(2,1)S(1)} %get-tuple-element.69.refs_3_.refs_1_.refs_2_, ...), custom_call_target="tpu_custom_call", output_to_operand_aliasing={{0}: (3, {}), {1}: (4, {})} | custom-call | flops 1000 | bytes 1000 | tf_op jit(solution)/shard_map/blocks3/pallas_call | solution.py:319
  34.9 0.5 %collective-permute-done.8.refs_0_ = bf16[256,1024]{1,0:T(8,128)(2,1)S(1)} collective-permute-done((bf16[256,1024]{1,0:T(8,128)(2,1)S(1)}, bf16[256,1024]{1,0:T(8,128)(2,1)S(1)}, u32[]{:S(2)}, u32[]{:S(2)}) %collective-permute-start.8) | collective-permute-done | bytes 524320 | tf_op jit(solution)/shard_map/ppermute | solution.py:306
  35.3 0.2 collective-permute-done.9.refs_1_
  35.6 2.0 %blocks5_6.1 = (f32[256,512]{1,0:T(8,128)S(1)}, f32[256,128]{1,0:T(8,128)S(1)}) custom-call(s32[1,4]{1,0:T(1,128)S(1)} %copy-done.3, bf16[256,1024]{1,0:T(8,128)(2,1)S(1)} %collective-permute-done.8.refs_0_, bf16[256,1024]{1,0:T(8,128)(2,1)S(1)} %collective-permute-done.9.refs_1_, bf16[4,128,512]{2,1,0:T(8,128)(2,1)S(1)} %get-tuple-element.69.refs_3_.refs_1_.refs_2_, ...), custom_call_target="tpu_custom_call" | custom-call | flops 1000 | bytes 1000 | tf_op jit(solution)/shard_map/blocks5_6/pallas_call | solution.py:319
  37.6 0.0 collective-permute-done.7.refs_3_
  37.6 1.0 %score.1.score_ref = f32[3,256,128]{2,1,0:T(8,128)S(1)} custom-call(bf16[256,512]{1,0:T(8,128)(2,1)S(1)} %copy-done, s32[3,256]{1,0:T(4,128)S(1)} %copy-done.2, f32[3,128]{1,0:T(4,128)S(1)} %pad.4.bias_ref, bf16[192,1024]{1,0:T(8,128)(2,1)S(1)} %own_bucket.1.refs_0_, bf16[192,1024]{1,0:T(8,128)(2,1)S(1)} %collective-permute-done.2.refs_1_, ...), custom_call_target="tpu_custom_call" | custom-call | flops 1000 | bytes 1000 | tf_op jit(solution)/shard_map/score/pallas_call | solution.py:341
  38.6 0.0 copy-start.1
  38.6 1.5 %weigh.1 = (f32[256,512]{1,0:T(8,128)S(1)}, f32[192,512]{1,0:T(8,128)S(1)}) custom-call(s32[3,256]{1,0:T(4,128)S(1)} %copy-done.2, f32[256,512]{1,0:T(8,128)S(1)} %get-tuple-element.76.acc_ref, f32[256,128]{1,0:T(8,128)S(1)} %get-tuple-element.77.stat_ref, f32[3,256,128]{2,1,0:T(8,128)S(1)} %score.1.score_ref, bf16[192,1024]{1,0:T(8,128)(2,1)S(1)} %own_bucket.1.refs_0_, ...), custom_call_target="tpu_custom_call" | custom-call | flops 1000 | bytes 1000 | tf_op jit(solution)/shard_map/weigh/pallas_call | solution.py:407
  40.2 0.5 %collective-permute-done.6.val_ref = bf16[192,512]{1,0:T(8,128)(2,1)S(1)} collective-permute-done((bf16[192,512]{1,0:T(8,128)(2,1)S(1)}, bf16[192,512]{1,0:T(8,128)(2,1)S(1)}, u32[]{:S(2)}, u32[]{:S(2)}) %collective-permute-start.6) | collective-permute-done | bytes 196640 | tf_op jit(solution)/shard_map/ppermute | solution.py:303
  40.7 0.0 copy-done.1
  40.7 1.3 %finish.1 = bf16[256,512]{1,0:T(8,128)(2,1)} custom-call(bf16[192,512]{1,0:T(8,128)(2,1)S(1)} %collective-permute-done.6.val_ref, s32[3,256]{1,0:T(4,128)S(1)} %copy-done.2, f32[256,512]{1,0:T(8,128)S(1)} %get-tuple-element.83.part_ref, f32[192,512]{1,0:T(8,128)S(1)} %get-tuple-element.84.edge_ref, bf16[512,512]{1,0:T(8,128)(2,1)S(1)} %copy-done.1), custom_call_target="tpu_custom_call" | custom-call | flops 1000 | bytes 1000 | tf_op jit(solution)/shard_map/finish/pallas_call | solution.py:419
  (1 shorter events, 0.0 us)
Async XLA Ops:
  0.0 9.9 %copy-start = (bf16[256,512]{1,0:T(8,128)(2,1)S(1)}, bf16[256,512]{1,0:T(8,128)(2,1)}, u32[]{:S(2)}) copy-start(bf16[256,512]{1,0:T(8,128)(2,1)} %q_ref.1) | copy-start | bytes 786436
  1.4 16.8 %collective-permute-start = (bf16[272,512]{1,0:T(8,128)(2,1)S(1)}, bf16[272,512]{1,0:T(8,128)(2,1)S(1)}, u32[]{:S(2)}, u32[]{:S(2)}) collective-permute-start(bf16[272,512]{1,0:T(8,128)(2,1)S(1)} %get-tuple-element.45), channel_id=1, source_target_pairs={{0,2},{1,3},{2,0},{3,1},{4,6},{5,7},{6,4},{7,5},{8,10},{9,11},{10,... | collective-permute-start | bytes 835592 | tf_op jit(solution)/shard_map/ppermute | solution.py:303
  5.5 4.4 %copy-start.3 = (s32[1,4]{1,0:T(1,128)S(1)}, s32[1,4]{1,0:T(1,128)}, u32[]{:S(2)}) copy-start(s32[1,4]{1,0:T(1,128)} %tiles_ref.7) | copy-start | bytes 52
  5.5 14.2 %collective-permute-start.3 = (bf16[256,1024]{1,0:T(8,128)(2,1)S(1)}, bf16[256,1024]{1,0:T(8,128)(2,1)S(1)}, u32[]{:S(2)}, u32[]{:S(2)}) collective-permute-start(bf16[256,1024]{1,0:T(8,128)(2,1)S(1)} %get-tuple-element.46.refs_0_.tile_ref), channel_id=1, source_target_pairs={{0,20},{4,16},{8,28},{12,24},{16,4},{20,0},{24,12},{28,8},{1,21},{... | collective-permute-start | bytes 1572872 | tf_op jit(solution)/shard_map/ppermute | solution.py:306
  6.2 14.8 %collective-permute-start.4 = (bf16[256,1024]{1,0:T(8,128)(2,1)S(1)}, bf16[256,1024]{1,0:T(8,128)(2,1)S(1)}, u32[]{:S(2)}, u32[]{:S(2)}) collective-permute-start(bf16[256,1024]{1,0:T(8,128)(2,1)S(1)} %get-tuple-element.46.refs_0_.tile_ref), channel_id=1, source_target_pairs={{0,8},{4,12},{8,0},{12,4},{16,24},{20,28},{24,16},{28,20},{1,9},{5... | collective-permute-start | bytes 1572872 | tf_op jit(solution)/shard_map/ppermute | solution.py:306
  7.7 13.3 %collective-permute-start.5 = (bf16[256,1024]{1,0:T(8,128)(2,1)S(1)}, bf16[256,1024]{1,0:T(8,128)(2,1)S(1)}, u32[]{:S(2)}, u32[]{:S(2)}) collective-permute-start(bf16[256,1024]{1,0:T(8,128)(2,1)S(1)} %get-tuple-element.46.refs_0_.tile_ref), channel_id=1, source_target_pairs={{0,4},{4,0},{8,12},{12,8},{16,20},{20,16},{24,28},{28,24},{1,5},{5... | collective-permute-start | bytes 1572872 | tf_op jit(solution)/shard_map/ppermute | solution.py:306
  8.4 9.9 %copy-start.4 = (bf16[256,512]{1,0:T(8,128)(2,1)S(1)}, bf16[256,512]{1,0:T(8,128)(2,1)}, u32[]{:S(2)}) copy-start(bf16[256,512]{1,0:T(8,128)(2,1)} %v_hbm.1) | copy-start | bytes 786436
  8.4 17.5 %collective-permute-start.2 = (bf16[192,1024]{1,0:T(8,128)(2,1)S(1)}, bf16[192,1024]{1,0:T(8,128)(2,1)S(1)}, u32[]{:S(2)}, u32[]{:S(2)}) collective-permute-start(bf16[192,1024]{1,0:T(8,128)(2,1)S(1)} %get-tuple-element.52), channel_id=1, source_target_pairs={{0,1},{1,0},{2,3},{3,2},{4,5},{5,4},{6,7},{7,6},{8,9},{9,8},{10,11... | collective-permute-start | bytes 1179656 | tf_op jit(solution)/shard_map/ppermute | solution.py:303
  18.2 14.1 %collective-permute-start.1 = (bf16[256,512]{1,0:T(8,128)(2,1)S(1)}, bf16[256,512]{1,0:T(8,128)(2,1)S(1)}, u32[]{:S(2)}, u32[]{:S(2)}) collective-permute-start(bf16[256,512]{1,0:T(8,128)(2,1)S(1)} %copy-done.4), channel_id=1, source_target_pairs={{0,2},{1,3},{2,0},{3,1},{4,6},{5,7},{6,4},{7,5},{8,10},{9,11},{10,... | collective-permute-start | bytes 786440 | tf_op jit(solution)/shard_map/ppermute | solution.py:303
  18.3 4.7 %copy-start.2 = (s32[3,256]{1,0:T(4,128)S(1)}, s32[3,256]{1,0:T(4,128)}, u32[]{:S(2)}) copy-start(s32[3,256]{1,0:T(4,128)} %order_ref.7) | copy-start | bytes 9220
  21.0 12.1 %collective-permute-start.10 = (bf16[256,1024]{1,0:T(8,128)(2,1)S(1)}, bf16[256,1024]{1,0:T(8,128)(2,1)S(1)}, u32[]{:S(2)}, u32[]{:S(2)}) collective-permute-start(bf16[256,1024]{1,0:T(8,128)(2,1)S(1)} %collective-permute-done.4.refs_1_), channel_id=1, source_target_pairs={{0,4},{4,0},{8,12},{12,8},{16,20},{20,16},{24,28},{28,24},{1,5},{5... | collective-permute-start | bytes 1572872 | tf_op jit(solution)/shard_map/ppermute | solution.py:306
  21.1 14.3 %collective-permute-start.8 = (bf16[256,1024]{1,0:T(8,128)(2,1)S(1)}, bf16[256,1024]{1,0:T(8,128)(2,1)S(1)}, u32[]{:S(2)}, u32[]{:S(2)}) collective-permute-start(bf16[256,1024]{1,0:T(8,128)(2,1)S(1)} %collective-permute-done.4.refs_1_), channel_id=1, source_target_pairs={{0,16},{4,20},{8,24},{12,28},{16,0},{20,4},{24,8},{28,12},{1,17},{... | collective-permute-start | bytes 1572872 | tf_op jit(solution)/shard_map/ppermute | solution.py:306
  21.5 14.1 %collective-permute-start.9 = (bf16[256,1024]{1,0:T(8,128)(2,1)S(1)}, bf16[256,1024]{1,0:T(8,128)(2,1)S(1)}, u32[]{:S(2)}, u32[]{:S(2)}) collective-permute-start(bf16[256,1024]{1,0:T(8,128)(2,1)S(1)} %collective-permute-done.3.refs_2_), channel_id=1, source_target_pairs={{0,8},{4,12},{8,0},{12,4},{16,24},{20,28},{24,16},{28,20},{1,9},{5... | collective-permute-start | bytes 1572872 | tf_op jit(solution)/shard_map/ppermute | solution.py:306
  25.9 11.7 %collective-permute-start.7 = (bf16[192,512]{1,0:T(8,128)(2,1)S(1)}, bf16[192,512]{1,0:T(8,128)(2,1)S(1)}, u32[]{:S(2)}, u32[]{:S(2)}) collective-permute-start(bf16[192,512]{1,0:T(8,128)(2,1)S(1)} %get-tuple-element.68), channel_id=1, source_target_pairs={{0,1},{1,0},{2,3},{3,2},{4,5},{5,4},{6,7},{7,6},{8,9},{9,8},{10,11... | collective-permute-start | bytes 589832 | tf_op jit(solution)/shard_map/ppermute | solution.py:303
  32.3 0.7 %copy-start.5 = (f32[3,8]{1,0:T(4,128)S(1)}, f32[3,8]{1,0:T(4,128)}, u32[]{:S(2)}) copy-start(f32[3,8]{1,0:T(4,128)} %param.13) | copy-start | bytes 292
  32.6 8.0 %collective-permute-start.6 = (bf16[192,512]{1,0:T(8,128)(2,1)S(1)}, bf16[192,512]{1,0:T(8,128)(2,1)S(1)}, u32[]{:S(2)}, u32[]{:S(2)}) collective-permute-start(bf16[192,512]{1,0:T(8,128)(2,1)S(1)} %get-tuple-element.67), channel_id=1, source_target_pairs={{0,1},{1,0},{2,3},{3,2},{4,5},{5,4},{6,7},{7,6},{8,9},{9,8},{10,11... | collective-permute-start | bytes 589832 | tf_op jit(solution)/shard_map/ppermute | solution.py:303
  38.6 2.1 %copy-start.1 = (bf16[512,512]{1,0:T(8,128)(2,1)S(1)}, bf16[512,512]{1,0:T(8,128)(2,1)}, u32[]{:S(2)}) copy-start(bf16[512,512]{1,0:T(8,128)(2,1)} %w_ref.1) | copy-start | bytes 1572868
